TPU v7x, 128 devices: a whole 4x4x4 slice. The times are simulated.
128 devices in a mesh: seq: 32 (over y, z, core), head: 4 (over x).
Axes of the slice: x: 4, y: 4, z: 4, core: 2. Of those that a mesh axis runs over, the one named last changes fastest.
Arguments:
- queries: bfloat16 [24576, 64, 128], P('seq', 'head'), may hold values from -6 to 6
- keys: bfloat16 [24576, 64, 128], P('seq', 'head'), may hold values from -6 to 6
- values: bfloat16 [24576, 64, 128], P('seq', 'head'), may hold values from -6 to 6
- out_grad: bfloat16 [24576, 64, 128], P('seq', 'head'), may hold values from -8 to 8
- gain: float32 [64, 128], P('head'), may hold values from 0.1 to 1.9
- entry_state: float32 [64, 128, 128], P('head'), may hold values from -3547.24 to 3547.24
Outputs:
- normed: bfloat16 [24576, 64, 128], P('seq', 'head')
- query_grad: bfloat16 [24576, 64, 128], P('seq', 'head')
- key_grad: bfloat16 [24576, 64, 128], P('seq', 'head')
- value_grad: bfloat16 [24576, 64, 128], P('seq', 'head')
- entry_grad: float32 [64, 128, 128], P('head', 'seq')
All inputs are finite; a program needn't handle non-finite values.
Results may differ from a plain program's by a relative error of at most 0.006.
Values sent between devices are 32-bit elements; how exact they have to be, the bound alone decides.
No kernel may reach another device: no remote copies, remote signals or barrier semaphores. Data moves between devices by JAX's collectives and lax.ppermute only.
A program may use at most 256 MiB of HBM per device.

v0:
```python
import jax
import jax.numpy as jnp
from jax import lax
from jax.sharding import PartitionSpec as P

H = 64
E = 128


epsilon = 1e-06


def carried_in(value, axis, join, neutral, backward):
    count, mine = (lax.axis_size(axis), lax.axis_index(axis))
    pieces = lax.all_gather(value, axis)
    if backward:
        pieces = pieces[::-1]
        mine = count - 1 - mine
    subtotal = jnp.full_like(value, 0) + jnp.asarray(neutral, value.dtype)

    def step(position, subtotal):
        longer = join(subtotal, pieces[position])
        return jnp.where(position < mine, longer, subtotal)

    return lax.fori_loop(0, count - 1, step, subtotal)


def body(queries, keys, values, out_grad, gain, entry_state):
    tok_rows = queries.shape[0]
    total_width = H * E
    row_index = jnp.arange(tok_rows)[:, None]
    col_index = jnp.arange(tok_rows)[None, :]
    causal = (col_index <= row_index)[None]
    f32 = jnp.float32
    bf16 = jnp.bfloat16
    local_kv = jnp.einsum("thj,the->hje", keys, values, preferred_element_type=f32)
    earlier = carried_in(local_kv, "seq", jnp.add, jnp.zeros_like(local_kv), False)
    state_bf = (entry_state + earlier).astype(bf16)
    causal_qk = jnp.where(
        causal, jnp.einsum("thj,shj->hts", queries, keys, preferred_element_type=f32), 0.0
    ).astype(bf16)
    attended = jnp.einsum(
        "thj,hje->the", queries, state_bf, preferred_element_type=f32
    ) + jnp.einsum("hts,she->the", causal_qk, values, preferred_element_type=f32)
    upstream = gain * out_grad.astype(f32)
    squares, products = lax.psum(
        (jnp.sum(attended * attended, axis=(1, 2)), jnp.sum(upstream * attended, axis=(1, 2))),
        "head",
    )
    rms_value = jnp.sqrt(squares / total_width + epsilon)[:, None, None]
    normed = (gain * attended / rms_value).astype(bf16)
    inner_sum = products[:, None, None]
    pre_bf = (
        (upstream - attended * inner_sum / (total_width * rms_value * rms_value)) / rms_value
    ).astype(bf16)
    causal_gv = jnp.where(
        causal, jnp.einsum("the,she->hts", pre_bf, values, preferred_element_type=f32), 0.0
    ).astype(bf16)
    query_grad = (
        jnp.einsum("the,hje->thj", pre_bf, state_bf, preferred_element_type=f32)
        + jnp.einsum("hts,shj->thj", causal_gv, keys, preferred_element_type=f32)
    ).astype(bf16)
    local_w = jnp.einsum("thj,the->hje", queries, pre_bf, preferred_element_type=f32)
    suffix_sum = carried_in(local_w, "seq", jnp.add, jnp.zeros_like(local_w), True)
    later_bf = suffix_sum.astype(bf16)
    key_grad = (
        jnp.einsum("the,hje->thj", values, later_bf, preferred_element_type=f32)
        + jnp.einsum("hts,thj->shj", causal_gv, queries, preferred_element_type=f32)
    ).astype(bf16)
    value_grad = (
        jnp.einsum("thj,hje->the", keys, later_bf, preferred_element_type=f32)
        + jnp.einsum("hts,the->she", causal_qk, pre_bf, preferred_element_type=f32)
    ).astype(bf16)
    entry_grad = lax.psum_scatter(local_w, "seq", scatter_dimension=1, tiled=True)
    return (normed, query_grad, key_grad, value_grad, entry_grad)


def solution(mesh):
    return jax.shard_map(
        body,
        mesh=mesh,
        in_specs=(
            P("seq", "head", None),
            P("seq", "head", None),
            P("seq", "head", None),
            P("seq", "head", None),
            P("head", None),
            P("head", None, None),
        ),
        out_specs=(
            P("seq", "head", None),
            P("seq", "head", None),
            P("seq", "head", None),
            P("seq", "head", None),
            P("head", "seq", None),
        ),
        check_vma=False,
    )
```

profile of v0, /device:TPU:1, one launch (start us, length us, event | category | flops | bytes accessed | tf_op | source)
XLA Modules:
  0.0 597.2 jit_solution(7587662717701037068)
XLA Ops:
  9.1 5.9 fusion.3
  15.3 4.9 copy.44
  21.2 14.4 %select_convert_fusion.1 = bf16[16,768,768]{2,1,0:T(8,128)(2,1)} fusion(pred[768,768]{1,0:T(8,128)(4,1)} %iota_compare_fusion, bf16[768,16,128]{2,1,0:T(8,128)(2,1)} %param.11, bf16[768,16,128]{2,1,0:T(8,128)(2,1)} %param.10), kind=kOutput, calls=%fused_computation.3 | convolution fusion | flops 2434793472 | bytes 25755648 | tf_op jit(solution)/shard_map/thj,shj->hts/dot_general | solution.py:40
  35.6 97.2 %all-gather.5.cloned.1.call-done = f32[512,128,128]{2,1,0:T(8,128)} async-done(((f32[16,128,128]{2,1,0:T(8,128)}), f32[512,128,128]{2,1,0:T(8,128)}) %all-gather.5.cloned.1.call-update) | async-done | bytes 33554448 | tf_op jit(solution)/shard_map/all_gather | solution.py:15
  132.8 82.2 %while.28 = (s32[]{:T(128)}, f32[16,128,128]{2,1,0:T(8,128)}, s32[]{:T(128)}, f32[32,16,128,128]{3,2,1,0:T(8,128)}, s32[]{:T(128)}, /*index=5*/s32[]{:T(128)}) while((s32[]{:T(128)}, f32[16,128,128]{2,1,0:T(8,128)}, s32[]{:T(128)}, f32[32,16,128,128]{3,2,1,0:T(8,128)}, s32[]{:T(128)}, /*index=5*/s32[]{:T(128)}) %tuple.81), condition=%wide.region_1.2_spmd.clone, body=%wide.region_0.1_spmd.clone.sunk | while | flops 786436 | bytes 3145829 | solution.py:25
  217.4 6.5 %fusion.12 = f32[16,128,768]{2,1,0:T(8,128)} fusion(bf16[16,128,128]{2,1,0:T(8,128)(2,1)S(1)} %add_convert_fusion.1, bf16[768,16,128]{2,1,0:T(8,128)(2,1)} %param.10), kind=kOutput, calls=%fused_computation.26 | convolution fusion | flops 402653184 | bytes 9961472 | tf_op jit(solution)/shard_map/thj,hje->the/dot_general | solution.py:42
  223.9 14.6 %multiply_reduce_fusion = (f32[768]{0:T(1024)S(1)}, f32[768]{0:T(1024)S(1)}, f32[768,16,128]{0,2,1:T(8,128)}) fusion(bf16[768,16,128]{0,2,1:T(8,128)(2,1)} %copy.44, f32[16,128]{1,0:T(8,128)S(1)} %copy-done.7, bf16[16,768,768]{2,1,0:T(8,128)(2,1)} %select_convert_fusion.1, bf16[768,16,128]{2,1,0:T(8,128)(2,1)S(1)} %copy-done, f32[16,128,768]{2,1,0:T(8,128)} %fusion.12), kind=kOutput, calls=%fused_computation.11 | convolution fusion | flops 2426927616 | bytes 37763072 | tf_op jit(solution)/shard_map/hts,she->the/dot_general | solution.py:44
  238.5 8.7 %all-reduce = (f32[768]{0:T(1024)S(1)}, f32[768]{0:T(1024)S(1)}) all-reduce(f32[768]{0:T(1024)S(1)} %get-tuple-element.206, f32[768]{0:T(1024)S(1)} %get-tuple-element.205), channel_id=1, replica_groups=mesh['seq'=32,'head'=4] {'head'}, use_global_device_ids=true, to_apply=%region_3.4 | all-reduce | flops 1536 | bytes 12288 | tf_op jit(solution)/shard_map/psum | solution.py:46
  247.2 6.0 %divide_convert_fusion = (bf16[768,16,128]{0,2,1:T(8,128)(2,1)S(1)}, bf16[768,16,128]{0,2,1:T(8,128)(2,1)}) fusion(f32[768,16,128]{0,2,1:T(8,128)} %get-tuple-element.229, bf16[768,16,128]{0,2,1:T(8,128)(2,1)} %copy.44, f32[768]{0:T(1024)S(1)} %get-tuple-element.227, f32[768]{0:T(1024)S(1)} %get-tuple-element.224, f32[768]{0:T(1024)S(1)} %get-tuple-element.228, ...), kind=kLoop, calls=%fused_computation.10 | loop fusion | flops 15728640 | bytes 15746048 | tf_op jit(solution)/shard_map/convert_element_type | solution.py:55
  254.9 2.9 fusion.19
  263.0 5.0 copy.59
  267.9 5.6 fusion.24
  273.6 12.0 %select_convert_fusion = bf16[16,768,768]{2,1,0:T(8,128)(2,1)} fusion(pred[768,768]{1,0:T(8,128)(4,1)} %iota_compare_fusion, bf16[768,16,128]{0,2,1:T(8,128)(2,1)} %copy-done.2, bf16[768,16,128]{2,1,0:T(8,128)(2,1)S(1)} %copy-done), kind=kOutput, calls=%fused_computation.2 | convolution fusion | flops 2434793472 | bytes 25755648 | tf_op jit(solution)/shard_map/the,she->hts/dot_general | solution.py:57
  285.5 13.5 %fusion.1 = bf16[768,16,128]{0,2,1:T(8,128)(2,1)} fusion(f32[16,128,768]{2,1,0:T(8,128)} %fusion.24, bf16[16,768,768]{2,1,0:T(8,128)(2,1)} %select_convert_fusion, bf16[768,16,128]{2,1,0:T(8,128)(2,1)} %param.11), kind=kOutput, calls=%fused_computation.7 | convolution fusion | flops 2419064832 | bytes 31457280 | tf_op jit(solution)/shard_map/hts,shj->thj/dot_general | solution.py:61
  299.1 5.0 copy.60
  304.0 12.7 %fusion.25 = f32[16,128,768]{2,1,0:T(8,128)} fusion(bf16[768,16,128]{0,2,1:T(8,128)(2,1)} %copy-done.2, bf16[16,768,768]{2,1,0:T(8,128)(2,1)} %select_convert_fusion.1), kind=kOutput, calls=%fused_computation.40 | convolution fusion | flops 2415919104 | bytes 28311552 | tf_op jit(solution)/shard_map/hts,the->she/dot_general | solution.py:72
  316.8 18.5 %reduce-scatter.2.cloned.1.call-done = f32[16,4,128]{2,0,1:T(8,128)} async-done(((f32[16,128,128]{2,0,1:T(8,128)}), f32[16,4,128]{2,0,1:T(8,128)}) %reduce-scatter.2.cloned.1.call-update) | async-done | bytes 32784 | tf_op jit(solution)/shard_map/reduce_scatter | solution.py:74
  336.7 116.4 %all-gather.7.cloned.1.call-done = f32[512,128,128]{2,1,0:T(8,128)} async-done(((f32[16,128,128]{2,1,0:T(8,128)}), f32[512,128,128]{2,1,0:T(8,128)}) %all-gather.7.cloned.1.call-update) | async-done | bytes 33554448 | tf_op jit(solution)/shard_map/all_gather | solution.py:15
  453.1 23.0 %rev.3 = f32[32,16,128,128]{3,2,1,0:T(8,128)} reverse(f32[32,16,128,128]{3,2,1,0:T(8,128)} %bitcast.40), dimensions={0} | reverse | bytes 67108864 | tf_op jit(solution)/shard_map/rev | solution.py:17
  476.1 82.2 %while.29 = (s32[]{:T(128)}, f32[16,128,128]{2,1,0:T(8,128)}, s32[]{:T(128)}, f32[32,16,128,128]{3,2,1,0:T(8,128)}, s32[]{:T(128)}, /*index=5*/s32[]{:T(128)}) while((s32[]{:T(128)}, f32[16,128,128]{2,1,0:T(8,128)}, s32[]{:T(128)}, f32[32,16,128,128]{3,2,1,0:T(8,128)}, s32[]{:T(128)}, /*index=5*/s32[]{:T(128)}) %tuple.72), condition=%wide.region_7.8_spmd.clone, body=%wide.region_6.7_spmd.clone.sunk | while | flops 786436 | bytes 3145829 | solution.py:25
  481.1 2.7 add_select_fusion.5
  494.5 2.7 add_select_fusion.5
  502.4 2.7 add_select_fusion.5
  510.4 2.7 add_select_fusion.5
  515.7 2.7 add_select_fusion.5
  523.7 2.7 add_select_fusion.5
  531.7 2.7 add_select_fusion.5
  558.3 5.8 fusion.15
  564.1 3.9 fusion.2
  568.0 5.0 copy.62
  573.0 12.8 %fusion = bf16[768,16,128]{0,2,1:T(8,128)(2,1)} fusion(f32[16,128,768]{2,1,0:T(8,128)} %fusion.15, bf16[16,768,768]{2,1,0:T(8,128)(2,1)} %select_convert_fusion, bf16[768,16,128]{2,1,0:T(8,128)(2,1)} %param.10), kind=kOutput, calls=%fused_computation.5 | convolution fusion | flops 2419064832 | bytes 31457280 | tf_op jit(solution)/shard_map/hts,thj->shj/dot_general | solution.py:68
  585.7 5.0 copy.61
  (85 shorter events, 159.5 us)
Async XLA Ops:
  7.2 1.9 copy-start
  7.2 125.6 %all-gather.5.cloned.1.call-start = ((), (), s32[]{:S(2)}) async-start(), calls=%async_computation.2 | async-start | bytes 34603008 | tf_op jit(solution)/shard_map/all_gather | solution.py:15
  15.0 320.3 %reduce-scatter.2.cloned.1.call-start = ((), (), s32[]{:S(2)}) async-start(), calls=%async_computation.1 | async-start | bytes 1081344 | tf_op jit(solution)/shard_map/reduce_scatter | solution.py:74
  216.6 0.8 copy-start.6
  217.4 6.5 %copy-start.7 = (f32[16,128]{1,0:T(8,128)S(1)}, f32[16,128]{1,0:T(8,128)}, u32[]{:S(2)}) copy-start(f32[16,128]{1,0:T(8,128)} %param.14) | copy-start | bytes 24580
  247.2 7.7 %copy-start.4 = (bf16[768,16,128]{2,1,0:T(8,128)(2,1)S(1)}, bf16[768,16,128]{2,1,0:T(8,128)(2,1)}, u32[]{:S(2)}) copy-start(bf16[768,16,128]{2,1,0:T(8,128)(2,1)} %param.10) | copy-start | bytes 9437188
  253.2 1.7 copy-start.2
  260.4 192.7 %all-gather.7.cloned.1.call-start = ((), (), s32[]{:S(2)}) async-start(), calls=%async_computation.3 | async-start | bytes 34603008 | tf_op jit(solution)/shard_map/all_gather | solution.py:15
  558.3 5.8 copy-start.1
  558.3 5.8 copy-start.3
  558.3 5.8 copy-start.5
Sparse Core Ops, SparseCore 0:
  15.1 117.5 all-gather.4
  260.5 74.7 reduce-scatter.1
  337.8 115.2 all-gather.6
where the time goes:
time: 600 us; the launch traced here: 597 us
  waiting for transfers between devices  232 us (39%)
  other arithmetic  173 us (29%)
  matrix products  111 us (18%)
  local copies, waits for them, and re-layouts  58.7 us (10%)
  between operations  13.8 us (2%)
  blocking collectives  8.7 us (1%)
    all_gather x2, waiting for transfers between devices, carried_in(): pieces = lax.all_gather(value, axis)  214 us
    select_n x62, other arithmetic, step(): return jnp.where(position < mine, longer, subtotal)  164 us
    unnamed x22, local copies, waits for them, and re-layouts  30.5 us
    rev x1, local copies, waits for them, and re-layouts, carried_in(): pieces = pieces[::-1]  23 us
    reduce_scatter x1, waiting for transfers between devices, body(): lax.psum_scatter(local_w, 'seq', scatter_dimension=1, tiled=True)  18.5 us
    dot_general x1, matrix products, body(): jnp.einsum('hts,she->the', causal_qk, values, preferred_element_type=f32)  14.6 us
    dot_general x1, matrix products, body(): jnp.einsum('thj,shj->hts', queries, keys, preferred_element_type=f32)  14.4 us
    dot_general x1, matrix products, body(): jnp.einsum('hts,shj->thj', causal_gv, keys, preferred_element_type=f32)  13.5 us
  transfers between devices with their start and end apart: 3, of which 3 were waited for; matrix products, arithmetic and copies ran while one was open for 13% of the time, Pallas kernels for 0%

commit v1 on v0

v1 whole, which is shorter than its diff:
```python
import jax
import jax.numpy as jnp
from jax import lax
from jax.experimental import pallas as pl
from jax.experimental.pallas import tpu as pltpu
from jax.sharding import PartitionSpec as P

H = 64
E = 128
T = 768
HL = 16
C = 256
NC = T // C
N = 32
WIDTH = H * E
epsilon = 1e-06
f32 = jnp.float32
bf16 = jnp.bfloat16
MIB = 1 << 20


def mm(a, b):
    return lax.dot_general(a, b, (((1,), (0,)), ((), ())), preferred_element_type=f32)


def mm_nt(a, b):
    return lax.dot_general(a, b, (((1,), (1,)), ((), ())), preferred_element_type=f32)


def mm_tn(a, b):
    return lax.dot_general(a, b, (((0,), (0,)), ((), ())), preferred_element_type=f32)


def causal():
    row = lax.broadcasted_iota(jnp.int32, (C, C), 0)
    col = lax.broadcasted_iota(jnp.int32, (C, C), 1)
    return col <= row


def heads_first(ref):
    return jnp.swapaxes(ref[...], 0, 1)


def params(vmem=40):
    return pltpu.CompilerParams(vmem_limit_bytes=vmem * MIB)


def tok_spec(order=None):
    return pl.BlockSpec((C, HL, E), order or (lambda i: (i, 0, 0)))


def head_spec(order=None):
    return pl.BlockSpec((HL, C, E), order or (lambda i: (0, i, 0)))


def whole(shape):
    return pl.BlockSpec(shape, lambda i: (0,) * len(shape))


def cost(flops, moved):
    return pl.CostEstimate(flops=flops, bytes_accessed=moved, transcendentals=0)


def kv_kernel(k_ref, v_ref, o_ref):
    @pl.when(pl.program_id(0) == 0)
    def _():
        o_ref[...] = jnp.zeros_like(o_ref)

    k = heads_first(k_ref)
    v = heads_first(v_ref)
    for h in range(HL):
        o_ref[h] += mm_tn(k[h], v[h])


def kv_sums(keys, values):
    return pl.pallas_call(
        kv_kernel,
        grid=(NC,),
        in_specs=[tok_spec(), tok_spec()],
        out_specs=whole((HL, E, E)),
        out_shape=jax.ShapeDtypeStruct((HL, E, E), f32),
        compiler_params=params(),
        cost_estimate=cost(2 * T * HL * E * E, 7 * MIB),
        name="kv_sums",
    )(keys, values)


def prefix_kernel(r_ref, x_ref, o_ref):
    total = x_ref[...]
    for i in range(N):
        o_ref[i] = total
        total = total + r_ref[i]


def prefix(pieces, start):
    return pl.pallas_call(
        prefix_kernel,
        out_shape=jax.ShapeDtypeStruct(pieces.shape, f32),
        compiler_params=params(8),
        cost_estimate=cost(N * 64 * E, 2 * MIB),
        name="prefix",
    )(pieces, start)


def suffix_kernel(r_ref, o_ref, t_ref):
    total = jnp.zeros_like(t_ref)
    for i in reversed(range(N)):
        o_ref[i] = total
        total = total + r_ref[i]
    t_ref[...] = total


def suffix(pieces):
    return pl.pallas_call(
        suffix_kernel,
        out_shape=[
            jax.ShapeDtypeStruct(pieces.shape, f32),
            jax.ShapeDtypeStruct(pieces.shape[1:], f32),
        ],
        compiler_params=params(8),
        cost_estimate=cost(N * 64 * E, 2 * MIB),
        name="suffix",
    )(pieces)


def local_kernel(q_ref, k_ref, v_ref, g_ref, qh_ref, kh_ref, vh_ref, gh_ref, att_ref, loc_ref, acc):
    @pl.when(pl.program_id(0) == 0)
    def _():
        acc[...] = jnp.zeros_like(acc)

    mask = causal()
    q = heads_first(q_ref)
    k = heads_first(k_ref)
    v = heads_first(v_ref)
    qh_ref[...] = q
    kh_ref[...] = k
    vh_ref[...] = v
    gh_ref[...] = heads_first(g_ref)
    for h in range(HL):
        qk = jnp.where(mask, mm_nt(q[h], k[h]), 0.0).astype(bf16)
        loc = acc[h].astype(bf16)
        loc_ref[0, h] = loc
        att_ref[h] = (mm(qk, v[h]) + mm(q[h], loc)).astype(bf16)
        acc[h] += mm_tn(k[h], v[h])


def local_part(queries, keys, values, out_grad):
    major = jax.ShapeDtypeStruct((HL, T, E), bf16)
    return pl.pallas_call(
        local_kernel,
        grid=(NC,),
        in_specs=[tok_spec()] * 4,
        out_specs=[head_spec()] * 5 + [pl.BlockSpec((1, HL, E, E), lambda i: (i, 0, 0, 0))],
        out_shape=[major] * 5 + [jax.ShapeDtypeStruct((NC, HL, E, E), bf16)],
        scratch_shapes=[pltpu.VMEM((HL, E, E), f32)],
        compiler_params=params(),
        cost_estimate=cost(2 * T * HL * (2 * C * E + 2 * E * E), 30 * MIB),
        name="local_part",
    )(queries, keys, values, out_grad)


def stats_kernel(q_ref, g_ref, a_ref, s_ref, gain_ref, o_ref):
    sq = jnp.zeros((C, E), f32)
    pr = jnp.zeros((C, E), f32)
    for h in range(HL):
        att = a_ref[h].astype(f32) + mm(q_ref[h], s_ref[h].astype(bf16))
        up = gain_ref[h : h + 1, :] * g_ref[h].astype(f32)
        sq = sq + att * att
        pr = pr + up * att
    o_ref[0:1, :] = jnp.sum(sq.T, axis=0, keepdims=True)
    o_ref[1:2, :] = jnp.sum(pr.T, axis=0, keepdims=True)


def stats(qh, gh, att, state, gain):
    return pl.pallas_call(
        stats_kernel,
        grid=(NC,),
        in_specs=[head_spec()] * 3 + [whole((HL, E, E)), whole((HL, E))],
        out_specs=pl.BlockSpec((2, C), lambda i: (0, i)),
        out_shape=jax.ShapeDtypeStruct((2, T), f32),
        compiler_params=params(),
        cost_estimate=cost(2 * T * HL * E * E, 10 * MIB),
        name="stats",
    )(qh, gh, att, state, gain)


def scales(sums):
    rms = jnp.sqrt(sums[0:1, :] / WIDTH + epsilon)
    a = 1.0 / rms
    b = sums[1:2, :] / (WIDTH * rms * rms) * a
    a = jnp.broadcast_to(a, (E, C)).T
    b = jnp.broadcast_to(b, (E, C)).T
    return a, b


def pre_kernel(q_ref, g_ref, a_ref, s_ref, gain_ref, sums_ref, p_ref, wl_ref, w_ref, acc):
    step = pl.program_id(0)

    @pl.when(step == 0)
    def _():
        acc[...] = jnp.zeros_like(acc)

    a, b = scales(sums_ref)
    for h in range(HL):
        q = q_ref[h]
        att = a_ref[h].astype(f32) + mm(q, s_ref[h].astype(bf16))
        up = gain_ref[h : h + 1, :] * g_ref[h].astype(f32)
        p = (up * a - att * b).astype(bf16)
        p_ref[h] = p
        wl_ref[0, h] = acc[h].astype(bf16)
        acc[h] += mm_tn(q, p)

    @pl.when(step == NC - 1)
    def _():
        low = lax.broadcasted_iota(jnp.int32, (HL, 8, E), 1) < 4
        for h in range(0, HL, 2):
            x = acc[h].reshape(HL, 8, E)
            y = acc[h + 1].reshape(HL, 8, E)
            w_ref[:, 0, 4 * h : 4 * h + 8, :] = jnp.where(low, x, pltpu.roll(y, 4, 1))
            w_ref[:, 1, 4 * h : 4 * h + 8, :] = jnp.where(low, pltpu.roll(x, 4, 1), y)


def pre_part(qh, gh, att, state, gain, sums):
    back = lambda i: (0, NC - 1 - i, 0)
    return pl.pallas_call(
        pre_kernel,
        grid=(NC,),
        in_specs=[head_spec(back)] * 3
        + [whole((HL, E, E)), whole((HL, E)), pl.BlockSpec((2, C), lambda i: (0, NC - 1 - i))],
        out_specs=[
            head_spec(back),
            pl.BlockSpec((1, HL, E, E), lambda i: (NC - 1 - i, 0, 0, 0)),
            whole((16, 2, 64, E)),
        ],
        out_shape=[
            jax.ShapeDtypeStruct((HL, T, E), bf16),
            jax.ShapeDtypeStruct((NC, HL, E, E), bf16),
            jax.ShapeDtypeStruct((16, 2, 64, E), f32),
        ],
        scratch_shapes=[pltpu.VMEM((HL, E, E), f32)],
        compiler_params=params(),
        cost_estimate=cost(4 * T * HL * E * E, 16 * MIB),
        name="pre_part",
    )(qh, gh, att, state, gain, sums)


def query_kernel(q_ref, k_ref, v_ref, p_ref, a_ref, s_ref, loc_ref, gain_ref, sums_ref, n_ref, qg_ref, gv_ref):
    mask = causal()
    a, _ = scales(sums_ref)
    normed = []
    grads = []
    for h in range(HL):
        state = s_ref[h].astype(bf16)
        att = a_ref[h].astype(f32) + mm(q_ref[h], state)
        normed.append((gain_ref[h : h + 1, :] * att * a).astype(bf16))
        p = p_ref[h]
        gv = jnp.where(mask, mm_nt(p, v_ref[h]), 0.0).astype(bf16)
        gv_ref[h] = gv
        grads.append((mm_nt(p, state) + mm_nt(p, loc_ref[0, h]) + mm(gv, k_ref[h])).astype(bf16))
    n_ref[...] = jnp.swapaxes(jnp.stack(normed), 0, 1)
    qg_ref[...] = jnp.swapaxes(jnp.stack(grads), 0, 1)


def query_part(qh, kh, vh, pre, att, state, loc, gain, sums):
    tok = jax.ShapeDtypeStruct((T, HL, E), bf16)
    return pl.pallas_call(
        query_kernel,
        grid=(NC,),
        in_specs=[head_spec()] * 5
        + [
            whole((HL, E, E)),
            pl.BlockSpec((1, HL, E, E), lambda i: (i, 0, 0, 0)),
            whole((HL, E)),
            pl.BlockSpec((2, C), lambda i: (0, i)),
        ],
        out_specs=[tok_spec()] * 2 + [pl.BlockSpec((HL, C, C), lambda i: (0, i, 0))],
        out_shape=[tok] * 2 + [jax.ShapeDtypeStruct((HL, T, C), bf16)],
        compiler_params=params(),
        cost_estimate=cost(2 * T * HL * (2 * C * E + 3 * E * E), 30 * MIB),
        name="query_part",
    )(qh, kh, vh, pre, att, state, loc, gain, sums)


def keyval_kernel(q_ref, k_ref, v_ref, p_ref, gv_ref, wl_ref, kg_ref, vg_ref):
    mask = causal()
    for h in range(HL):
        later = wl_ref[0, h]
        qk = jnp.where(mask, mm_nt(q_ref[h], k_ref[h]), 0.0).astype(bf16)
        kg_ref[h] = (mm_tn(gv_ref[h], q_ref[h]) + mm_nt(v_ref[h], later)).astype(bf16)
        vg_ref[h] = (mm_tn(qk, p_ref[h]) + mm(k_ref[h], later)).astype(bf16)


def keyval_part(qh, kh, vh, pre, gv, wloc):
    major = jax.ShapeDtypeStruct((HL, T, E), bf16)
    return pl.pallas_call(
        keyval_kernel,
        grid=(NC,),
        in_specs=[head_spec()] * 4
        + [
            pl.BlockSpec((HL, C, C), lambda i: (0, i, 0)),
            pl.BlockSpec((1, HL, E, E), lambda i: (i, 0, 0, 0)),
        ],
        out_specs=[head_spec()] * 2,
        out_shape=[major] * 2,
        compiler_params=params(),
        cost_estimate=cost(2 * T * HL * (3 * C * E + 2 * E * E), 28 * MIB),
        name="keyval_part",
    )(qh, kh, vh, pre, gv, wloc)


def final_kernel(k_ref, v_ref, kp_ref, vp_ref, l_ref, kg_ref, vg_ref):
    low = lax.broadcasted_iota(jnp.int32, (HL, 8, E), 1) < 4
    kg = []
    vg = []
    for h in range(0, HL, 2):
        even = l_ref[:, 0, 4 * h : 4 * h + 8, :]
        odd = l_ref[:, 1, 4 * h : 4 * h + 8, :]
        first = jnp.where(low, even, pltpu.roll(odd, 4, 1)).reshape(E, E).astype(bf16)
        second = jnp.where(low, pltpu.roll(even, 4, 1), odd).reshape(E, E).astype(bf16)
        for at, later in ((h, first), (h + 1, second)):
            kg.append((kp_ref[at].astype(f32) + mm_nt(v_ref[at], later)).astype(bf16))
            vg.append((vp_ref[at].astype(f32) + mm(k_ref[at], later)).astype(bf16))
    kg_ref[...] = jnp.swapaxes(jnp.stack(kg), 0, 1)
    vg_ref[...] = jnp.swapaxes(jnp.stack(vg), 0, 1)


def final_part(kh, vh, kpart, vpart, later):
    tok = jax.ShapeDtypeStruct((T, HL, E), bf16)
    return pl.pallas_call(
        final_kernel,
        grid=(NC,),
        in_specs=[head_spec()] * 4 + [whole((16, 2, 64, E))],
        out_specs=[tok_spec()] * 2,
        out_shape=[tok] * 2,
        compiler_params=params(),
        cost_estimate=cost(4 * T * HL * E * E, 19 * MIB),
        name="final_part",
    )(kh, vh, kpart, vpart, later)


def swap(pieces):
    return lax.all_to_all(pieces, "seq", 0, 0, tiled=True)


def body(queries, keys, values, out_grad, gain, entry_state):
    mine = lax.axis_index("seq")
    start = lax.dynamic_slice_in_dim(entry_state.reshape(N, 64, E), mine, 1, 0)[0]
    kv = kv_sums(keys, values).reshape(N, 64, E)
    got = swap(kv)
    qh, kh, vh, gh, att, loc = local_part(queries, keys, values, out_grad)
    state = swap(prefix(got, start)).reshape(HL, E, E)
    sums = lax.psum(stats(qh, gh, att, state, gain), "head")
    pre, wloc, w = pre_part(qh, gh, att, state, gain, sums)
    back = swap(w.reshape(N, 64, E))
    normed, query_grad, gv = query_part(qh, kh, vh, pre, att, state, loc, gain, sums)
    rest, total = suffix(back)
    later = swap(rest).reshape(16, 2, 64, E)
    kpart, vpart = keyval_part(qh, kh, vh, pre, gv, wloc)
    key_grad, value_grad = final_part(kh, vh, kpart, vpart, later)
    return normed, query_grad, key_grad, value_grad, total.reshape(HL, 4, E)


def solution(mesh):
    tok = P("seq", "head", None)
    return jax.shard_map(
        body,
        mesh=mesh,
        in_specs=(tok, tok, tok, tok, P("head", None), P("head", None, None)),
        out_specs=(tok, tok, tok, tok, P("head", "seq", None)),
        check_vma=False,
    )
```

time: 600 us -> 163 us (0.27)
  waiting for transfers between devices: 232 us -> 16.9 us
  other arithmetic: 173 us -> 0 us
  matrix products: 111 us -> 0 us
  Pallas kernels: 0 us -> 56.7 us
  blocking collectives: 8.7 us -> 34.7 us
  local copies, waits for them, and re-layouts: 58.7 us -> 34.4 us
  starting transfers between devices: 0.3 us -> 18.7 us
  between operations: 13.8 us -> 0.79 us
    all_gather x2 -> x0, waiting for transfers between devices: 214 us -> none  [carried_in(): pieces = lax.all_gather(value, axis)]
    select_n x62 -> x0, other arithmetic: 164 us -> none  [step(): return jnp.where(position < mine, longer, subtotal)]
    dot_general x12 -> x0, matrix products: 111 us -> none  [the longest x1 14.6 us: body(): jnp.einsum('hts,she->the', causal_qk, values, preferred_element_type=f32)]
    pallas_call x0 -> x9, Pallas kernels: none -> 56.7 us  [the longest x1 12.7 us: query_part(): pl.pallas_call(query_kernel, grid=(NC,), in_specs=[head_spec()] * 5 + [wh...]
    all_to_all x0 -> x1, blocking collectives: none -> 26.1 us  [swap(): return lax.all_to_all(pieces, 'seq', 0, 0, tiled=True)]
    rev x1 -> x0, local copies, waits for them, and re-layouts: 23 us -> none  [carried_in(): pieces = pieces[::-1]]
    all_to_all x0 -> x3, starting transfers between devices: none -> 18.7 us  [swap(): return lax.all_to_all(pieces, 'seq', 0, 0, tiled=True)]
    reduce_scatter x1 -> x0, waiting for transfers between devices: 18.5 us -> none  [body(): lax.psum_scatter(local_w, 'seq', scatter_dimension=1, tiled=True)]
  transfers between devices with their start and end apart: 3 -> 3, of which waited for: 3 -> 1; matrix products, arithmetic and copies ran while one was open for 13% -> 0% of each run, Pallas kernels for 0% -> 22%
where the time goes in v1:
time: 163 us; the launch traced here: 162 us
  Pallas kernels  56.7 us (35%)
  blocking collectives  34.7 us (21%)
  local copies, waits for them, and re-layouts  34.4 us (21%)
  starting transfers between devices  18.7 us (11%)
  waiting for transfers between devices  16.9 us (10%)
    unnamed x50, local copies, waits for them, and re-layouts  34.4 us
    all_to_all x1, blocking collectives, swap(): return lax.all_to_all(pieces, 'seq', 0, 0, tiled=True)  26.1 us
    all_to_all x3, starting transfers between devices, swap(): return lax.all_to_all(pieces, 'seq', 0, 0, tiled=True)  18.7 us
    all_to_all x3, waiting for transfers between devices, swap(): return lax.all_to_all(pieces, 'seq', 0, 0, tiled=True)  16.9 us
    pallas_call x1, Pallas kernels, query_part(): pl.pallas_call(query_kernel, grid=(NC,), in_specs=[head_spec()] * 5 + [wh...  12.7 us
    pallas_call x1, Pallas kernels, keyval_part(): pl.pallas_call(keyval_kernel, grid=(NC,), in_specs=[head_spec()] * 4 + [p...  11.9 us
    pallas_call x1, Pallas kernels, local_part(): pl.pallas_call(local_kernel, grid=(NC,), in_specs=[tok_spec()] * 4, out_s...  11.5 us
    psum x1, blocking collectives, body(): sums = lax.psum(stats(qh, gh, att, state, gain), 'head')  8.56 us
  transfers between devices with their start and end apart: 3, of which 1 were waited for; matrix products, arithmetic and copies ran while one was open for 0% of the time, Pallas kernels for 22%

profile of v1, /device:TPU:1, one launch (start us, length us, event | category | flops | bytes accessed | tf_op | source)
XLA Modules:
  0.0 162.2 jit_solution(294533406086275695)
XLA Ops:
  0.7 2.0 %copy-done.10 = bf16[768,16,128]{2,1,0:T(8,128)(2,1)S(1)} copy-done((bf16[768,16,128]{2,1,0:T(8,128)(2,1)S(1)}, bf16[768,16,128]{2,1,0:T(8,128)(2,1)}, u32[]{:S(2)}) %copy-start.10) | copy-done | bytes 3145752
  2.6 1.9 %copy-done.11 = bf16[768,16,128]{2,1,0:T(8,128)(2,1)S(1)} copy-done((bf16[768,16,128]{2,1,0:T(8,128)(2,1)S(1)}, bf16[768,16,128]{2,1,0:T(8,128)(2,1)}, u32[]{:S(2)}) %copy-start.11) | copy-done | bytes 3145752
  4.5 3.2 %kv_sums.1 = f32[16,128,128]{2,1,0:T(8,128)} custom-call(bf16[768,16,128]{2,1,0:T(8,128)(2,1)S(1)} %copy-done.10, bf16[768,16,128]{2,1,0:T(8,128)(2,1)S(1)} %copy-done.11), custom_call_target="tpu_custom_call" | custom-call | flops 402653184 | bytes 7340032 | tf_op jit(solution)/shard_map/kv_sums/pallas_call | solution.py:76
  7.7 9.6 %all-to-all-start = ((f32[32,64,128]{2,1,0:T(8,128)}), f32[32,64,128]{2,1,0:T(8,128)S(1)}, u32[]{:S(2)}, u32[]{:S(2)}) async-start(f32[32,64,128]{2,1,0:T(8,128)} %bitcast), calls=%async_computation | async-start | bytes 2097152 | tf_op jit(solution)/shard_map/all_to_all | solution.py:342
  17.4 16.9 %all-to-all-done.r_ref = f32[32,64,128]{2,1,0:T(8,128)S(1)} async-done(((f32[32,64,128]{2,1,0:T(8,128)}), f32[32,64,128]{2,1,0:T(8,128)S(1)}, u32[]{:S(2)}, u32[]{:S(2)}) %all-to-all-start) | async-done | bytes 1048608 | tf_op jit(solution)/shard_map/all_to_all | solution.py:342
  35.3 4.5 %all-to-all-start.1 = ((f32[32,64,128]{2,1,0:T(8,128)}), f32[32,64,128]{2,1,0:T(8,128)}, u32[]{:S(2)}, u32[]{:S(2)}) async-start(f32[32,64,128]{2,1,0:T(8,128)} %prefix.1), calls=%async_computation.1 | async-start | bytes 2097152 | tf_op jit(solution)/shard_map/all_to_all | solution.py:342
  39.8 11.5 %local_part.1 = (bf16[16,768,128]{2,1,0:T(8,128)(2,1)S(1)}, bf16[16,768,128]{2,1,0:T(8,128)(2,1)S(1)}, bf16[16,768,128]{2,1,0:T(8,128)(2,1)S(1)}, bf16[16,768,12...) custom-call(bf16[768,16,128]{2,1,0:T(8,128)(2,1)} %q_ref.1, ...), custom_call_target="tpu_custom_call" | custom-call | flops 2415919104 | bytes 31457280 | tf_op jit(solution)/shard_map/local_part/pallas_call | solution.py:149
  51.3 1.7 %copy-done.2 = bf16[16,768,128]{2,1,0:T(8,128)(2,1)} copy-done((bf16[16,768,128]{2,1,0:T(8,128)(2,1)}, bf16[16,768,128]{2,1,0:T(8,128)(2,1)S(1)}, u32[]{:S(2)}) %copy-start.2) | copy-done | bytes 3145752
  53.0 1.7 %copy-done.5 = bf16[16,768,128]{2,1,0:T(8,128)(2,1)} copy-done((bf16[16,768,128]{2,1,0:T(8,128)(2,1)}, bf16[16,768,128]{2,1,0:T(8,128)(2,1)S(1)}, u32[]{:S(2)}) %copy-start.5) | copy-done | bytes 3145752
  54.7 1.7 %copy-done.12 = bf16[16,768,128]{2,1,0:T(8,128)(2,1)} copy-done((bf16[16,768,128]{2,1,0:T(8,128)(2,1)}, bf16[16,768,128]{2,1,0:T(8,128)(2,1)S(1)}, u32[]{:S(2)}) %copy-start.12) | copy-done | bytes 3145752
  56.3 1.1 copy-done.19
  57.5 1.9 %copy-done.8 = bf16[16,768,128]{2,1,0:T(8,128)(2,1)S(1)} copy-done((bf16[16,768,128]{2,1,0:T(8,128)(2,1)S(1)}, bf16[16,768,128]{2,1,0:T(8,128)(2,1)}, u32[]{:S(2)}) %copy-start.8) | copy-done | bytes 3145752
  59.4 1.9 %copy-done.13 = bf16[16,768,128]{2,1,0:T(8,128)(2,1)S(1)} copy-done((bf16[16,768,128]{2,1,0:T(8,128)(2,1)S(1)}, bf16[16,768,128]{2,1,0:T(8,128)(2,1)}, u32[]{:S(2)}) %copy-start.13) | copy-done | bytes 3145752
  61.3 4.2 %stats.1 = f32[2,768]{1,0:T(2,128)S(1)} custom-call(bf16[16,768,128]{2,1,0:T(8,128)(2,1)S(1)} %get-tuple-element.23.q_ref, bf16[16,768,128]{2,1,0:T(8,128)(2,1)S(1)} %copy-done.13, bf16[16,768,128]{2,1,0:T(8,128)(2,1)S(1)} %copy-done.8, f32[16,128,128]{2,1,0:T(8,128)} %bitcast.3.s_ref, f32[16,128]{1,0:T(8,128)S(1)} %copy-done.24), custom_call_target="tpu_custom_call" | custom-call | flops 402653184 | bytes 10485760 | tf_op jit(solution)/shard_map/stats/pallas_call | solution.py:175
  65.5 8.6 %psum.7.sums_ref = f32[2,768]{1,0:T(2,128)S(1)} all-reduce(f32[2,768]{1,0:T(2,128)S(1)} %stats.1), channel_id=1, replica_groups=mesh['seq'=32,'head'=4] {'head'}, use_global_device_ids=true, to_apply=%region_0.0 | all-reduce | flops 1536 | bytes 12288 | tf_op jit(solution)/shard_map/psum | solution.py:352
  74.1 1.9 %copy-done.14 = bf16[16,768,128]{2,1,0:T(8,128)(2,1)S(1)} copy-done((bf16[16,768,128]{2,1,0:T(8,128)(2,1)S(1)}, bf16[16,768,128]{2,1,0:T(8,128)(2,1)}, u32[]{:S(2)}) %copy-start.14) | copy-done | bytes 3145752
  76.0 5.2 %pre_part.1 = (bf16[16,768,128]{2,1,0:T(8,128)(2,1)S(1)}, bf16[3,16,128,128]{3,2,1,0:T(8,128)(2,1)S(1)}, f32[16,2,64,128]{3,2,1,0:T(8,128)S(1)}) custom-call(bf16[16,768,128]{2,1,0:T(8,128)(2,1)S(1)} %get-tuple-element.23.q_ref, bf16[16,768,128]{2,1,0:T(8,128)(2,1)S(1)} %copy-done.14, bf16[16,768,128]{2,1,0:T(8,128)(2,1)} %get-tuple-element.27.a_ref, ...), custom_call_target="tpu_custom_call" | custom-call | flops 805306368 | bytes 16777216 | tf_op jit(solution)/shard_map/pre_part/pallas_call | solution.py:225
  81.2 1.7 %copy-done.9 = bf16[16,768,128]{2,1,0:T(8,128)(2,1)} copy-done((bf16[16,768,128]{2,1,0:T(8,128)(2,1)}, bf16[16,768,128]{2,1,0:T(8,128)(2,1)S(1)}, u32[]{:S(2)}) %copy-start.9) | copy-done | bytes 3145752
  82.8 26.1 %all_to_all.20.r_ref = f32[32,64,128]{2,1,0:T(8,128)S(1)} all-to-all(f32[32,64,128]{2,1,0:T(8,128)S(1)} %bitcast.9), channel_id=1, replica_groups=mesh['seq'=32,'head'=4] {'seq'}, dimensions={0} | all-to-all | bytes 2097152 | tf_op jit(solution)/shard_map/all_to_all | solution.py:342
  110.7 4.6 %all-to-all-start.3 = ((f32[32,64,128]{2,1,0:T(8,128)}), f32[32,64,128]{2,1,0:T(8,128)}, u32[]{:S(2)}, u32[]{:S(2)}) async-start(f32[32,64,128]{2,1,0:T(8,128)} %copy-done.23), calls=%async_computation.3 | async-start | bytes 2097152 | tf_op jit(solution)/shard_map/all_to_all | solution.py:342
  115.3 1.9 %copy-done.3 = bf16[16,768,128]{2,1,0:T(8,128)(2,1)S(1)} copy-done((bf16[16,768,128]{2,1,0:T(8,128)(2,1)S(1)}, bf16[16,768,128]{2,1,0:T(8,128)(2,1)}, u32[]{:S(2)}) %copy-start.3) | copy-done | bytes 3145752
  117.2 1.9 %copy-done.6 = bf16[16,768,128]{2,1,0:T(8,128)(2,1)S(1)} copy-done((bf16[16,768,128]{2,1,0:T(8,128)(2,1)S(1)}, bf16[16,768,128]{2,1,0:T(8,128)(2,1)}, u32[]{:S(2)}) %copy-start.6) | copy-done | bytes 3145752
  119.1 1.4 copy-done.20
  120.5 12.7 %query_part.1 = (bf16[768,16,128]{2,1,0:T(8,128)(2,1)}, bf16[768,16,128]{2,1,0:T(8,128)(2,1)}, bf16[16,768,256]{2,1,0:T(8,128)(2,1)}) custom-call(bf16[16,768,128]{2,1,0:T(8,128)(2,1)S(1)} %get-tuple-element.23.q_ref, bf16[16,768,128]{2,1,0:T(8,128)(2,1)S(1)} %copy-done.3, bf16[16,768,128]{2,1,0:T(8,128)(2,1)S(1)} %copy-done.6, ...), custom_call_target="tpu_custom_call" | custom-call | flops 2818572288 | bytes 31457280 | tf_op jit(solution)/shard_map/query_part/pallas_call | solution.py:266
  133.2 11.9 %keyval_part.1 = (bf16[16,768,128]{2,1,0:T(8,128)(2,1)S(1)}, bf16[16,768,128]{2,1,0:T(8,128)(2,1)S(1)}) custom-call(bf16[16,768,128]{2,1,0:T(8,128)(2,1)S(1)} %get-tuple-element.23.q_ref, bf16[16,768,128]{2,1,0:T(8,128)(2,1)S(1)} %copy-done.3, bf16[16,768,128]{2,1,0:T(8,128)(2,1)} %copy-done.5, bf16[16,768,128]{2,1,0:T(8,128)(2,1)} %copy-done.9, ...), custom_call_target="tpu_custom_call" | custom-call | flops 3221225472 | bytes 29360128 | tf_op jit(solution)/shard_map/keyval_part/pallas_call | solution.py:295
  145.2 1.7 %copy-done.15 = bf16[16,768,128]{2,1,0:T(8,128)(2,1)} copy-done((bf16[16,768,128]{2,1,0:T(8,128)(2,1)}, bf16[16,768,128]{2,1,0:T(8,128)(2,1)S(1)}, u32[]{:S(2)}) %copy-start.15) | copy-done | bytes 3145752
  146.8 1.6 %copy-done.17 = bf16[16,768,128]{2,1,0:T(8,128)(2,1)} copy-done((bf16[16,768,128]{2,1,0:T(8,128)(2,1)}, bf16[16,768,128]{2,1,0:T(8,128)(2,1)S(1)}, u32[]{:S(2)}) %copy-start.17) | copy-done | bytes 3145752
  148.4 1.9 %copy-done.4 = bf16[16,768,128]{2,1,0:T(8,128)(2,1)S(1)} copy-done((bf16[16,768,128]{2,1,0:T(8,128)(2,1)S(1)}, bf16[16,768,128]{2,1,0:T(8,128)(2,1)}, u32[]{:S(2)}) %copy-start.4) | copy-done | bytes 3145752
  150.3 1.9 %copy-done.7 = bf16[16,768,128]{2,1,0:T(8,128)(2,1)S(1)} copy-done((bf16[16,768,128]{2,1,0:T(8,128)(2,1)S(1)}, bf16[16,768,128]{2,1,0:T(8,128)(2,1)}, u32[]{:S(2)}) %copy-start.7) | copy-done | bytes 3145752
  152.2 1.9 %copy-done.16 = bf16[16,768,128]{2,1,0:T(8,128)(2,1)S(1)} copy-done((bf16[16,768,128]{2,1,0:T(8,128)(2,1)S(1)}, bf16[16,768,128]{2,1,0:T(8,128)(2,1)}, u32[]{:S(2)}) %copy-start.16) | copy-done | bytes 3145752
  154.1 1.9 %copy-done.18 = bf16[16,768,128]{2,1,0:T(8,128)(2,1)S(1)} copy-done((bf16[16,768,128]{2,1,0:T(8,128)(2,1)S(1)}, bf16[16,768,128]{2,1,0:T(8,128)(2,1)}, u32[]{:S(2)}) %copy-start.18) | copy-done | bytes 3145752
  156.0 6.2 %final_part.1 = (bf16[768,16,128]{2,1,0:T(8,128)(2,1)}, bf16[768,16,128]{2,1,0:T(8,128)(2,1)}) custom-call(bf16[16,768,128]{2,1,0:T(8,128)(2,1)S(1)} %copy-done.4, bf16[16,768,128]{2,1,0:T(8,128)(2,1)S(1)} %copy-done.7, bf16[16,768,128]{2,1,0:T(8,128)(2,1)S(1)} %copy-done.16, bf16[16,768,128]{2,1,0:T(8,128)(2,1)S(1)} %copy-done.18, ...), custom_call_target="tpu_custom_call" | custom-call | flops 805306368 | bytes 19922944 | tf_op jit(solution)/shard_map/final_part/pallas_call | solution.py:329
  (36 shorter events, 2.8 us)
Async XLA Ops:
  0.6 16.7 %copy-start = (f32[16,128,128]{2,1,0:T(8,128)S(1)}, f32[16,128,128]{2,1,0:T(8,128)}, u32[]{:S(2)}) copy-start(f32[16,128,128]{2,1,0:T(8,128)} %param.11) | copy-start | bytes 3145732
  0.6 2.0 %copy-start.10 = (bf16[768,16,128]{2,1,0:T(8,128)(2,1)S(1)}, bf16[768,16,128]{2,1,0:T(8,128)(2,1)}, u32[]{:S(2)}) copy-start(bf16[768,16,128]{2,1,0:T(8,128)(2,1)} %k_ref.3) | copy-start | bytes 9437188
  2.6 1.9 %copy-start.11 = (bf16[768,16,128]{2,1,0:T(8,128)(2,1)S(1)}, bf16[768,16,128]{2,1,0:T(8,128)(2,1)}, u32[]{:S(2)}) copy-start(bf16[768,16,128]{2,1,0:T(8,128)(2,1)} %v_ref.3) | copy-start | bytes 9437188
  7.7 26.5 %all-to-all-start = ((f32[32,64,128]{2,1,0:T(8,128)}), f32[32,64,128]{2,1,0:T(8,128)S(1)}, u32[]{:S(2)}, u32[]{:S(2)}) async-start(f32[32,64,128]{2,1,0:T(8,128)} %bitcast), calls=%async_computation | async-start | bytes 2097152 | tf_op jit(solution)/shard_map/all_to_all | solution.py:342
  35.3 22.2 %all-to-all-start.1 = ((f32[32,64,128]{2,1,0:T(8,128)}), f32[32,64,128]{2,1,0:T(8,128)}, u32[]{:S(2)}, u32[]{:S(2)}) async-start(f32[32,64,128]{2,1,0:T(8,128)} %prefix.1), calls=%async_computation.1 | async-start | bytes 2097152 | tf_op jit(solution)/shard_map/all_to_all | solution.py:342
  39.8 17.7 %copy-start.24 = (f32[16,128]{1,0:T(8,128)S(1)}, f32[16,128]{1,0:T(8,128)}, u32[]{:S(2)}) copy-start(f32[16,128]{1,0:T(8,128)} %gain_ref.5) | copy-start | bytes 24580
  51.3 1.7 %copy-start.2 = (bf16[16,768,128]{2,1,0:T(8,128)(2,1)}, bf16[16,768,128]{2,1,0:T(8,128)(2,1)S(1)}, u32[]{:S(2)}) copy-start(bf16[16,768,128]{2,1,0:T(8,128)(2,1)S(1)} %get-tuple-element.24.k_ref) | copy-start | bytes 9437188
  53.0 1.7 %copy-start.5 = (bf16[16,768,128]{2,1,0:T(8,128)(2,1)}, bf16[16,768,128]{2,1,0:T(8,128)(2,1)S(1)}, u32[]{:S(2)}) copy-start(bf16[16,768,128]{2,1,0:T(8,128)(2,1)S(1)} %get-tuple-element.25.v_ref) | copy-start | bytes 9437188
  54.7 1.7 %copy-start.12 = (bf16[16,768,128]{2,1,0:T(8,128)(2,1)}, bf16[16,768,128]{2,1,0:T(8,128)(2,1)S(1)}, u32[]{:S(2)}) copy-start(bf16[16,768,128]{2,1,0:T(8,128)(2,1)S(1)} %get-tuple-element.26.g_ref) | copy-start | bytes 9437188
  56.3 1.1 copy-start.19
  57.5 1.9 %copy-start.8 = (bf16[16,768,128]{2,1,0:T(8,128)(2,1)S(1)}, bf16[16,768,128]{2,1,0:T(8,128)(2,1)}, u32[]{:S(2)}) copy-start(bf16[16,768,128]{2,1,0:T(8,128)(2,1)} %get-tuple-element.27.a_ref) | copy-start | bytes 9437188
  59.4 1.9 %copy-start.13 = (bf16[16,768,128]{2,1,0:T(8,128)(2,1)S(1)}, bf16[16,768,128]{2,1,0:T(8,128)(2,1)}, u32[]{:S(2)}) copy-start(bf16[16,768,128]{2,1,0:T(8,128)(2,1)} %copy-done.12) | copy-start | bytes 9437188
  74.1 1.9 %copy-start.14 = (bf16[16,768,128]{2,1,0:T(8,128)(2,1)S(1)}, bf16[16,768,128]{2,1,0:T(8,128)(2,1)}, u32[]{:S(2)}) copy-start(bf16[16,768,128]{2,1,0:T(8,128)(2,1)} %copy-done.12) | copy-start | bytes 9437188
  81.2 1.7 %copy-start.9 = (bf16[16,768,128]{2,1,0:T(8,128)(2,1)}, bf16[16,768,128]{2,1,0:T(8,128)(2,1)S(1)}, u32[]{:S(2)}) copy-start(bf16[16,768,128]{2,1,0:T(8,128)(2,1)S(1)} %get-tuple-element.28.p_ref) | copy-start | bytes 9437188
  82.8 26.8 %copy-start.21 = (bf16[3,16,128,128]{3,2,1,0:T(8,128)(2,1)}, bf16[3,16,128,128]{3,2,1,0:T(8,128)(2,1)S(1)}, u32[]{:S(2)}) copy-start(bf16[3,16,128,128]{3,2,1,0:T(8,128)(2,1)S(1)} %get-tuple-element.33.wl_ref) | copy-start | bytes 4718596
  109.7 1.0 copy-start.23
  110.7 37.8 %all-to-all-start.3 = ((f32[32,64,128]{2,1,0:T(8,128)}), f32[32,64,128]{2,1,0:T(8,128)}, u32[]{:S(2)}, u32[]{:S(2)}) async-start(f32[32,64,128]{2,1,0:T(8,128)} %copy-done.23), calls=%async_computation.3 | async-start | bytes 2097152 | tf_op jit(solution)/shard_map/all_to_all | solution.py:342
  115.3 1.9 %copy-start.3 = (bf16[16,768,128]{2,1,0:T(8,128)(2,1)S(1)}, bf16[16,768,128]{2,1,0:T(8,128)(2,1)}, u32[]{:S(2)}) copy-start(bf16[16,768,128]{2,1,0:T(8,128)(2,1)} %copy-done.2) | copy-start | bytes 9437188
  117.2 1.9 %copy-start.6 = (bf16[16,768,128]{2,1,0:T(8,128)(2,1)S(1)}, bf16[16,768,128]{2,1,0:T(8,128)(2,1)}, u32[]{:S(2)}) copy-start(bf16[16,768,128]{2,1,0:T(8,128)(2,1)} %copy-done.5) | copy-start | bytes 9437188
  119.1 1.4 copy-start.20
  120.5 12.7 %copy-start.22 = (bf16[3,16,128,128]{3,2,1,0:T(8,128)(2,1)S(1)}, bf16[3,16,128,128]{3,2,1,0:T(8,128)(2,1)}, u32[]{:S(2)}) copy-start(bf16[3,16,128,128]{3,2,1,0:T(8,128)(2,1)} %copy-done.21) | copy-start | bytes 4718596
  145.1 1.7 %copy-start.15 = (bf16[16,768,128]{2,1,0:T(8,128)(2,1)}, bf16[16,768,128]{2,1,0:T(8,128)(2,1)S(1)}, u32[]{:S(2)}) copy-start(bf16[16,768,128]{2,1,0:T(8,128)(2,1)S(1)} %get-tuple-element.34.kp_ref) | copy-start | bytes 9437188
  146.8 1.6 %copy-start.17 = (bf16[16,768,128]{2,1,0:T(8,128)(2,1)}, bf16[16,768,128]{2,1,0:T(8,128)(2,1)S(1)}, u32[]{:S(2)}) copy-start(bf16[16,768,128]{2,1,0:T(8,128)(2,1)S(1)} %get-tuple-element.35.vp_ref) | copy-start | bytes 9437188
  148.4 1.9 %copy-start.4 = (bf16[16,768,128]{2,1,0:T(8,128)(2,1)S(1)}, bf16[16,768,128]{2,1,0:T(8,128)(2,1)}, u32[]{:S(2)}) copy-start(bf16[16,768,128]{2,1,0:T(8,128)(2,1)} %copy-done.2) | copy-start | bytes 9437188
  150.3 1.9 %copy-start.7 = (bf16[16,768,128]{2,1,0:T(8,128)(2,1)S(1)}, bf16[16,768,128]{2,1,0:T(8,128)(2,1)}, u32[]{:S(2)}) copy-start(bf16[16,768,128]{2,1,0:T(8,128)(2,1)} %copy-done.5) | copy-start | bytes 9437188
  152.2 1.9 %copy-start.16 = (bf16[16,768,128]{2,1,0:T(8,128)(2,1)S(1)}, bf16[16,768,128]{2,1,0:T(8,128)(2,1)}, u32[]{:S(2)}) copy-start(bf16[16,768,128]{2,1,0:T(8,128)(2,1)} %copy-done.15) | copy-start | bytes 9437188
  154.1 1.9 %copy-start.18 = (bf16[16,768,128]{2,1,0:T(8,128)(2,1)S(1)}, bf16[16,768,128]{2,1,0:T(8,128)(2,1)}, u32[]{:S(2)}) copy-start(bf16[16,768,128]{2,1,0:T(8,128)(2,1)} %copy-done.17) | copy-start | bytes 9437188
  156.0 6.2 %copy-start.1 = (f32[16,128,128]{2,1,0:T(8,128)S(1)}, f32[16,128,128]{2,1,0:T(8,128)}, u32[]{:S(2)}) copy-start(f32[16,128,128]{2,1,0:T(8,128)} %param.11) | copy-start | bytes 3145732

commit v2 on v1

v2 whole, which is shorter than its diff:
```python
import jax
import jax.numpy as jnp
from jax import lax
from jax.experimental import pallas as pl
from jax.experimental.pallas import tpu as pltpu
from jax.sharding import PartitionSpec as P

H = 64
E = 128
T = 768
HL = 16
C = 256
NC = T // C
B = 128
NB = T // B
N = 32
X = 4
WIDTH = H * E
epsilon = 1e-06
f32 = jnp.float32
bf16 = jnp.bfloat16
MIB = 1 << 20


def mm(a, b):
    return lax.dot_general(a, b, (((1,), (0,)), ((), ())), preferred_element_type=f32)


def mm_nt(a, b):
    return lax.dot_general(a, b, (((1,), (1,)), ((), ())), preferred_element_type=f32)


def mm_tn(a, b):
    return lax.dot_general(a, b, (((0,), (0,)), ((), ())), preferred_element_type=f32)


def causal(later=False):
    row = lax.broadcasted_iota(jnp.int32, (C, C), 0)
    col = lax.broadcasted_iota(jnp.int32, (C, C), 1)
    return row <= col if later else col <= row


def heads_first(ref):
    return jnp.swapaxes(ref[...], 0, 1)


def params(vmem=24):
    return pltpu.CompilerParams(vmem_limit_bytes=vmem * MIB)


def cost(flops, moved):
    return pl.CostEstimate(flops=flops, bytes_accessed=moved, transcendentals=0)


HERE = pl.BlockSpec(memory_space=pltpu.VMEM)
ORDER = pl.BlockSpec(memory_space=pl.ANY)
TOK = pl.BlockSpec((C, HL, E), lambda i: (i, 0, 0))
HEAD = pl.BlockSpec((HL, C, E), lambda i: (0, i, 0))
HEAD_BACK = pl.BlockSpec((HL, C, E), lambda i: (0, NC - 1 - i, 0))
CHUNK = pl.BlockSpec((1, HL, E, E), lambda i: (i, 0, 0, 0))
MAJOR = pltpu.HBM((HL, T, E), bf16)
STATES = pltpu.HBM((NC, HL, E, E), bf16)
TOKENS = pltpu.HBM((T, HL, E), bf16)


def rows(step):
    return pl.ds(pl.multiple_of(step * C, C), C)


def far(*arrays):
    return tuple(pltpu.with_memory_space_constraint(a, pltpu.HBM) for a in arrays)


def near(*arrays):
    return tuple(pltpu.with_memory_space_constraint(a, pltpu.VMEM) for a in arrays)


def kv_kernel(k_hbm, v_hbm, o_ref, k_buf, v_buf, sems):
    copies = []
    for i in range(NC):
        at = pl.ds(i * C, C)
        for n, (src, dst) in enumerate(((k_hbm, k_buf), (v_hbm, v_buf))):
            copies.append(pltpu.make_async_copy(src.at[at], dst.at[at], sems.at[i, n]))
            copies[-1].start()
    for i in range(NC):
        copies[2 * i].wait()
        copies[2 * i + 1].wait()
        k = jnp.swapaxes(k_buf[i * C : (i + 1) * C], 0, 1)
        v = jnp.swapaxes(v_buf[i * C : (i + 1) * C], 0, 1)
        for h in range(HL):
            part = mm_tn(k[h], v[h])
            o_ref[h] = part if i == 0 else o_ref[h] + part


def kv_sums(keys, values):
    return pl.pallas_call(
        kv_kernel,
        in_specs=[ORDER, ORDER],
        out_specs=HERE,
        out_shape=pltpu.VMEM((HL, E, E), f32),
        scratch_shapes=[
            pltpu.VMEM((T, HL, E), bf16),
            pltpu.VMEM((T, HL, E), bf16),
            pltpu.SemaphoreType.DMA((NC, 2)),
        ],
        compiler_params=params(32),
        cost_estimate=cost(2 * T * HL * E * E, 7 * MIB),
        name="kv_sums",
    )(*far(keys, values))


def prefix_kernel(r_ref, x_hbm, _, o_ref, x_ref, sem):
    first = pltpu.make_async_copy(x_hbm.at[lax.axis_index("seq")], x_ref, sem)
    first.start()
    first.wait()
    total = x_ref[...]
    for i in range(N):
        o_ref[i] = total
        total = total + r_ref[i]


def prefix(pieces, start, order):
    return pl.pallas_call(
        prefix_kernel,
        in_specs=[HERE, ORDER, ORDER],
        out_specs=HERE,
        out_shape=pltpu.VMEM(pieces.shape, f32),
        scratch_shapes=[pltpu.VMEM((64, E), f32), pltpu.SemaphoreType.DMA],
        compiler_params=params(4),
        cost_estimate=cost(N * 64 * E, 2 * MIB),
        name="prefix",
    )(*near(pieces), *far(start), order)


def suffix_kernel(r_ref, _, o_ref, t_ref):
    total = jnp.zeros_like(t_ref)
    for i in reversed(range(N)):
        o_ref[i] = total
        total = total + r_ref[i]
    t_ref[...] = total


def suffix(pieces, order):
    return pl.pallas_call(
        suffix_kernel,
        in_specs=[HERE, ORDER],
        out_specs=[HERE] * 2,
        out_shape=[
            pltpu.VMEM(pieces.shape, f32),
            jax.ShapeDtypeStruct(pieces.shape[1:], f32),
        ],
        compiler_params=params(4),
        cost_estimate=cost(N * 64 * E, 2 * MIB),
        name="suffix",
    )(*near(pieces), order)


def local_kernel(
    q_ref, k_ref, v_ref, g_ref, _, qh_ref, kh_ref, vh_ref, gh_ref, att_ref, loc_ref, order_ref, acc
):
    @pl.when(pl.program_id(0) == 0)
    def _():
        acc[...] = jnp.zeros_like(acc)
        order_ref[...] = jnp.zeros_like(order_ref)

    mask = causal()
    q = heads_first(q_ref)
    k = heads_first(k_ref)
    v = heads_first(v_ref)
    qh_ref[...] = q
    kh_ref[...] = k
    vh_ref[...] = v
    gh_ref[...] = heads_first(g_ref)
    for h in range(HL):
        qk = jnp.where(mask, mm_nt(q[h], k[h]), 0.0).astype(bf16)
        loc = acc[h].astype(bf16)
        loc_ref[0, h] = loc
        att_ref[h] = (mm(qk, v[h]) + mm(q[h], loc)).astype(bf16)
        acc[h] += mm_tn(k[h], v[h])


def local_part(queries, keys, values, out_grad, order):
    return pl.pallas_call(
        local_kernel,
        grid=(NC,),
        in_specs=[TOK] * 4 + [ORDER],
        out_specs=[HEAD] * 5 + [CHUNK, pl.BlockSpec((8, E), lambda i: (0, 0))],
        out_shape=[MAJOR] * 5 + [STATES, jax.ShapeDtypeStruct((8, E), f32)],
        scratch_shapes=[pltpu.VMEM((HL, E, E), f32)],
        compiler_params=params(32),
        cost_estimate=cost(2 * T * HL * (2 * C * E + 2 * E * E), 30 * MIB),
        name="local_part",
    )(*far(queries, keys, values, out_grad), order)


def stats_kernel(q_ref, g_ref, a_ref, s_ref, gain_ref, att_ref, o_ref, sb_ref):
    step = pl.program_id(0)
    at = rows(step)

    @pl.when(step == 0)
    def _():
        sb_ref[...] = s_ref[...].astype(bf16)

    sq = jnp.zeros((C, E), f32)
    pr = jnp.zeros((C, E), f32)
    for h in range(HL):
        att = a_ref[h, at, :].astype(f32) + mm(q_ref[h, at, :], sb_ref[h])
        att_ref[h, at, :] = att
        up = gain_ref[h : h + 1, :] * g_ref[h, at, :].astype(f32)
        sq = sq + att * att
        pr = pr + up * att
    sq = jnp.sum(sq.T, axis=0, keepdims=True)
    pr = jnp.sum(pr.T, axis=0, keepdims=True)
    for x in range(X):
        o_ref[x, 0:1, :] = sq
        o_ref[x, 1:2, :] = pr


def stats(qh, gh, part, state, gain):
    return pl.pallas_call(
        stats_kernel,
        grid=(NC,),
        in_specs=[HERE] * 5,
        out_specs=[
            HERE,
            pl.BlockSpec((X, 2, C), lambda i: (0, 0, i)),
            pl.BlockSpec((HL, E, E), lambda i: (0, 0, 0)),
        ],
        out_shape=[
            pltpu.VMEM((HL, T, E), f32),
            jax.ShapeDtypeStruct((X, 2, T), f32),
            pltpu.HBM((HL, E, E), bf16),
        ],
        compiler_params=params(12),
        cost_estimate=cost(2 * T * HL * E * E, 10 * MIB),
        name="stats",
    )(*near(qh, gh, part, state, gain))


def scales(sums_ref):
    sums = (sums_ref[0] + sums_ref[1]) + (sums_ref[2] + sums_ref[3])
    rms = jnp.sqrt(sums[0:1, :] / WIDTH + epsilon)
    a = 1.0 / rms
    b = sums[1:2, :] / (WIDTH * rms * rms) * a
    a = jnp.broadcast_to(a, (E, C)).T
    b = jnp.broadcast_to(b, (E, C)).T
    return a, b


def pre_kernel(q_ref, g_ref, a_ref, gain_ref, sums_ref, p_ref, wl_ref, w_ref, acc):
    step = pl.program_id(0)
    at = rows(NC - 1 - step)

    @pl.when(step == 0)
    def _():
        acc[...] = jnp.zeros_like(acc)

    a, b = scales(sums_ref)
    for h in range(HL):
        up = gain_ref[h : h + 1, :] * g_ref[h, at, :].astype(f32)
        p = (up * a - a_ref[h, at, :] * b).astype(bf16)
        p_ref[h] = p
        wl_ref[0, h] = acc[h].astype(bf16)
        acc[h] += mm_tn(q_ref[h, at, :], p)

    @pl.when(step == NC - 1)
    def _():
        low = lax.broadcasted_iota(jnp.int32, (HL, 8, E), 1) < 4
        for h in range(0, HL, 2):
            x = acc[h].reshape(HL, 8, E)
            y = acc[h + 1].reshape(HL, 8, E)
            w_ref[:, 0, 4 * h : 4 * h + 8, :] = jnp.where(low, x, pltpu.roll(y, 4, 1))
            w_ref[:, 1, 4 * h : 4 * h + 8, :] = jnp.where(low, pltpu.roll(x, 4, 1), y)


def pre_part(qh, gh, att, gain, sums):
    return pl.pallas_call(
        pre_kernel,
        grid=(NC,),
        in_specs=[HERE] * 4 + [pl.BlockSpec((X, 2, C), lambda i: (0, 0, NC - 1 - i))],
        out_specs=[
            HEAD_BACK,
            pl.BlockSpec((1, HL, E, E), lambda i: (NC - 1 - i, 0, 0, 0)),
            HERE,
        ],
        out_shape=[MAJOR, STATES, pltpu.VMEM((16, 2, 64, E), f32)],
        scratch_shapes=[pltpu.VMEM((HL, E, E), f32)],
        compiler_params=params(16),
        cost_estimate=cost(4 * T * HL * E * E, 16 * MIB),
        name="pre_part",
    )(*near(qh, gh, att, gain), sums)


def query_kernel(
    q_ref, k_ref, v_ref, p_ref, a_ref, s_ref, loc_ref, gain_ref, sums_ref, n_ref, qg_ref, order_ref
):
    mask = causal()
    order_ref[...] = jnp.zeros_like(order_ref)
    a, _ = scales(sums_ref)
    normed = []
    grads = []
    for h in range(HL):
        state = s_ref[h]
        att = a_ref[h].astype(f32) + mm(q_ref[h], state)
        normed.append((gain_ref[h : h + 1, :] * att * a).astype(bf16))
        p = p_ref[h]
        gv = jnp.where(mask, mm_nt(p, v_ref[h]), 0.0).astype(bf16)
        grads.append((mm_nt(p, state) + mm_nt(p, loc_ref[0, h]) + mm(gv, k_ref[h])).astype(bf16))
    n_ref[...] = jnp.swapaxes(jnp.stack(normed), 0, 1)
    qg_ref[...] = jnp.swapaxes(jnp.stack(grads), 0, 1)


def query_part(qh, kh, vh, pre, part, state, loc, gain, sums):
    return pl.pallas_call(
        query_kernel,
        grid=(NC,),
        in_specs=[HEAD] * 5
        + [
            pl.BlockSpec((HL, E, E), lambda i: (0, 0, 0)),
            CHUNK,
            pl.BlockSpec((HL, E), lambda i: (0, 0)),
            pl.BlockSpec((X, 2, C), lambda i: (0, 0, i)),
        ],
        out_specs=[TOK] * 2 + [pl.BlockSpec((8, E), lambda i: (0, 0))],
        out_shape=[TOKENS] * 2 + [jax.ShapeDtypeStruct((8, E), f32)],
        compiler_params=params(32),
        cost_estimate=cost(2 * T * HL * (2 * C * E + 3 * E * E), 30 * MIB),
        name="query_part",
    )(*far(qh, kh, vh, pre, part, state, loc, gain, sums))


def keyval_kernel(q_ref, k_ref, v_ref, p_ref, wl_ref, _, kg_ref, vg_ref):
    mask = causal(later=True)
    for h in range(HL):
        later = wl_ref[0, h]
        q = q_ref[h]
        k = k_ref[h]
        v = v_ref[h]
        p = p_ref[h]
        kq = jnp.where(mask, mm_nt(k, q), 0.0).astype(bf16)
        vg = jnp.where(mask, mm_nt(v, p), 0.0).astype(bf16)
        kg_ref[h] = (mm(vg, q) + mm_nt(v, later)).astype(bf16)
        vg_ref[h] = (mm(kq, p) + mm(k, later)).astype(bf16)


def keyval_part(qh, kh, vh, pre, wloc, order):
    return pl.pallas_call(
        keyval_kernel,
        grid=(NC,),
        in_specs=[HEAD] * 4 + [CHUNK, ORDER],
        out_specs=[HEAD] * 2,
        out_shape=[MAJOR] * 2,
        compiler_params=params(32),
        cost_estimate=cost(2 * T * HL * (4 * C * E + 2 * E * E), 22 * MIB),
        name="keyval_part",
    )(*far(qh, kh, vh, pre, wloc), order)


def final_kernel(
    k_hbm, v_hbm, kp_hbm, vp_hbm, l_ref, kg_hbm, vg_hbm, k_buf, v_buf, kp_buf, vp_buf, kg_buf, vg_buf, sems, out_sems
):
    copies = []
    for i in range(NB):
        at = pl.ds(i * B, B)
        for n, (src, dst) in enumerate(
            ((k_hbm, k_buf), (v_hbm, v_buf), (kp_hbm, kp_buf), (vp_hbm, vp_buf))
        ):
            copies.append(pltpu.make_async_copy(src.at[:, at], dst.at[:, at], sems.at[i, n]))
            copies[-1].start()
    low = lax.broadcasted_iota(jnp.int32, (HL, 8, E), 1) < 4
    later = []
    for h in range(0, HL, 2):
        even = l_ref[:, 0, 4 * h : 4 * h + 8, :]
        odd = l_ref[:, 1, 4 * h : 4 * h + 8, :]
        later.append(jnp.where(low, even, pltpu.roll(odd, 4, 1)).reshape(E, E).astype(bf16))
        later.append(jnp.where(low, pltpu.roll(even, 4, 1), odd).reshape(E, E).astype(bf16))
    outs = []
    for i in range(NB):
        for n in range(4):
            copies[4 * i + n].wait()
        at = slice(i * B, (i + 1) * B)
        kg = []
        vg = []
        for h in range(HL):
            kg.append((kp_buf[h, at].astype(f32) + mm_nt(v_buf[h, at], later[h])).astype(bf16))
            vg.append((vp_buf[h, at].astype(f32) + mm(k_buf[h, at], later[h])).astype(bf16))
        kg_buf[at] = jnp.swapaxes(jnp.stack(kg), 0, 1)
        vg_buf[at] = jnp.swapaxes(jnp.stack(vg), 0, 1)
        at = pl.ds(i * B, B)
        for n, (src, dst) in enumerate(((kg_buf, kg_hbm), (vg_buf, vg_hbm))):
            outs.append(pltpu.make_async_copy(src.at[at], dst.at[at], out_sems.at[i, n]))
            outs[-1].start()
    for copy in outs:
        copy.wait()


def final_part(kh, vh, kpart, vpart, later):
    return pl.pallas_call(
        final_kernel,
        in_specs=[ORDER] * 4 + [HERE],
        out_specs=[ORDER] * 2,
        out_shape=[TOKENS] * 2,
        scratch_shapes=[pltpu.VMEM((HL, T, E), bf16)] * 4
        + [pltpu.VMEM((T, HL, E), bf16)] * 2
        + [pltpu.SemaphoreType.DMA((NB, 4)), pltpu.SemaphoreType.DMA((NB, 2))],
        compiler_params=params(40),
        cost_estimate=cost(4 * T * HL * E * E, 19 * MIB),
        name="final_part",
    )(*far(kh, vh, kpart, vpart), *near(later))


def swap(pieces):
    return lax.all_to_all(pieces, "seq", 0, 0, tiled=True)


def body(queries, keys, values, out_grad, gain, entry_state):
    start = entry_state.reshape(N, 64, E)
    got = swap(kv_sums(keys, values).reshape(N, 64, E))
    qh, kh, vh, gh, part, loc, order = local_part(queries, keys, values, out_grad, start)
    state = swap(prefix(got, start, order)).reshape(HL, E, E)
    att, sums, state = stats(qh, gh, part, state, gain)
    sums = lax.all_to_all(sums, "head", 0, 0, tiled=True)
    pre, wloc, w = pre_part(qh, gh, att, gain, sums)
    back = swap(w.reshape(N, 64, E))
    normed, query_grad, order = query_part(qh, kh, vh, pre, part, state, loc, gain, sums)
    rest, total = suffix(back, order)
    later = swap(rest).reshape(16, 2, 64, E)
    kpart, vpart = keyval_part(qh, kh, vh, pre, wloc, total)
    key_grad, value_grad = final_part(kh, vh, kpart, vpart, later)
    return normed, query_grad, key_grad, value_grad, total.reshape(HL, 4, E)


def solution(mesh):
    tok = P("seq", "head", None)
    return jax.shard_map(
        body,
        mesh=mesh,
        in_specs=(tok, tok, tok, tok, P("head", None), P("head", None, None)),
        out_specs=(tok, tok, tok, tok, P("head", "seq", None)),
        check_vma=False,
    )
```

time: 163 us -> 131 us (0.80)
  local copies, waits for them, and re-layouts: 34.4 us -> 5.51 us
  Pallas kernels: 56.7 us -> 65 us
  waiting for transfers between devices: 16.9 us -> 9.14 us
  blocking collectives: 34.7 us -> 30.4 us
    unnamed x50 -> x18, local copies, waits for them, and re-layouts: 34.4 us -> 5.51 us
    psum x1 -> x0, blocking collectives: 8.56 us -> none  [body(): sums = lax.psum(stats(qh, gh, att, state, gain), 'head')]
    pallas_call x9, Pallas kernels: 56.7 us -> 65 us  [the longest x1 15 us: local_part(): pl.pallas_call(local_kernel, grid=(NC,), in_specs=[TOK] * 4 + [ORDER], ou...]
    all_to_all x0 -> x1, blocking collectives: none -> 8.05 us  [body(): sums = lax.all_to_all(sums, 'head', 0, 0, tiled=True)]
    all_to_all x3, waiting for transfers between devices: 16.9 us -> 9.14 us  [swap(): return lax.all_to_all(pieces, 'seq', 0, 0, tiled=True)]
    all_to_all x1, blocking collectives: 26.1 us -> 22.3 us  [swap(): return lax.all_to_all(pieces, 'seq', 0, 0, tiled=True)]
  transfers between devices with their start and end apart: 3 -> 3, of which waited for: 1 -> 3; matrix products, arithmetic and copies ran while one was open for 0% -> 0% of each run, Pallas kernels for 22% -> 31%
where the time goes in v2:
time: 131 us; the launch traced here: 130 us
  Pallas kernels  65 us (50%)
  blocking collectives  30.4 us (23%)
  starting transfers between devices  19 us (15%)
  waiting for transfers between devices  9.14 us (7%)
  local copies, waits for them, and re-layouts  5.51 us (4%)
    all_to_all x1, blocking collectives, swap(): return lax.all_to_all(pieces, 'seq', 0, 0, tiled=True)  22.3 us
    all_to_all x3, starting transfers between devices, swap(): return lax.all_to_all(pieces, 'seq', 0, 0, tiled=True)  19 us
    pallas_call x1, Pallas kernels, local_part(): pl.pallas_call(local_kernel, grid=(NC,), in_specs=[TOK] * 4 + [ORDER], ou...  15 us
    pallas_call x1, Pallas kernels, keyval_part(): pl.pallas_call(keyval_kernel, grid=(NC,), in_specs=[HEAD] * 4 + [CHUNK, O...  13.4 us
    pallas_call x1, Pallas kernels, query_part(): pl.pallas_call(query_kernel, grid=(NC,), in_specs=[HEAD] * 5 + [pl.BlockS...  12.5 us
    all_to_all x3, waiting for transfers between devices, swap(): return lax.all_to_all(pieces, 'seq', 0, 0, tiled=True)  9.14 us
    all_to_all x1, blocking collectives, body(): sums = lax.all_to_all(sums, 'head', 0, 0, tiled=True)  8.05 us
    pallas_call x1, Pallas kernels, final_part(): pl.pallas_call(final_kernel, in_specs=[ORDER] * 4 + [HERE], out_specs=[OR...  7.96 us
  transfers between devices with their start and end apart: 3, of which 3 were waited for; matrix products, arithmetic and copies ran while one was open for 0% of the time, Pallas kernels for 31%

profile of v2, /device:TPU:1, one launch (start us, length us, event | category | flops | bytes accessed | tf_op | source)
XLA Modules:
  0.0 129.9 jit_solution(2925427148298923548)
XLA Ops:
  0.6 0.0 copy-start.4
  0.6 5.7 %kv_sums.1 = f32[16,128,128]{2,1,0:T(8,128)} custom-call(bf16[768,16,128]{2,1,0:T(8,128)(2,1)} %k_hbm.1, bf16[768,16,128]{2,1,0:T(8,128)(2,1)} %v_hbm.1), custom_call_target="tpu_custom_call" | custom-call | flops 402653184 | bytes 7340032 | tf_op jit(solution)/shard_map/kv_sums/pallas_call | solution.py:96
  6.4 9.7 %all-to-all-start = ((f32[32,64,128]{2,1,0:T(8,128)}), f32[32,64,128]{2,1,0:T(8,128)}, u32[]{:S(2)}, u32[]{:S(2)}) async-start(f32[32,64,128]{2,1,0:T(8,128)} %bitcast.1), calls=%async_computation | async-start | bytes 2097152 | tf_op jit(solution)/shard_map/all_to_all | solution.py:413
  16.1 0.0 copy-done.4
  16.1 15.0 %local_part.1 = (bf16[16,768,128]{2,1,0:T(8,128)(2,1)}, bf16[16,768,128]{2,1,0:T(8,128)(2,1)}, bf16[16,768,128]{2,1,0:T(8,128)(2,1)}, bf16[16,768,128]{2,1,0:T(8...) custom-call(bf16[768,16,128]{2,1,0:T(8,128)(2,1)} %q_ref.1, ...), custom_call_target="tpu_custom_call" | custom-call | flops 2415919104 | bytes 31457280 | tf_op jit(solution)/shard_map/local_part/pallas_call | solution.py:183
  31.1 0.0 copy-start
  31.1 0.0 copy-start.7
  31.1 1.9 %all-to-all-done.r_ref = f32[32,64,128]{2,1,0:T(8,128)} async-done(((f32[32,64,128]{2,1,0:T(8,128)}), f32[32,64,128]{2,1,0:T(8,128)}, u32[]{:S(2)}, u32[]{:S(2)}) %all-to-all-start) | async-done | bytes 1048608 | tf_op jit(solution)/shard_map/all_to_all | solution.py:413
  33.0 2.1 %prefix.1 = f32[32,64,128]{2,1,0:T(8,128)S(1)} custom-call(f32[32,64,128]{2,1,0:T(8,128)} %all-to-all-done.r_ref, f32[32,64,128]{2,1,0:T(8,128)} %bitcast.7, f32[8,128]{1,0:T(8,128)S(1)} %get-tuple-element.32._), custom_call_target="tpu_custom_call" | custom-call | flops 262144 | bytes 2097152 | tf_op jit(solution)/shard_map/prefix/pallas_call | solution.py:123
  35.1 22.3 %all_to_all.25 = f32[32,64,128]{2,1,0:T(8,128)S(1)} all-to-all(f32[32,64,128]{2,1,0:T(8,128)S(1)} %prefix.1), channel_id=1, replica_groups=mesh['seq'=32,'head'=4] {'seq'}, dimensions={0} | all-to-all | bytes 2097152 | tf_op jit(solution)/shard_map/all_to_all | solution.py:413
  57.4 0.0 copy-done
  57.4 0.0 copy-done.7
  57.4 0.0 copy-start.1
  57.4 1.9 %copy-done.1 = bf16[16,768,128]{2,1,0:T(8,128)(2,1)S(1)} copy-done((bf16[16,768,128]{2,1,0:T(8,128)(2,1)S(1)}, bf16[16,768,128]{2,1,0:T(8,128)(2,1)}, u32[]{:S(2)}) %copy-start.1) | copy-done | bytes 3145752
  59.3 0.0 copy-start.3
  59.3 1.9 %copy-done.3 = bf16[16,768,128]{2,1,0:T(8,128)(2,1)S(1)} copy-done((bf16[16,768,128]{2,1,0:T(8,128)(2,1)S(1)}, bf16[16,768,128]{2,1,0:T(8,128)(2,1)}, u32[]{:S(2)}) %copy-start.3) | copy-done | bytes 3145752
  61.2 3.3 %stats.1 = (f32[16,768,128]{2,1,0:T(8,128)S(1)}, f32[4,2,768]{2,1,0:T(2,128)S(1)}, bf16[16,128,128]{2,1,0:T(8,128)(2,1)}) custom-call(bf16[16,768,128]{2,1,0:T(8,128)(2,1)S(1)} %copy-done, bf16[16,768,128]{2,1,0:T(8,128)(2,1)S(1)} %copy-done.1, bf16[16,768,128]{2,1,0:T(8,128)(2,1)S(1)} %copy-done.3, f32[16,128,128]{2,1,0:T(8,128)S(1)} %bitcast.6, ...), custom_call_target="tpu_custom_call" | custom-call | flops 402653184 | bytes 10485760 | tf_op jit(solution)/shard_map/stats/pallas_call | solution.py:220
  64.5 8.1 %all_to_all.26.sums_ref = f32[4,2,768]{2,1,0:T(2,128)S(1)} all-to-all(f32[4,2,768]{2,1,0:T(2,128)S(1)} %get-tuple-element.34), channel_id=1, replica_groups=mesh['seq'=32,'head'=4] {'head'}, dimensions={0} | all-to-all | bytes 49152 | tf_op jit(solution)/shard_map/all_to_all | solution.py:422
  72.6 0.0 copy-done.2
  72.6 4.0 %pre_part.1 = (bf16[16,768,128]{2,1,0:T(8,128)(2,1)}, bf16[3,16,128,128]{3,2,1,0:T(8,128)(2,1)}, f32[16,2,64,128]{3,2,1,0:T(8,128)S(1)}) custom-call(bf16[16,768,128]{2,1,0:T(8,128)(2,1)S(1)} %copy-done, bf16[16,768,128]{2,1,0:T(8,128)(2,1)S(1)} %copy-done.2, f32[16,768,128]{2,1,0:T(8,128)S(1)} %get-tuple-element.33.a_ref, f32[16,128]{1,0:T(8,128)S(1)} %copy-done.7, ...), custom_call_target="tpu_custom_call" | custom-call | flops 805306368 | bytes 16777216 | tf_op jit(solution)/shard_map/pre_part/pallas_call | solution.py:277
  76.6 0.0 copy-done.6
  76.6 1.0 copy-done.5
  77.6 5.4 %all-to-all-start.3 = ((f32[32,64,128]{2,1,0:T(8,128)}), f32[32,64,128]{2,1,0:T(8,128)S(1)}, u32[]{:S(2)}, u32[]{:S(2)}) async-start(f32[32,64,128]{2,1,0:T(8,128)} %bitcast.10), calls=%async_computation.3 | async-start | bytes 2097152 | tf_op jit(solution)/shard_map/all_to_all | solution.py:413
  83.0 12.5 %query_part.1 = (bf16[768,16,128]{2,1,0:T(8,128)(2,1)}, bf16[768,16,128]{2,1,0:T(8,128)(2,1)}, f32[8,128]{1,0:T(8,128)S(1)}) custom-call(bf16[16,768,128]{2,1,0:T(8,128)(2,1)} %get-tuple-element.27.q_ref, bf16[16,768,128]{2,1,0:T(8,128)(2,1)} %get-tuple-element.28.k_ref.k_hbm, bf16[16,768,128]{2,1,0:T(8,128)(2,1)} %get-tuple-element.29.v_ref.v_hbm, ...), custom_call_target="tpu_custom_call" | custom-call | flops 2818572288 | bytes 31457280 | tf_op jit(solution)/shard_map/query_part/pallas_call | solution.py:314
  95.4 4.5 %all-to-all-done.3.r_ref = f32[32,64,128]{2,1,0:T(8,128)S(1)} async-done(((f32[32,64,128]{2,1,0:T(8,128)}), f32[32,64,128]{2,1,0:T(8,128)S(1)}, u32[]{:S(2)}, u32[]{:S(2)}) %all-to-all-start.3) | async-done | bytes 1048608 | tf_op jit(solution)/shard_map/all_to_all | solution.py:413
  99.9 1.0 suffix.1
  100.9 4.0 %all-to-all-start.4 = ((f32[32,64,128]{2,1,0:T(8,128)}), f32[32,64,128]{2,1,0:T(8,128)S(1)}, u32[]{:S(2)}, u32[]{:S(2)}) async-start(f32[32,64,128]{2,1,0:T(8,128)} %get-tuple-element.46), calls=%async_computation.4 | async-start | bytes 2097152 | tf_op jit(solution)/shard_map/all_to_all | solution.py:413
  104.9 0.0 copy-start.8
  104.9 0.7 copy-done.8
  105.6 13.4 %keyval_part.1 = (bf16[16,768,128]{2,1,0:T(8,128)(2,1)}, bf16[16,768,128]{2,1,0:T(8,128)(2,1)}) custom-call(bf16[16,768,128]{2,1,0:T(8,128)(2,1)} %get-tuple-element.27.q_ref, bf16[16,768,128]{2,1,0:T(8,128)(2,1)} %get-tuple-element.28.k_ref.k_hbm, bf16[16,768,128]{2,1,0:T(8,128)(2,1)} %get-tuple-element.29.v_ref.v_hbm, ...), custom_call_target="tpu_custom_call" | custom-call | flops 4026531840 | bytes 23068672 | tf_op jit(solution)/shard_map/keyval_part/pallas_call | solution.py:347
  119.0 2.8 %all-to-all-done.4 = f32[32,64,128]{2,1,0:T(8,128)S(1)} async-done(((f32[32,64,128]{2,1,0:T(8,128)}), f32[32,64,128]{2,1,0:T(8,128)S(1)}, u32[]{:S(2)}, u32[]{:S(2)}) %all-to-all-start.4) | async-done | bytes 1048608 | tf_op jit(solution)/shard_map/all_to_all | solution.py:413
  121.8 8.0 %final_part.1 = (bf16[768,16,128]{2,1,0:T(8,128)(2,1)}, bf16[768,16,128]{2,1,0:T(8,128)(2,1)}) custom-call(bf16[16,768,128]{2,1,0:T(8,128)(2,1)} %get-tuple-element.28.k_ref.k_hbm, bf16[16,768,128]{2,1,0:T(8,128)(2,1)} %get-tuple-element.29.v_ref.v_hbm, bf16[16,768,128]{2,1,0:T(8,128)(2,1)} %get-tuple-element.44.kp_hbm, ...), custom_call_target="tpu_custom_call" | custom-call | flops 805306368 | bytes 19922944 | tf_op jit(solution)/shard_map/final_part/pallas_call | solution.py:398
  (3 shorter events, 0.0 us)
Async XLA Ops:
  0.6 15.4 %copy-start.4 = (f32[16,128,128]{2,1,0:T(8,128)S(1)}, f32[16,128,128]{2,1,0:T(8,128)}, u32[]{:S(2)}) copy-start(f32[16,128,128]{2,1,0:T(8,128)} %param.11) | copy-start | bytes 3145732
  6.4 26.6 %all-to-all-start = ((f32[32,64,128]{2,1,0:T(8,128)}), f32[32,64,128]{2,1,0:T(8,128)}, u32[]{:S(2)}, u32[]{:S(2)}) async-start(f32[32,64,128]{2,1,0:T(8,128)} %bitcast.1), calls=%async_computation | async-start | bytes 2097152 | tf_op jit(solution)/shard_map/all_to_all | solution.py:413
  31.1 26.3 %copy-start = (bf16[16,768,128]{2,1,0:T(8,128)(2,1)S(1)}, bf16[16,768,128]{2,1,0:T(8,128)(2,1)}, u32[]{:S(2)}) copy-start(bf16[16,768,128]{2,1,0:T(8,128)(2,1)} %get-tuple-element.27.q_ref) | copy-start | bytes 9437188
  31.1 26.3 %copy-start.7 = (f32[16,128]{1,0:T(8,128)S(1)}, f32[16,128]{1,0:T(8,128)}, u32[]{:S(2)}) copy-start(f32[16,128]{1,0:T(8,128)} %gain_ref.5) | copy-start | bytes 24580
  57.4 1.9 %copy-start.1 = (bf16[16,768,128]{2,1,0:T(8,128)(2,1)S(1)}, bf16[16,768,128]{2,1,0:T(8,128)(2,1)}, u32[]{:S(2)}) copy-start(bf16[16,768,128]{2,1,0:T(8,128)(2,1)} %get-tuple-element.30.g_ref) | copy-start | bytes 9437188
  59.3 1.9 %copy-start.3 = (bf16[16,768,128]{2,1,0:T(8,128)(2,1)S(1)}, bf16[16,768,128]{2,1,0:T(8,128)(2,1)}, u32[]{:S(2)}) copy-start(bf16[16,768,128]{2,1,0:T(8,128)(2,1)} %get-tuple-element.31.a_ref) | copy-start | bytes 9437188
  61.2 11.4 %copy-start.2 = (bf16[16,768,128]{2,1,0:T(8,128)(2,1)S(1)}, bf16[16,768,128]{2,1,0:T(8,128)(2,1)}, u32[]{:S(2)}) copy-start(bf16[16,768,128]{2,1,0:T(8,128)(2,1)} %get-tuple-element.30.g_ref) | copy-start | bytes 9437188
  72.6 4.0 %copy-start.6 = (f32[4,2,768]{2,1,0:T(2,128)}, f32[4,2,768]{2,1,0:T(2,128)S(1)}, u32[]{:S(2)}) copy-start(f32[4,2,768]{2,1,0:T(2,128)S(1)} %all_to_all.26.sums_ref) | copy-start | bytes 73732
  76.6 1.0 copy-start.5
  77.6 22.3 %all-to-all-start.3 = ((f32[32,64,128]{2,1,0:T(8,128)}), f32[32,64,128]{2,1,0:T(8,128)S(1)}, u32[]{:S(2)}, u32[]{:S(2)}) async-start(f32[32,64,128]{2,1,0:T(8,128)} %bitcast.10), calls=%async_computation.3 | async-start | bytes 2097152 | tf_op jit(solution)/shard_map/all_to_all | solution.py:413
  100.9 20.9 %all-to-all-start.4 = ((f32[32,64,128]{2,1,0:T(8,128)}), f32[32,64,128]{2,1,0:T(8,128)S(1)}, u32[]{:S(2)}, u32[]{:S(2)}) async-start(f32[32,64,128]{2,1,0:T(8,128)} %get-tuple-element.46), calls=%async_computation.4 | async-start | bytes 2097152 | tf_op jit(solution)/shard_map/all_to_all | solution.py:413
  104.9 0.8 copy-start.8

commit v3 on v2

v3 whole, which is shorter than its diff:
```python
import functools

import jax
import jax.numpy as jnp
from jax import lax
from jax.experimental import pallas as pl
from jax.experimental.pallas import tpu as pltpu
from jax.sharding import PartitionSpec as P

H = 64
E = 128
T = 768
HL = 16
C = 256
NC = T // C
B = 128
N = 32
L = 4
HALF = HL // 2
X = 4
WIDTH = H * E
epsilon = 1e-06
f32 = jnp.float32
bf16 = jnp.bfloat16
MIB = 1 << 20


def mm(a, b):
    return lax.dot_general(a, b, (((1,), (0,)), ((), ())), preferred_element_type=f32)


def mm_nt(a, b):
    return lax.dot_general(a, b, (((1,), (1,)), ((), ())), preferred_element_type=f32)


def mm_tn(a, b):
    return lax.dot_general(a, b, (((0,), (0,)), ((), ())), preferred_element_type=f32)


def causal(later=False):
    row = lax.broadcasted_iota(jnp.int32, (C, C), 0)
    col = lax.broadcasted_iota(jnp.int32, (C, C), 1)
    return row <= col if later else col <= row


def heads_first(ref):
    return jnp.swapaxes(ref[...], 0, 1)


def params(vmem=24):
    return pltpu.CompilerParams(vmem_limit_bytes=vmem * MIB)


def cost(flops, moved):
    return pl.CostEstimate(flops=flops, bytes_accessed=moved, transcendentals=0)


HERE = pl.BlockSpec(memory_space=pltpu.VMEM)
ORDER = pl.BlockSpec(memory_space=pl.ANY)
TOK = pl.BlockSpec((C, HL, E), lambda i: (i, 0, 0))
MAJOR = pltpu.VMEM((HL, T, E), bf16)
SQUARES = pltpu.VMEM((HL, T, C), bf16)
STATES = pltpu.VMEM((NC, HL, E, E), bf16)
TOKENS = pltpu.HBM((T, HL, E), bf16)
QUARTER = pltpu.VMEM((HALF * E // L, E), f32)
QUARTERS = pltpu.VMEM((L, HALF * E // L, E), f32)
MARK = pltpu.HBM((8, E), f32)
MARKER = pl.BlockSpec((8, E), lambda i: (0, 0))


def my_place():
    me = lax.axis_index("seq")
    return me // (2 * L), lax.rem(me // 2, L), lax.rem(me, 2)


def far(*arrays):
    return tuple(pltpu.with_memory_space_constraint(a, pltpu.HBM) for a in arrays)


def near(*arrays):
    return tuple(pltpu.with_memory_space_constraint(a, pltpu.VMEM) for a in arrays)


def rows(step):
    return pl.ds(pl.multiple_of(step * C, C), C)


def mm_lower(a, b):
    return jnp.concatenate([mm(a[:B, :B], b[:B]), mm(a[B:], b)], axis=0)


def mm_upper(a, b):
    return jnp.concatenate([mm(a[:B], b), mm(a[B:, B:], b[B:])], axis=0)


def kv_kernel(k_hbm, v_hbm, o_ref, k_buf, v_buf, sems):
    _, _, core = my_place()
    copies = []
    for i in range(NC):
        at = pl.ds(i * C, C)
        for n, (src, dst) in enumerate(((k_hbm, k_buf), (v_hbm, v_buf))):
            copies.append(pltpu.make_async_copy(src.at[at], dst.at[at], sems.at[i, n]))
            copies[-1].start()
    for i in range(NC):
        copies[2 * i].wait()
        copies[2 * i + 1].wait()
        k = jnp.swapaxes(k_buf[i * C : (i + 1) * C], 0, 1)
        v = jnp.swapaxes(v_buf[i * C : (i + 1) * C], 0, 1)
        for h in range(HL):
            part = mm_tn(k[h], v[h])
            half = lax.rem(h // HALF + core, 2)
            o_ref[half, h % HALF] = part if i == 0 else o_ref[half, h % HALF] + part


def kv_sums(keys, values):
    return pl.pallas_call(
        kv_kernel,
        in_specs=[ORDER, ORDER],
        out_specs=HERE,
        out_shape=pltpu.VMEM((2, HALF, E, E), f32),
        scratch_shapes=[
            pltpu.VMEM((T, HL, E), bf16),
            pltpu.VMEM((T, HL, E), bf16),
            pltpu.SemaphoreType.DMA((NC, 2)),
        ],
        compiler_params=params(24),
        cost_estimate=cost(2 * T * HL * E * E, 7 * MIB),
        name="kv_sums",
    )(*far(keys, values))


def pair_kernel(first, m_ref, r_ref, *outs):
    _, z, core = my_place()
    for k in range(L):
        at = lax.rem(z + k, L)
        outs[k][...] = m_ref[at] + r_ref[at]
    outs[L][...] = jnp.where(core == first, m_ref[...], r_ref[...])


def pair(mine, got, first):
    return pl.pallas_call(
        functools.partial(pair_kernel, first),
        in_specs=[HERE] * 2,
        out_specs=[HERE] * (L + 1),
        out_shape=[QUARTER] * L + [QUARTERS],
        compiler_params=params(2),
        cost_estimate=cost(HALF * E * E, 2 * MIB),
        name="pair",
    )(*near(mine, got))


def row_kernel(backward, *refs):
    parts, (_, e_ref, t_ref, buf) = refs[:L], refs[L:]
    _, z, _ = my_place()
    for k in range(L):
        buf[lax.rem(z + L - k, L)] = parts[k][...]
    total = jnp.zeros_like(t_ref)
    for i in reversed(range(L)) if backward else range(L):
        e_ref[i] = total
        total = total + buf[i]
    t_ref[...] = total


def row_sums(parts, order, backward):
    return pl.pallas_call(
        functools.partial(row_kernel, backward),
        in_specs=[HERE] * L + [ORDER],
        out_specs=[HERE] * 2,
        out_shape=[QUARTERS, QUARTER],
        scratch_shapes=[QUARTERS],
        compiler_params=params(2),
        cost_estimate=cost(HALF * E * E, MIB),
        name="row_sums",
    )(*near(*parts), *far(order))


def prior_kernel(e_ref, u1, u2, u3, x_hbm, _, *refs):
    outs, (x_ref, sem) = refs[:L], refs[L:]
    y, z, core = my_place()
    first = pltpu.make_async_copy(x_hbm.at[core * L + z], x_ref, sem)
    first.start()
    first.wait()
    total = x_ref[...]
    for k, u in enumerate((u1, u2, u3)):
        total = total + jnp.where(k + 1 <= y, u[...], 0.0)
    for k in range(L):
        outs[k][...] = total + e_ref[lax.rem(z + k, L)]


def prior_sums(inrow, others, start, order):
    return pl.pallas_call(
        prior_kernel,
        in_specs=[HERE] * L + [ORDER] * 2,
        out_specs=[HERE] * L,
        out_shape=[QUARTER] * L,
        scratch_shapes=[QUARTER, pltpu.SemaphoreType.DMA],
        compiler_params=params(2),
        cost_estimate=cost(HALF * E * E, MIB),
        name="prior_sums",
    )(*near(inrow, *others), *far(start, order))


def later_kernel(e_ref, t_ref, u1, u2, u3, _, *refs):
    outs, (sum_ref, buf) = refs[:L], refs[L:]
    y, z, _ = my_place()
    total = jnp.zeros_like(t_ref)
    for k, u in enumerate((u1, u2, u3)):
        total = total + jnp.where(k + 1 > y, u[...], 0.0)
    for k in range(L):
        outs[k][...] = total + e_ref[lax.rem(z + k, L)]
    buf[...] = (t_ref[...] + u1[...] + u2[...] + u3[...]).reshape(buf.shape)
    sum_ref[...] = buf[y]


def later_sums(inrow, total, others, order):
    return pl.pallas_call(
        later_kernel,
        in_specs=[HERE] * (L + 1) + [ORDER],
        out_specs=[HERE] * (L + 1),
        out_shape=[QUARTER] * L + [jax.ShapeDtypeStruct((HL * L, E), f32)],
        scratch_shapes=[pltpu.VMEM((L, HL * L, E), f32)],
        compiler_params=params(2),
        cost_estimate=cost(HALF * E * E, MIB),
        name="later_sums",
    )(*near(inrow, total, *others), *far(order))


def split_kernel(first, *refs):
    parts, (x_ref, _, own_ref, send_ref) = refs[:L], refs[L:]
    _, z, core = my_place()
    for k in range(L):
        at = lax.rem(z + L - k, L)
        scan = parts[k][...]
        more = scan + x_ref[at]
        own_ref[at] = jnp.where(core == first, scan, more)
        send_ref[at] = jnp.where(core == first, more, scan)


def split(parts, extra, order, first):
    return pl.pallas_call(
        functools.partial(split_kernel, first),
        in_specs=[HERE] * (L + 1) + [ORDER],
        out_specs=[HERE] * 2,
        out_shape=[QUARTERS] * 2,
        compiler_params=params(2),
        cost_estimate=cost(HALF * E * E, 2 * MIB),
        name="split",
    )(*near(*parts, extra), *far(order))


def local_kernel(
    q_ref, k_ref, v_ref, _, qh_ref, kh_ref, vh_ref, att_ref, loc_ref, mark_ref, acc, qk_ref
):
    step = pl.program_id(0)
    at = rows(step)

    @pl.when(step == 0)
    def _():
        acc[...] = jnp.zeros_like(acc)
        mark_ref[...] = jnp.zeros_like(mark_ref)

    mask = causal()
    q = heads_first(q_ref)
    k = heads_first(k_ref)
    v = heads_first(v_ref)
    qh_ref[:, at] = q
    kh_ref[:, at] = k
    vh_ref[:, at] = v
    for h in range(HL):
        qk_ref[h] = jnp.where(mask, mm_nt(q[h], k[h]), 0.0).astype(bf16)
    for h in range(HL):
        loc = acc[h].astype(bf16)
        loc_ref[step, h] = loc
        att_ref[h, at] = (mm_lower(qk_ref[h], v[h]) + mm(q[h], loc)).astype(bf16)
        acc[h] += mm_tn(k[h], v[h])


def local_part(queries, keys, values, order):
    return pl.pallas_call(
        local_kernel,
        grid=(NC,),
        in_specs=[TOK] * 3 + [ORDER],
        out_specs=[HERE] * 5 + [MARKER],
        out_shape=[MAJOR] * 4 + [STATES, MARK],
        scratch_shapes=[pltpu.VMEM((HL, E, E), f32), pltpu.VMEM((HL, C, C), bf16)],
        compiler_params=params(18),
        cost_estimate=cost(2 * T * HL * (2 * C * E + 2 * E * E), 24 * MIB),
        name="local_part",
    )(*far(queries, keys, values, order))


def square_kernel(g_ref, q_ref, k_ref, _, gh_ref, kq_ref, mark_ref):
    at = rows(pl.program_id(0))
    mask = causal(later=True)
    mark_ref[...] = jnp.zeros_like(mark_ref)
    gh_ref[:, at] = heads_first(g_ref)
    for h in range(HL):
        kq_ref[h, at] = jnp.where(mask, mm_nt(k_ref[h, at], q_ref[h, at]), 0.0).astype(bf16)


def square_part(out_grad, qh, kh, order):
    return pl.pallas_call(
        square_kernel,
        grid=(NC,),
        in_specs=[TOK, HERE, HERE, ORDER],
        out_specs=[HERE, HERE, MARKER],
        out_shape=[MAJOR, SQUARES, MARK],
        compiler_params=params(12),
        cost_estimate=cost(2 * T * HL * C * E, 19 * MIB),
        name="square_part",
    )(*far(out_grad), *near(qh, kh), *far(order))


def stats_kernel(q_ref, g_ref, a_ref, own_ref, got_ref, gain_ref, att_ref, o_ref, sb_ref):
    step = pl.program_id(0)
    at = rows(step)

    @pl.when(step == 0)
    def _():
        _, _, core = my_place()
        sb_ref[pl.ds(core * HALF, HALF)] = own_ref[...].astype(bf16)
        sb_ref[pl.ds((1 - core) * HALF, HALF)] = got_ref[...].astype(bf16)

    sq = jnp.zeros((C, E), f32)
    pr = jnp.zeros((C, E), f32)
    for h in range(HL):
        att = a_ref[h, at].astype(f32) + mm(q_ref[h, at], sb_ref[h])
        att_ref[h, at] = att
        up = gain_ref[h : h + 1, :] * g_ref[h, at].astype(f32)
        sq = sq + att * att
        pr = pr + up * att
    sq = jnp.sum(sq.T, axis=0, keepdims=True)
    pr = jnp.sum(pr.T, axis=0, keepdims=True)
    for x in range(X):
        o_ref[x, step, 0:1, :] = sq
        o_ref[x, step, 1:2, :] = pr


def stats(qh, gh, part, own, got, gain):
    return pl.pallas_call(
        stats_kernel,
        grid=(NC,),
        in_specs=[HERE] * 6,
        out_specs=[HERE] * 3,
        out_shape=[
            pltpu.VMEM((HL, T, E), f32),
            pltpu.VMEM((X, NC, 2, C), f32),
            pltpu.VMEM((HL, E, E), bf16),
        ],
        compiler_params=params(8),
        cost_estimate=cost(2 * T * HL * E * E, 10 * MIB),
        name="stats",
    )(*near(qh, gh, part, own, got, gain))


def scales(sums_ref, step):
    sums = (sums_ref[0, step] + sums_ref[1, step]) + (sums_ref[2, step] + sums_ref[3, step])
    rms = jnp.sqrt(sums[0:1, :] / WIDTH + epsilon)
    a = 1.0 / rms
    b = sums[1:2, :] / (WIDTH * rms * rms) * a
    a = jnp.broadcast_to(a, (E, C)).T
    b = jnp.broadcast_to(b, (E, C)).T
    return a, b


def pre_kernel(q_ref, g_ref, a_ref, gain_ref, sums_ref, p_ref, wl_ref, w_ref, other_ref, acc):
    step = pl.program_id(0)
    chunk = NC - 1 - step
    at = rows(chunk)

    @pl.when(step == 0)
    def _():
        acc[...] = jnp.zeros_like(acc)

    a, b = scales(sums_ref, chunk)
    for h in range(HL):
        up = gain_ref[h : h + 1, :] * g_ref[h, at].astype(f32)
        p = (up * a - a_ref[h, at] * b).astype(bf16)
        p_ref[h, at] = p
        wl_ref[chunk, h] = acc[h].astype(bf16)
        acc[h] += mm_tn(q_ref[h, at], p)

    @pl.when(step == NC - 1)
    def _():
        low = lax.broadcasted_iota(jnp.int32, (HL, 8, E), 1) < 4
        _, _, core = my_place()
        for h in range(0, HL, 2):
            x = acc[h].reshape(HL, 8, E)
            y = acc[h + 1].reshape(HL, 8, E)
            even = jnp.where(low, x, pltpu.roll(y, 4, 1))
            odd = jnp.where(low, pltpu.roll(x, 4, 1), y)
            mine = jnp.where(core == 0, even, odd)
            other = jnp.where(core == 0, odd, even)
            for p in range(L * L):
                at = slice(64 * (p // L) + 4 * h, 64 * (p // L) + 4 * h + 8)
                w_ref[p % L, at, :] = mine[p]
                other_ref[p % L, at, :] = other[p]


def pre_part(qh, gh, att, gain, sums):
    return pl.pallas_call(
        pre_kernel,
        grid=(NC,),
        in_specs=[HERE] * 5,
        out_specs=[HERE] * 4,
        out_shape=[MAJOR, STATES, QUARTERS, QUARTERS],
        scratch_shapes=[pltpu.VMEM((HL, E, E), f32)],
        compiler_params=params(8),
        cost_estimate=cost(4 * T * HL * E * E, 16 * MIB),
        name="pre_part",
    )(*near(qh, gh, att, gain, sums))


def query_kernel(
    k_ref, v_ref, p_ref, a_ref, s_ref, loc_ref, gain_ref, sums_ref, _, n_ref, qg_ref, mark_ref, gv_ref
):
    step = pl.program_id(0)
    at = rows(step)
    mask = causal()
    mark_ref[...] = jnp.zeros_like(mark_ref)
    a, _ = scales(sums_ref, step)
    for h in range(HL):
        gv_ref[h] = jnp.where(mask, mm_nt(p_ref[h, at], v_ref[h, at]), 0.0).astype(bf16)
    normed = [(gain_ref[h : h + 1, :] * a_ref[h, at] * a).astype(bf16) for h in range(HL)]
    n_ref[...] = jnp.swapaxes(jnp.stack(normed), 0, 1)
    grads = []
    for h in range(HL):
        p = p_ref[h, at]
        both = mm_nt(
            jnp.concatenate([p, p], axis=1),
            jnp.concatenate([s_ref[h], loc_ref[step, h]], axis=1),
        )
        grads.append((both + mm_lower(gv_ref[h], k_ref[h, at])).astype(bf16))
    qg_ref[...] = jnp.swapaxes(jnp.stack(grads), 0, 1)


def query_part(kh, vh, pre, att, state, loc, gain, sums, order):
    return pl.pallas_call(
        query_kernel,
        grid=(NC,),
        in_specs=[HERE] * 8 + [ORDER],
        out_specs=[TOK] * 2 + [MARKER],
        out_shape=[TOKENS] * 2 + [MARK],
        scratch_shapes=[pltpu.VMEM((HL, C, C), bf16)],
        compiler_params=params(18),
        cost_estimate=cost(2 * T * HL * (2 * C * E + 3 * E * E), 30 * MIB),
        name="query_part",
    )(*near(kh, vh, pre, att, state, loc, gain, sums), *far(order))


def keyval_kernel(q_ref, k_ref, v_ref, p_ref, kq_ref, wl_ref, _, kg_ref, vg_ref, mark_ref, vp_ref):
    step = pl.program_id(0)
    at = rows(step)
    mask = causal(later=True)
    mark_ref[...] = jnp.zeros_like(mark_ref)
    for h in range(HL):
        vp_ref[h] = jnp.where(mask, mm_nt(v_ref[h, at], p_ref[h, at]), 0.0).astype(bf16)
    for h in range(HL):
        later = wl_ref[step, h]
        kg_ref[h, at] = (mm_upper(vp_ref[h], q_ref[h, at]) + mm_nt(v_ref[h, at], later)).astype(bf16)
        vg_ref[h, at] = (mm_upper(kq_ref[h, at], p_ref[h, at]) + mm(k_ref[h, at], later)).astype(bf16)


def keyval_part(qh, kh, vh, pre, kq, wloc, order):
    return pl.pallas_call(
        keyval_kernel,
        grid=(NC,),
        in_specs=[HERE] * 6 + [ORDER],
        out_specs=[HERE] * 2 + [MARKER],
        out_shape=[MAJOR] * 2 + [MARK],
        scratch_shapes=[pltpu.VMEM((HL, C, C), bf16)],
        compiler_params=params(12),
        cost_estimate=cost(2 * T * HL * (3 * C * E + 2 * E * E), 28 * MIB),
        name="keyval_part",
    )(*near(qh, kh, vh, pre, kq, wloc), *far(order))


def final_kernel(k_ref, v_ref, kp_ref, vp_ref, own_ref, got_ref, kg_ref, vg_ref, l_ref):
    step = pl.program_id(0)
    at = rows(step)

    @pl.when(step == 0)
    def _():
        low = lax.broadcasted_iota(jnp.int32, (HL, 8, E), 1) < 4
        _, _, core = my_place()

        def in_order(ref, h):
            parts = []
            for p in range(L * L):
                first = 64 * (p // L) + 4 * h
                parts.append(ref[p % L, first : first + 8, :])
            return jnp.stack(parts)

        for h in range(0, HL, 2):
            own = in_order(own_ref, h)
            got = in_order(got_ref, h)
            even = jnp.where(core == 0, own, got)
            odd = jnp.where(core == 0, got, own)
            l_ref[h] = jnp.where(low, even, pltpu.roll(odd, 4, 1)).reshape(E, E).astype(bf16)
            l_ref[h + 1] = jnp.where(low, pltpu.roll(even, 4, 1), odd).reshape(E, E).astype(bf16)

    kg = []
    for h in range(HL):
        kg.append((kp_ref[h, at].astype(f32) + mm_nt(v_ref[h, at], l_ref[h])).astype(bf16))
    kg_ref[...] = jnp.swapaxes(jnp.stack(kg), 0, 1)
    vg = []
    for h in range(HL):
        vg.append((vp_ref[h, at].astype(f32) + mm(k_ref[h, at], l_ref[h])).astype(bf16))
    vg_ref[...] = jnp.swapaxes(jnp.stack(vg), 0, 1)


def final_part(kh, vh, kpart, vpart, own, got):
    return pl.pallas_call(
        final_kernel,
        grid=(NC,),
        in_specs=[HERE] * 6,
        out_specs=[TOK] * 2,
        out_shape=[TOKENS] * 2,
        scratch_shapes=[pltpu.VMEM((HL, E, E), bf16)],
        compiler_params=params(14),
        cost_estimate=cost(4 * T * HL * E * E, 19 * MIB),
        name="final_part",
    )(*near(kh, vh, kpart, vpart, own, got))


def along(x, move):
    def seq(y, z, core):
        return (y * L + z) * 2 + core

    places = [(y, z, core) for y in range(L) for z in range(L) for core in range(2)]
    return lax.ppermute(x, "seq", [(seq(*p), seq(*move(*p))) for p in places])


def across_cores(x):
    return along(x, lambda y, z, core: (y, z, 1 - core))


def across_z(parts):
    sent = [along(parts[k], lambda y, z, core: (y, (z + k) % L, core)) for k in range(1, L)]
    return [parts[0]] + sent


def across_y(x):
    return [along(x, lambda y, z, core: ((y + k) % L, z, core)) for k in range(1, L)]


def body(queries, keys, values, out_grad, gain, entry_state):
    start = entry_state.reshape(2 * L, HALF * E // L, E)
    kv = kv_sums(keys, values)
    mine, other = (kv[i].reshape(L, HALF * E // L, E) for i in range(2))
    *parts, extra = pair(mine, across_cores(other), 0)
    near_row = across_z(parts)
    qh, kh, vh, part, loc, mark = local_part(queries, keys, values, parts[0])
    inrow, total = row_sums(near_row, mark, False)
    others = across_y(total)
    gh, kq, mark = square_part(out_grad, qh, kh, total)
    scan = across_z(prior_sums(inrow, others, start, mark))
    own, other = split(scan, extra, mark, 0)
    halves = [x.reshape(HALF, E, E) for x in (own, across_cores(other))]
    att, sums, state = stats(qh, gh, part, *halves, gain)
    sums = lax.all_to_all(sums, "head", 0, 0, tiled=True)
    pre, wloc, mine, other = pre_part(qh, gh, att, gain, sums)
    *parts, extra = pair(mine, across_cores(other), 1)
    near_row = across_z(parts)
    normed, query_grad, mark = query_part(kh, vh, pre, att, state, loc, gain, sums, parts[0])
    inrow, total = row_sums(near_row, mark, True)
    others = across_y(total)
    kpart, vpart, mark = keyval_part(qh, kh, vh, pre, kq, wloc, total)
    *parts, entry_grad = later_sums(inrow, total, others, mark)
    own, other = split(across_z(parts), extra, mark, 1)
    key_grad, value_grad = final_part(kh, vh, kpart, vpart, own, across_cores(other))
    return normed, query_grad, key_grad, value_grad, entry_grad.reshape(HL, L, E)


def solution(mesh):
    tok = P("seq", "head", None)
    return jax.shard_map(
        body,
        mesh=mesh,
        in_specs=(tok, tok, tok, tok, P("head", None), P("head", None, None)),
        out_specs=(tok, tok, tok, tok, P("head", "seq", None)),
        check_vma=False,
    )
```

time: 131 us -> 104 us (0.79)
  blocking collectives: 30.4 us -> 8.06 us
  Pallas kernels: 65 us -> 42.7 us
  waiting for transfers between devices: 9.14 us -> 20.7 us
  starting transfers between devices: 19 us -> 28.8 us
  local copies, waits for them, and re-layouts: 5.51 us -> 2.32 us
    ppermute x0 -> x22, starting transfers between devices: none -> 28.8 us  [along(): return lax.ppermute(x, 'seq', [(seq(*p), seq(*move(*p))) for p in places])]
    all_to_all x1 -> x0, blocking collectives: 22.3 us -> none  [swap(): return lax.all_to_all(pieces, 'seq', 0, 0, tiled=True)]
    pallas_call x8 -> x15, Pallas kernels: 59.2 us -> 38 us  [the longest x1 7.77 us: local_part(): pl.pallas_call(local_kernel, grid=(NC,), in_specs=[TOK] * 3 + [ORDER], ou...]
    ppermute x0 -> x22, waiting for transfers between devices: none -> 20.7 us  [along(): return lax.ppermute(x, 'seq', [(seq(*p), seq(*move(*p))) for p in places])]
    all_to_all x3 -> x0, starting transfers between devices: 19 us -> none  [swap(): return lax.all_to_all(pieces, 'seq', 0, 0, tiled=True)]
    all_to_all x3 -> x0, waiting for transfers between devices: 9.14 us -> none  [swap(): return lax.all_to_all(pieces, 'seq', 0, 0, tiled=True)]
    unnamed x18 -> x16, local copies, waits for them, and re-layouts: 5.51 us -> 2.23 us
  transfers between devices with their start and end apart: 3 -> 22, of which waited for: 3 -> 11; matrix products, arithmetic and copies ran while one was open for 0% -> 0% of each run, Pallas kernels for 31% -> 26%
where the time goes in v3:
time: 104 us; the launch traced here: 103 us
  Pallas kernels  42.7 us (41%)
  starting transfers between devices  28.8 us (28%)
  waiting for transfers between devices  20.7 us (20%)
  blocking collectives  8.06 us (8%)
  local copies, waits for them, and re-layouts  2.32 us (2%)
    ppermute x22, starting transfers between devices, along(): return lax.ppermute(x, 'seq', [(seq(*p), seq(*move(*p))) for p in places])  28.8 us
    ppermute x22, waiting for transfers between devices, along(): return lax.ppermute(x, 'seq', [(seq(*p), seq(*move(*p))) for p in places])  20.7 us
    all_to_all x1, blocking collectives, body(): sums = lax.all_to_all(sums, 'head', 0, 0, tiled=True)  8.06 us
    pallas_call x1, Pallas kernels, local_part(): pl.pallas_call(local_kernel, grid=(NC,), in_specs=[TOK] * 3 + [ORDER], ou...  7.77 us
    pallas_call x1, Pallas kernels, keyval_part(): pl.pallas_call(keyval_kernel, grid=(NC,), in_specs=[HERE] * 6 + [ORDER],...  7.31 us
    pallas_call x1, Pallas kernels, query_part(): pl.pallas_call(query_kernel, grid=(NC,), in_specs=[HERE] * 8 + [ORDER], o...  6.94 us
    pallas_call x1, Pallas kernels, square_part(): pl.pallas_call(square_kernel, grid=(NC,), in_specs=[TOK, HERE, HERE, ORDE...  4.98 us
    pallas_call x1, Pallas kernels, kv_sums(): pl.pallas_call(kv_kernel, in_specs=[ORDER, ORDER], out_specs=HERE, out_sh...  4.69 us
  transfers between devices with their start and end apart: 22, of which 11 were waited for; matrix products, arithmetic and copies ran while one was open for 0% of the time, Pallas kernels for 26%

profile of v3, /device:TPU:1, one launch (start us, length us, event | category | flops | bytes accessed | tf_op | source)
XLA Modules:
  0.0 103.4 jit_solution(8435346358692665697)
XLA Ops:
  0.6 4.7 %kv_sums.1 = f32[2,8,128,128]{3,2,1,0:T(8,128)S(1)} custom-call(bf16[768,16,128]{2,1,0:T(8,128)(2,1)} %k_ref.1, bf16[768,16,128]{2,1,0:T(8,128)(2,1)} %v_ref.1), custom_call_target="tpu_custom_call" | custom-call | flops 402653184 | bytes 7340032 | tf_op jit(solution)/shard_map/kv_sums/pallas_call | solution.py:116
  5.4 1.5 %collective-permute-start = (f32[4,256,128]{2,1,0:T(8,128)S(1)}, f32[4,256,128]{2,1,0:T(8,128)S(1)}, u32[]{:S(2)}, u32[]{:S(2)}) collective-permute-start(f32[4,256,128]{2,1,0:T(8,128)S(1)} %bitcast.10), channel_id=1, source_target_pairs={{0,4},{4,0},{8,12},{12,8},{16,20},{20,16},{24,28},{28,24},{32,36},... | collective-permute-start | bytes 1572872 | tf_op jit(solution)/shard_map/ppermute | solution.py:531
  6.9 1.5 %collective-permute-done.r_ref = f32[4,256,128]{2,1,0:T(8,128)S(1)} collective-permute-done((f32[4,256,128]{2,1,0:T(8,128)S(1)}, f32[4,256,128]{2,1,0:T(8,128)S(1)}, u32[]{:S(2)}, u32[]{:S(2)}) %collective-permute-start) | collective-permute-done | bytes 524320 | tf_op jit(solution)/shard_map/ppermute | solution.py:531
  9.2 1.7 %collective-permute-start.1 = (f32[256,128]{1,0:T(8,128)S(1)}, f32[256,128]{1,0:T(8,128)S(1)}, u32[]{:S(2)}, u32[]{:S(2)}) collective-permute-start(f32[256,128]{1,0:T(8,128)S(1)} %get-tuple-element.60), channel_id=1, source_target_pairs={{0,8},{4,12},{8,16},{12,20},{16,24},{20,28},{24,0},{28,4},{32,40},... | collective-permute-start | bytes 393224 | tf_op jit(solution)/shard_map/ppermute | solution.py:531
  11.0 3.3 %collective-permute-start.2 = (f32[256,128]{1,0:T(8,128)S(1)}, f32[256,128]{1,0:T(8,128)S(1)}, u32[]{:S(2)}, u32[]{:S(2)}) collective-permute-start(f32[256,128]{1,0:T(8,128)S(1)} %get-tuple-element.61), channel_id=1, source_target_pairs={{0,16},{4,20},{8,24},{12,28},{16,0},{20,4},{24,8},{28,12},{32,48},... | collective-permute-start | bytes 393224 | tf_op jit(solution)/shard_map/ppermute | solution.py:531
  15.0 7.8 %local_part.1 = (bf16[16,768,128]{2,1,0:T(8,128)(2,1)S(1)}, bf16[16,768,128]{2,1,0:T(8,128)(2,1)S(1)}, bf16[16,768,128]{2,1,0:T(8,128)(2,1)S(1)}, bf16[16,768,12...) custom-call(bf16[768,16,128]{2,1,0:T(8,128)(2,1)} %q_ref.1, ...), custom_call_target="tpu_custom_call" | custom-call | flops 2415919104 | bytes 25165824 | tf_op jit(solution)/shard_map/local_part/pallas_call | solution.py:279
  22.9 2.8 %collective-permute-start.6 = (f32[256,128]{1,0:T(8,128)S(1)}, f32[256,128]{1,0:T(8,128)S(1)}, u32[]{:S(2)}, u32[]{:S(2)}) collective-permute-start(f32[256,128]{1,0:T(8,128)S(1)} %get-tuple-element.64._), channel_id=1, source_target_pairs={{0,96},{4,100},{8,104},{12,108},{16,112},{20,116},{24,120},{28,124... | collective-permute-start | bytes 393224 | tf_op jit(solution)/shard_map/ppermute | solution.py:531
  26.8 5.0 %square_part.1 = (bf16[16,768,128]{2,1,0:T(8,128)(2,1)S(1)}, bf16[16,768,256]{2,1,0:T(8,128)(2,1)S(1)}, f32[8,128]{1,0:T(8,128)}) custom-call(bf16[768,16,128]{2,1,0:T(8,128)(2,1)} %g_ref.1, bf16[16,768,128]{2,1,0:T(8,128)(2,1)S(1)} %get-tuple-element.59.q_ref, bf16[16,768,128]{2,1,0:T(8,128)(2,1)S(1)} %get-tuple-element.57.k_ref, f32[256,128]{1,0:T(8,128)} %copy-done.6), custom_call_target="tpu_custom_call" | custom-call | flops 805306368 | bytes 19922944 | tf_op jit(solution)/shard_map/square_part/pallas_call | solution.py:302
  31.8 3.0 %collective-permute-done.4.u1 = f32[256,128]{1,0:T(8,128)S(1)} collective-permute-done((f32[256,128]{1,0:T(8,128)S(1)}, f32[256,128]{1,0:T(8,128)S(1)}, u32[]{:S(2)}, u32[]{:S(2)}) %collective-permute-start.4) | collective-permute-done | bytes 131104 | tf_op jit(solution)/shard_map/ppermute | solution.py:531
  34.8 1.0 prior_sums.1
  37.3 1.7 %collective-permute-start.9 = (f32[256,128]{1,0:T(8,128)S(1)}, f32[256,128]{1,0:T(8,128)S(1)}, u32[]{:S(2)}, u32[]{:S(2)}) collective-permute-start(f32[256,128]{1,0:T(8,128)S(1)} %get-tuple-element.72), channel_id=1, source_target_pairs={{0,24},{4,28},{8,0},{12,4},{16,8},{20,12},{24,16},{28,20},{32,56},... | collective-permute-start | bytes 393224 | tf_op jit(solution)/shard_map/ppermute | solution.py:531
  39.0 2.5 %collective-permute-done.7.refs_1_ = f32[256,128]{1,0:T(8,128)S(1)} collective-permute-done((f32[256,128]{1,0:T(8,128)S(1)}, f32[256,128]{1,0:T(8,128)S(1)}, u32[]{:S(2)}, u32[]{:S(2)}) %collective-permute-start.7) | collective-permute-done | bytes 131104 | tf_op jit(solution)/shard_map/ppermute | solution.py:531
  41.6 0.9 collective-permute-done.8.refs_2_
  42.5 1.5 %collective-permute-done.9.refs_3_ = f32[256,128]{1,0:T(8,128)S(1)} collective-permute-done((f32[256,128]{1,0:T(8,128)S(1)}, f32[256,128]{1,0:T(8,128)S(1)}, u32[]{:S(2)}, u32[]{:S(2)}) %collective-permute-start.9) | collective-permute-done | bytes 131104 | tf_op jit(solution)/shard_map/ppermute | solution.py:531
  44.1 2.4 %collective-permute-start.10 = (f32[4,256,128]{2,1,0:T(8,128)S(1)}, f32[4,256,128]{2,1,0:T(8,128)S(1)}, u32[]{:S(2)}, u32[]{:S(2)}) collective-permute-start(f32[4,256,128]{2,1,0:T(8,128)S(1)} %get-tuple-element.75), channel_id=1, source_target_pairs={{0,4},{4,0},{8,12},{12,8},{16,20},{20,16},{24,28},{28,24},{32,36},... | collective-permute-start | bytes 1572872 | tf_op jit(solution)/shard_map/ppermute | solution.py:531
  46.5 1.5 %collective-permute-done.10 = f32[4,256,128]{2,1,0:T(8,128)S(1)} collective-permute-done((f32[4,256,128]{2,1,0:T(8,128)S(1)}, f32[4,256,128]{2,1,0:T(8,128)S(1)}, u32[]{:S(2)}, u32[]{:S(2)}) %collective-permute-start.10) | collective-permute-done | bytes 524320 | tf_op jit(solution)/shard_map/ppermute | solution.py:531
  48.0 2.5 %stats.1 = (f32[16,768,128]{2,1,0:T(8,128)S(1)}, f32[4,3,2,256]{3,2,1,0:T(2,128)S(1)}, bf16[16,128,128]{2,1,0:T(8,128)(2,1)S(1)}) custom-call(bf16[16,768,128]{2,1,0:T(8,128)(2,1)S(1)} %get-tuple-element.59.q_ref, bf16[16,768,128]{2,1,0:T(8,128)(2,1)S(1)} %get-tuple-element.65.g_ref, bf16[16,768,128]{2,1,0:T(8,128)(2,1)S(1)} %get-tuple-element.66.a_ref, ...), custom_call_target="tpu_custom_call" | custom-call | flops 402653184 | bytes 10485760 | tf_op jit(solution)/shard_map/stats/pallas_call | solution.py:340
  50.5 8.1 %all_to_all.5.sums_ref = f32[4,3,2,256]{3,2,1,0:T(2,128)S(1)} all-to-all(f32[4,3,2,256]{3,2,1,0:T(2,128)S(1)} %get-tuple-element.77), channel_id=1, replica_groups=mesh['seq'=32,'head'=4] {'head'}, dimensions={0} | all-to-all | bytes 49152 | tf_op jit(solution)/shard_map/all_to_all | solution.py:561
  58.6 2.4 %pre_part.1 = (bf16[16,768,128]{2,1,0:T(8,128)(2,1)S(1)}, bf16[3,16,128,128]{3,2,1,0:T(8,128)(2,1)S(1)}, f32[4,256,128]{2,1,0:T(8,128)S(1)}, f32[4,256,128]{2,1,0:T(8,128)S(1)}) custom-call(bf16[16,768,128]{2,1,0:T(8,128)(2,1)S(1)} %get-tuple-element.59.q_ref, bf16[16,768,128]{2,1,0:T(8,128)(2,1)S(1)} %get-tuple-element.65.g_ref, ...), custom_call_target="tpu_custom_call" | custom-call | flops 805306368 | bytes 16777216 | tf_op jit(solution)/shard_map/pre_part/pallas_call | solution.py:401
  61.0 2.1 %collective-permute-start.11 = (f32[4,256,128]{2,1,0:T(8,128)S(1)}, f32[4,256,128]{2,1,0:T(8,128)S(1)}, u32[]{:S(2)}, u32[]{:S(2)}) collective-permute-start(f32[4,256,128]{2,1,0:T(8,128)S(1)} %get-tuple-element.82), channel_id=1, source_target_pairs={{0,4},{4,0},{8,12},{12,8},{16,20},{20,16},{24,28},{28,24},{32,36},... | collective-permute-start | bytes 1572872 | tf_op jit(solution)/shard_map/ppermute | solution.py:531
  63.1 1.5 %collective-permute-done.11.r_ref = f32[4,256,128]{2,1,0:T(8,128)S(1)} collective-permute-done((f32[4,256,128]{2,1,0:T(8,128)S(1)}, f32[4,256,128]{2,1,0:T(8,128)S(1)}, u32[]{:S(2)}, u32[]{:S(2)}) %collective-permute-start.11) | collective-permute-done | bytes 524320 | tf_op jit(solution)/shard_map/ppermute | solution.py:531
  65.9 3.0 %collective-permute-start.13 = (f32[256,128]{1,0:T(8,128)S(1)}, f32[256,128]{1,0:T(8,128)S(1)}, u32[]{:S(2)}, u32[]{:S(2)}) collective-permute-start(f32[256,128]{1,0:T(8,128)S(1)} %get-tuple-element.89), channel_id=1, source_target_pairs={{0,16},{4,20},{8,24},{12,28},{16,0},{20,4},{24,8},{28,12},{32,48},... | collective-permute-start | bytes 393224 | tf_op jit(solution)/shard_map/ppermute | solution.py:531
  69.0 6.9 %query_part.1 = (bf16[768,16,128]{2,1,0:T(8,128)(2,1)}, bf16[768,16,128]{2,1,0:T(8,128)(2,1)}, f32[8,128]{1,0:T(8,128)}) custom-call(bf16[16,768,128]{2,1,0:T(8,128)(2,1)S(1)} %get-tuple-element.57.k_ref, bf16[16,768,128]{2,1,0:T(8,128)(2,1)S(1)} %get-tuple-element.58.v_ref, bf16[16,768,128]{2,1,0:T(8,128)(2,1)S(1)} %get-tuple-element.78.p_ref, ...), custom_call_target="tpu_custom_call" | custom-call | flops 2818572288 | bytes 31457280 | tf_op jit(solution)/shard_map/query_part/pallas_call | solution.py:438
  76.6 1.0 collective-permute-start.15
  77.6 7.3 %keyval_part.1 = (bf16[16,768,128]{2,1,0:T(8,128)(2,1)S(1)}, bf16[16,768,128]{2,1,0:T(8,128)(2,1)S(1)}, f32[8,128]{1,0:T(8,128)}) custom-call(bf16[16,768,128]{2,1,0:T(8,128)(2,1)S(1)} %get-tuple-element.59.q_ref, bf16[16,768,128]{2,1,0:T(8,128)(2,1)S(1)} %get-tuple-element.57.k_ref, bf16[16,768,128]{2,1,0:T(8,128)(2,1)S(1)} %get-tuple-element.58.v_ref, ...), custom_call_target="tpu_custom_call" | custom-call | flops 3221225472 | bytes 29360128 | tf_op jit(solution)/shard_map/keyval_part/pallas_call | solution.py:465
  87.4 1.0 collective-permute-start.18
  88.4 2.2 %collective-permute-start.19 = (f32[256,128]{1,0:T(8,128)S(1)}, f32[256,128]{1,0:T(8,128)S(1)}, u32[]{:S(2)}, u32[]{:S(2)}) collective-permute-start(f32[256,128]{1,0:T(8,128)S(1)} %get-tuple-element.99), channel_id=1, source_target_pairs={{0,16},{4,20},{8,24},{12,28},{16,0},{20,4},{24,8},{28,12},{32,48},... | collective-permute-start | bytes 393224 | tf_op jit(solution)/shard_map/ppermute | solution.py:531
  90.8 2.2 %collective-permute-done.18.refs_1_ = f32[256,128]{1,0:T(8,128)S(1)} collective-permute-done((f32[256,128]{1,0:T(8,128)S(1)}, f32[256,128]{1,0:T(8,128)S(1)}, u32[]{:S(2)}, u32[]{:S(2)}) %collective-permute-start.18) | collective-permute-done | bytes 131104 | tf_op jit(solution)/shard_map/ppermute | solution.py:531
  92.9 3.6 %collective-permute-done.19.refs_2_ = f32[256,128]{1,0:T(8,128)S(1)} collective-permute-done((f32[256,128]{1,0:T(8,128)S(1)}, f32[256,128]{1,0:T(8,128)S(1)}, u32[]{:S(2)}, u32[]{:S(2)}) %collective-permute-start.19) | collective-permute-done | bytes 131104 | tf_op jit(solution)/shard_map/ppermute | solution.py:531
  96.6 1.5 %collective-permute-start.21 = (f32[4,256,128]{2,1,0:T(8,128)S(1)}, f32[4,256,128]{2,1,0:T(8,128)S(1)}, u32[]{:S(2)}, u32[]{:S(2)}) collective-permute-start(f32[4,256,128]{2,1,0:T(8,128)S(1)} %get-tuple-element.103), channel_id=1, source_target_pairs={{0,4},{4,0},{8,12},{12,8},{16,20},{20,16},{24,28},{28,24},{32,36},... | collective-permute-start | bytes 1572872 | tf_op jit(solution)/shard_map/ppermute | solution.py:531
  98.1 1.5 %collective-permute-done.21.got_ref = f32[4,256,128]{2,1,0:T(8,128)S(1)} collective-permute-done((f32[4,256,128]{2,1,0:T(8,128)S(1)}, f32[4,256,128]{2,1,0:T(8,128)S(1)}, u32[]{:S(2)}, u32[]{:S(2)}) %collective-permute-start.21) | collective-permute-done | bytes 524320 | tf_op jit(solution)/shard_map/ppermute | solution.py:531
  99.6 3.8 %final_part.1 = (bf16[768,16,128]{2,1,0:T(8,128)(2,1)}, bf16[768,16,128]{2,1,0:T(8,128)(2,1)}) custom-call(bf16[16,768,128]{2,1,0:T(8,128)(2,1)S(1)} %get-tuple-element.57.k_ref, bf16[16,768,128]{2,1,0:T(8,128)(2,1)S(1)} %get-tuple-element.58.v_ref, bf16[16,768,128]{2,1,0:T(8,128)(2,1)S(1)} %get-tuple-element.93.kp_ref, ...), custom_call_target="tpu_custom_call" | custom-call | flops 805306368 | bytes 19922944 | tf_op jit(solution)/shard_map/final_part/pallas_call | solution.py:513
  (46 shorter events, 9.0 us)
Async XLA Ops:
  5.4 3.0 %collective-permute-start = (f32[4,256,128]{2,1,0:T(8,128)S(1)}, f32[4,256,128]{2,1,0:T(8,128)S(1)}, u32[]{:S(2)}, u32[]{:S(2)}) collective-permute-start(f32[4,256,128]{2,1,0:T(8,128)S(1)} %bitcast.10), channel_id=1, source_target_pairs={{0,4},{4,0},{8,12},{12,8},{16,20},{20,16},{24,28},{28,24},{32,36},... | collective-permute-start | bytes 1572872 | tf_op jit(solution)/shard_map/ppermute | solution.py:531
  8.6 0.7 copy-start.2
  9.2 13.5 %collective-permute-start.1 = (f32[256,128]{1,0:T(8,128)S(1)}, f32[256,128]{1,0:T(8,128)S(1)}, u32[]{:S(2)}, u32[]{:S(2)}) collective-permute-start(f32[256,128]{1,0:T(8,128)S(1)} %get-tuple-element.60), channel_id=1, source_target_pairs={{0,8},{4,12},{8,16},{12,20},{16,24},{20,28},{24,0},{28,4},{32,40},... | collective-permute-start | bytes 393224 | tf_op jit(solution)/shard_map/ppermute | solution.py:531
  11.0 11.8 %collective-permute-start.2 = (f32[256,128]{1,0:T(8,128)S(1)}, f32[256,128]{1,0:T(8,128)S(1)}, u32[]{:S(2)}, u32[]{:S(2)}) collective-permute-start(f32[256,128]{1,0:T(8,128)S(1)} %get-tuple-element.61), channel_id=1, source_target_pairs={{0,16},{4,20},{8,24},{12,28},{16,0},{20,4},{24,8},{28,12},{32,48},... | collective-permute-start | bytes 393224 | tf_op jit(solution)/shard_map/ppermute | solution.py:531
  14.3 8.5 %collective-permute-start.3 = (f32[256,128]{1,0:T(8,128)S(1)}, f32[256,128]{1,0:T(8,128)S(1)}, u32[]{:S(2)}, u32[]{:S(2)}) collective-permute-start(f32[256,128]{1,0:T(8,128)S(1)} %get-tuple-element.62), channel_id=1, source_target_pairs={{0,24},{4,28},{8,0},{12,4},{16,8},{20,12},{24,16},{28,20},{32,56},... | collective-permute-start | bytes 393224 | tf_op jit(solution)/shard_map/ppermute | solution.py:531
  15.0 7.8 %copy-start.3 = (f32[256,128]{1,0:T(8,128)S(1)}, f32[256,128]{1,0:T(8,128)}, u32[]{:S(2)}) copy-start(f32[256,128]{1,0:T(8,128)} %copy-done.2) | copy-start | bytes 393220
  22.9 3.9 %copy-start.6 = (f32[256,128]{1,0:T(8,128)}, f32[256,128]{1,0:T(8,128)S(1)}, u32[]{:S(2)}) copy-start(f32[256,128]{1,0:T(8,128)S(1)} %get-tuple-element.64._) | copy-start | bytes 393220
  22.9 8.8 %collective-permute-start.6 = (f32[256,128]{1,0:T(8,128)S(1)}, f32[256,128]{1,0:T(8,128)S(1)}, u32[]{:S(2)}, u32[]{:S(2)}) collective-permute-start(f32[256,128]{1,0:T(8,128)S(1)} %get-tuple-element.64._), channel_id=1, source_target_pairs={{0,96},{4,100},{8,104},{12,108},{16,112},{20,116},{24,120},{28,124... | collective-permute-start | bytes 393224 | tf_op jit(solution)/shard_map/ppermute | solution.py:531
  25.7 6.0 %collective-permute-start.5 = (f32[256,128]{1,0:T(8,128)S(1)}, f32[256,128]{1,0:T(8,128)S(1)}, u32[]{:S(2)}, u32[]{:S(2)}) collective-permute-start(f32[256,128]{1,0:T(8,128)S(1)} %get-tuple-element.64._), channel_id=1, source_target_pairs={{0,64},{4,68},{8,72},{12,76},{16,80},{20,84},{24,88},{28,92},{32,9... | collective-permute-start | bytes 393224 | tf_op jit(solution)/shard_map/ppermute | solution.py:531
  26.1 8.7 %collective-permute-start.4 = (f32[256,128]{1,0:T(8,128)S(1)}, f32[256,128]{1,0:T(8,128)S(1)}, u32[]{:S(2)}, u32[]{:S(2)}) collective-permute-start(f32[256,128]{1,0:T(8,128)S(1)} %get-tuple-element.64._), channel_id=1, source_target_pairs={{0,32},{4,36},{8,40},{12,44},{16,48},{20,52},{24,56},{28,60},{32,6... | collective-permute-start | bytes 393224 | tf_op jit(solution)/shard_map/ppermute | solution.py:531
  26.8 21.2 %copy-start.7 = (f32[16,128]{1,0:T(8,128)S(1)}, f32[16,128]{1,0:T(8,128)}, u32[]{:S(2)}) copy-start(f32[16,128]{1,0:T(8,128)} %gain_ref.5) | copy-start | bytes 24580
  35.7 5.8 %collective-permute-start.7 = (f32[256,128]{1,0:T(8,128)S(1)}, f32[256,128]{1,0:T(8,128)S(1)}, u32[]{:S(2)}, u32[]{:S(2)}) collective-permute-start(f32[256,128]{1,0:T(8,128)S(1)} %get-tuple-element.70), channel_id=1, source_target_pairs={{0,8},{4,12},{8,16},{12,20},{16,24},{20,28},{24,0},{28,4},{32,40},... | collective-permute-start | bytes 393224 | tf_op jit(solution)/shard_map/ppermute | solution.py:531
  36.5 6.0 %collective-permute-start.8 = (f32[256,128]{1,0:T(8,128)S(1)}, f32[256,128]{1,0:T(8,128)S(1)}, u32[]{:S(2)}, u32[]{:S(2)}) collective-permute-start(f32[256,128]{1,0:T(8,128)S(1)} %get-tuple-element.71), channel_id=1, source_target_pairs={{0,16},{4,20},{8,24},{12,28},{16,0},{20,4},{24,8},{28,12},{32,48},... | collective-permute-start | bytes 393224 | tf_op jit(solution)/shard_map/ppermute | solution.py:531
  37.3 6.7 %collective-permute-start.9 = (f32[256,128]{1,0:T(8,128)S(1)}, f32[256,128]{1,0:T(8,128)S(1)}, u32[]{:S(2)}, u32[]{:S(2)}) collective-permute-start(f32[256,128]{1,0:T(8,128)S(1)} %get-tuple-element.72), channel_id=1, source_target_pairs={{0,24},{4,28},{8,0},{12,4},{16,8},{20,12},{24,16},{28,20},{32,56},... | collective-permute-start | bytes 393224 | tf_op jit(solution)/shard_map/ppermute | solution.py:531
  44.1 3.9 %collective-permute-start.10 = (f32[4,256,128]{2,1,0:T(8,128)S(1)}, f32[4,256,128]{2,1,0:T(8,128)S(1)}, u32[]{:S(2)}, u32[]{:S(2)}) collective-permute-start(f32[4,256,128]{2,1,0:T(8,128)S(1)} %get-tuple-element.75), channel_id=1, source_target_pairs={{0,4},{4,0},{8,12},{12,8},{16,20},{20,16},{24,28},{28,24},{32,36},... | collective-permute-start | bytes 1572872 | tf_op jit(solution)/shard_map/ppermute | solution.py:531
  61.0 3.6 %collective-permute-start.11 = (f32[4,256,128]{2,1,0:T(8,128)S(1)}, f32[4,256,128]{2,1,0:T(8,128)S(1)}, u32[]{:S(2)}, u32[]{:S(2)}) collective-permute-start(f32[4,256,128]{2,1,0:T(8,128)S(1)} %get-tuple-element.82), channel_id=1, source_target_pairs={{0,4},{4,0},{8,12},{12,8},{16,20},{20,16},{24,28},{28,24},{32,36},... | collective-permute-start | bytes 1572872 | tf_op jit(solution)/shard_map/ppermute | solution.py:531
  64.7 0.7 copy-start
  65.4 10.5 %collective-permute-start.12 = (f32[256,128]{1,0:T(8,128)S(1)}, f32[256,128]{1,0:T(8,128)S(1)}, u32[]{:S(2)}, u32[]{:S(2)}) collective-permute-start(f32[256,128]{1,0:T(8,128)S(1)} %get-tuple-element.88), channel_id=1, source_target_pairs={{0,8},{4,12},{8,16},{12,20},{16,24},{20,28},{24,0},{28,4},{32,40},... | collective-permute-start | bytes 393224 | tf_op jit(solution)/shard_map/ppermute | solution.py:531
  65.9 10.0 %collective-permute-start.13 = (f32[256,128]{1,0:T(8,128)S(1)}, f32[256,128]{1,0:T(8,128)S(1)}, u32[]{:S(2)}, u32[]{:S(2)}) collective-permute-start(f32[256,128]{1,0:T(8,128)S(1)} %get-tuple-element.89), channel_id=1, source_target_pairs={{0,16},{4,20},{8,24},{12,28},{16,0},{20,4},{24,8},{28,12},{32,48},... | collective-permute-start | bytes 393224 | tf_op jit(solution)/shard_map/ppermute | solution.py:531
  68.9 7.0 %collective-permute-start.14 = (f32[256,128]{1,0:T(8,128)S(1)}, f32[256,128]{1,0:T(8,128)S(1)}, u32[]{:S(2)}, u32[]{:S(2)}) collective-permute-start(f32[256,128]{1,0:T(8,128)S(1)} %get-tuple-element.90), channel_id=1, source_target_pairs={{0,24},{4,28},{8,0},{12,4},{16,8},{20,12},{24,16},{28,20},{32,56},... | collective-permute-start | bytes 393224 | tf_op jit(solution)/shard_map/ppermute | solution.py:531
  69.0 7.0 %copy-start.1 = (f32[256,128]{1,0:T(8,128)S(1)}, f32[256,128]{1,0:T(8,128)}, u32[]{:S(2)}) copy-start(f32[256,128]{1,0:T(8,128)} %copy-done) | copy-start | bytes 393220
  76.0 1.6 %copy-start.4 = (f32[256,128]{1,0:T(8,128)}, f32[256,128]{1,0:T(8,128)S(1)}, u32[]{:S(2)}) copy-start(f32[256,128]{1,0:T(8,128)S(1)} %get-tuple-element.92._.t_ref) | copy-start | bytes 393220
  76.0 8.9 %collective-permute-start.17 = (f32[256,128]{1,0:T(8,128)S(1)}, f32[256,128]{1,0:T(8,128)S(1)}, u32[]{:S(2)}, u32[]{:S(2)}) collective-permute-start(f32[256,128]{1,0:T(8,128)S(1)} %get-tuple-element.92._.t_ref), channel_id=1, source_target_pairs={{0,96},{4,100},{8,104},{12,108},{16,112},{20,116},{24,120},{28,124... | collective-permute-start | bytes 393224 | tf_op jit(solution)/shard_map/ppermute | solution.py:531
  76.1 8.8 %collective-permute-start.16 = (f32[256,128]{1,0:T(8,128)S(1)}, f32[256,128]{1,0:T(8,128)S(1)}, u32[]{:S(2)}, u32[]{:S(2)}) collective-permute-start(f32[256,128]{1,0:T(8,128)S(1)} %get-tuple-element.92._.t_ref), channel_id=1, source_target_pairs={{0,64},{4,68},{8,72},{12,76},{16,80},{20,84},{24,88},{28,92},{32,9... | collective-permute-start | bytes 393224 | tf_op jit(solution)/shard_map/ppermute | solution.py:531
  76.6 9.2 %collective-permute-start.15 = (f32[256,128]{1,0:T(8,128)S(1)}, f32[256,128]{1,0:T(8,128)S(1)}, u32[]{:S(2)}, u32[]{:S(2)}) collective-permute-start(f32[256,128]{1,0:T(8,128)S(1)} %get-tuple-element.92._.t_ref), channel_id=1, source_target_pairs={{0,32},{4,36},{8,40},{12,44},{16,48},{20,52},{24,56},{28,60},{32,6... | collective-permute-start | bytes 393224 | tf_op jit(solution)/shard_map/ppermute | solution.py:531
  85.8 0.9 copy-start.5
  87.4 5.6 %collective-permute-start.18 = (f32[256,128]{1,0:T(8,128)S(1)}, f32[256,128]{1,0:T(8,128)S(1)}, u32[]{:S(2)}, u32[]{:S(2)}) collective-permute-start(f32[256,128]{1,0:T(8,128)S(1)} %get-tuple-element.98), channel_id=1, source_target_pairs={{0,8},{4,12},{8,16},{12,20},{16,24},{20,28},{24,0},{28,4},{32,40},... | collective-permute-start | bytes 393224 | tf_op jit(solution)/shard_map/ppermute | solution.py:531
  88.4 8.1 %collective-permute-start.19 = (f32[256,128]{1,0:T(8,128)S(1)}, f32[256,128]{1,0:T(8,128)S(1)}, u32[]{:S(2)}, u32[]{:S(2)}) collective-permute-start(f32[256,128]{1,0:T(8,128)S(1)} %get-tuple-element.99), channel_id=1, source_target_pairs={{0,16},{4,20},{8,24},{12,28},{16,0},{20,4},{24,8},{28,12},{32,48},... | collective-permute-start | bytes 393224 | tf_op jit(solution)/shard_map/ppermute | solution.py:531
  90.6 5.9 %collective-permute-start.20 = (f32[256,128]{1,0:T(8,128)S(1)}, f32[256,128]{1,0:T(8,128)S(1)}, u32[]{:S(2)}, u32[]{:S(2)}) collective-permute-start(f32[256,128]{1,0:T(8,128)S(1)} %get-tuple-element.100), channel_id=1, source_target_pairs={{0,24},{4,28},{8,0},{12,4},{16,8},{20,12},{24,16},{28,20},{32,56},... | collective-permute-start | bytes 393224 | tf_op jit(solution)/shard_map/ppermute | solution.py:531
  96.6 3.0 %collective-permute-start.21 = (f32[4,256,128]{2,1,0:T(8,128)S(1)}, f32[4,256,128]{2,1,0:T(8,128)S(1)}, u32[]{:S(2)}, u32[]{:S(2)}) collective-permute-start(f32[4,256,128]{2,1,0:T(8,128)S(1)} %get-tuple-element.103), channel_id=1, source_target_pairs={{0,4},{4,0},{8,12},{12,8},{16,20},{20,16},{24,28},{28,24},{32,36},... | collective-permute-start | bytes 1572872 | tf_op jit(solution)/shard_map/ppermute | solution.py:531

commit v4 on v3

v4 whole, which is shorter than its diff:
```python
import functools

import jax
import jax.numpy as jnp
from jax import lax
from jax.experimental import pallas as pl
from jax.experimental.pallas import tpu as pltpu
from jax.sharding import PartitionSpec as P

H = 64
E = 128
T = 768
HL = 16
C = 256
NC = T // C
B = 128
NB = T // B
AHEAD = 3
ZSTEPS = (0, 2, 1, 3)
YSTEPS = (1, 3, 2)
N = 32
L = 4
HALF = HL // 2
X = 4
WIDTH = H * E
epsilon = 1e-06
f32 = jnp.float32
bf16 = jnp.bfloat16
MIB = 1 << 20


def mm(a, b):
    return lax.dot_general(a, b, (((1,), (0,)), ((), ())), preferred_element_type=f32)


def mm_nt(a, b):
    return lax.dot_general(a, b, (((1,), (1,)), ((), ())), preferred_element_type=f32)


def mm_tn(a, b):
    return lax.dot_general(a, b, (((0,), (0,)), ((), ())), preferred_element_type=f32)


def causal(later=False):
    row = lax.broadcasted_iota(jnp.int32, (C, C), 0)
    col = lax.broadcasted_iota(jnp.int32, (C, C), 1)
    return row <= col if later else col <= row


def heads_first(ref):
    return jnp.swapaxes(ref[...], 0, 1)


def params(vmem=24):
    return pltpu.CompilerParams(vmem_limit_bytes=vmem * MIB)


def cost(flops, moved):
    return pl.CostEstimate(flops=flops, bytes_accessed=moved, transcendentals=0)


HERE = pl.BlockSpec(memory_space=pltpu.VMEM)
AWAY = pl.BlockSpec(memory_space=pl.ANY)
TOK = pl.BlockSpec((C, HL, E), lambda i: (i, 0, 0))
MAJOR = pltpu.VMEM((HL, T, E), bf16)
SQUARES = pltpu.VMEM((HL, T, C), bf16)
STATES = pltpu.VMEM((NC, HL, E, E), bf16)
TOKENS = pltpu.HBM((T, HL, E), bf16)
QUARTER = pltpu.VMEM((HALF * E // L, E), f32)
QUARTERS = pltpu.VMEM((L, HALF * E // L, E), f32)
MARK = pltpu.VMEM((8, E), f32)


def my_place():
    me = lax.axis_index("seq")
    return me // (2 * L), lax.rem(me // 2, L), lax.rem(me, 2)


def my_heads():
    _, _, core = my_place()
    return core * HALF, (1 - core) * HALF


def far(*arrays):
    return tuple(pltpu.with_memory_space_constraint(a, pltpu.HBM) for a in arrays)


def near(*arrays):
    return tuple(pltpu.with_memory_space_constraint(a, pltpu.VMEM) for a in arrays)


def rows(step):
    return pl.ds(pl.multiple_of(step * C, C), C)


def mm_lower(a, b):
    return jnp.concatenate([mm(a[:B, :B], b[:B]), mm(a[B:], b)], axis=0)


def mm_upper(a, b):
    return jnp.concatenate([mm(a[:B], b), mm(a[B:, B:], b[B:])], axis=0)


def kv_other_kernel(k_hbm, v_hbm, kh_ref, vh_ref, o_ref, k_buf, v_buf, sems):
    _, other = my_heads()
    copies = []
    for i in range(NB):
        at = pl.ds(i * B, B)
        for n, (src, dst) in enumerate(((k_hbm, k_buf), (v_hbm, v_buf))):
            copies.append(pltpu.make_async_copy(src.at[at], dst.at[at], sems.at[i, n]))
    for copy in copies[: 2 * AHEAD]:
        copy.start()
    for i in range(NB):
        at = slice(i * B, (i + 1) * B)
        copies[2 * i].wait()
        copies[2 * i + 1].wait()
        for copy in copies[2 * (i + AHEAD) : 2 * (i + AHEAD) + 2]:
            copy.start()
        kh_ref[:, at] = jnp.swapaxes(k_buf[at], 0, 1)
        vh_ref[:, at] = jnp.swapaxes(v_buf[at], 0, 1)
        for j in range(HALF):
            part = mm_tn(kh_ref[other + j, at], vh_ref[other + j, at])
            o_ref[j] = part if i == 0 else o_ref[j] + part


def kv_other(keys, values):
    return pl.pallas_call(
        kv_other_kernel,
        in_specs=[AWAY, AWAY],
        out_specs=[HERE] * 3,
        out_shape=[MAJOR] * 2 + [pltpu.VMEM((HALF, E, E), f32)],
        scratch_shapes=[
            pltpu.VMEM((T, HL, E), bf16),
            pltpu.VMEM((T, HL, E), bf16),
            pltpu.SemaphoreType.DMA((NB, 2)),
        ],
        compiler_params=params(24),
        cost_estimate=cost(T * HL * E * E, 7 * MIB),
        name="kv_other",
    )(*far(keys, values))


def kv_mine_kernel(k_ref, v_ref, o_ref):
    mine, _ = my_heads()
    for j in range(HALF):
        o_ref[j] = mm_tn(k_ref[mine + j], v_ref[mine + j])


def kv_mine(kh, vh):
    return pl.pallas_call(
        kv_mine_kernel,
        in_specs=[HERE] * 2,
        out_specs=HERE,
        out_shape=pltpu.VMEM((HALF, E, E), f32),
        compiler_params=params(4),
        cost_estimate=cost(T * HL * E * E, MIB),
        name="kv_mine",
    )(*near(kh, vh))


def pair_kernel(first, m_ref, r_ref, *outs):
    _, z, core = my_place()
    for out, k in zip(outs, ZSTEPS):
        at = lax.rem(z + k, L)
        out[...] = m_ref[at] + r_ref[at]
    outs[L][...] = jnp.where(core == first, m_ref[...], r_ref[...])


def pair(mine, got, first):
    return pl.pallas_call(
        functools.partial(pair_kernel, first),
        in_specs=[HERE] * 2,
        out_specs=[HERE] * (L + 1),
        out_shape=[QUARTER] * L + [QUARTERS],
        compiler_params=params(2),
        cost_estimate=cost(HALF * E * E, 2 * MIB),
        name="pair",
    )(*near(mine, got))


def row_kernel(backward, *refs):
    parts, (_, e_ref, t_ref, buf) = refs[:L], refs[L:]
    _, z, _ = my_place()
    for part, k in zip(parts, ZSTEPS):
        buf[lax.rem(z + L - k, L)] = part[...]
    total = jnp.zeros_like(t_ref)
    for i in reversed(range(L)) if backward else range(L):
        e_ref[i] = total
        total = total + buf[i]
    t_ref[...] = total


def row_sums(parts, order, backward):
    return pl.pallas_call(
        functools.partial(row_kernel, backward),
        in_specs=[HERE] * (L + 1),
        out_specs=[HERE] * 2,
        out_shape=[QUARTERS, QUARTER],
        scratch_shapes=[QUARTERS],
        compiler_params=params(2),
        cost_estimate=cost(HALF * E * E, MIB),
        name="row_sums",
    )(*near(*parts, order))


def prior_kernel(e_ref, u1, u2, u3, x_ref, _, *outs):
    y, z, _ = my_place()
    total = x_ref[...]
    for k, u in zip(YSTEPS, (u1, u2, u3)):
        total = total + jnp.where(k <= y, u[...], 0.0)
    for out, k in zip(outs, ZSTEPS):
        out[...] = total + e_ref[lax.rem(z + k, L)]


def prior_sums(inrow, others, start, order):
    return pl.pallas_call(
        prior_kernel,
        in_specs=[HERE] * (L + 2),
        out_specs=[HERE] * L,
        out_shape=[QUARTER] * L,
        compiler_params=params(2),
        cost_estimate=cost(HALF * E * E, MIB),
        name="prior_sums",
    )(*near(inrow, *others, start, order))


def later_kernel(e_ref, t_ref, u1, u2, u3, _, *refs):
    outs, (keep_ref, send_ref, buf) = refs[:L], refs[L:]
    y, z, core = my_place()
    total = jnp.zeros_like(t_ref)
    for k, u in zip(YSTEPS, (u1, u2, u3)):
        total = total + jnp.where(k > y, u[...], 0.0)
    for out, k in zip(outs, ZSTEPS):
        out[...] = total + e_ref[lax.rem(z + k, L)]
    buf[...] = (t_ref[...] + u1[...] + u2[...] + u3[...]).reshape(buf.shape)
    low = lax.broadcasted_iota(jnp.int32, (8, E), 0) < 4
    for j in range(0, HALF, 2):
        a = buf[y, 8 * j : 8 * j + 8]
        b = buf[y, 8 * j + 8 : 8 * j + 16]
        even = jnp.where(low, a, pltpu.roll(b, 4, 0))
        odd = jnp.where(low, pltpu.roll(a, 4, 0), b)
        keep_ref[4 * j : 4 * j + 8] = jnp.where(core == 0, even, odd)
        send_ref[4 * j : 4 * j + 8] = jnp.where(core == 0, odd, even)


def later_sums(inrow, total, others, order):
    return pl.pallas_call(
        later_kernel,
        in_specs=[HERE] * (L + 2),
        out_specs=[HERE] * (L + 2),
        out_shape=[QUARTER] * L + [pltpu.VMEM((HALF * L, E), f32)] * 2,
        scratch_shapes=[pltpu.VMEM((L, HALF * 8, E), f32)],
        compiler_params=params(2),
        cost_estimate=cost(HALF * E * E, MIB),
        name="later_sums",
    )(*near(inrow, total, *others, order))


def split_kernel(first, *refs):
    parts, (x_ref, _, own_ref, send_ref) = refs[:L], refs[L:]
    _, z, core = my_place()
    for part, k in zip(parts, ZSTEPS):
        at = lax.rem(z + L - k, L)
        scan = part[...]
        more = scan + x_ref[at]
        own_ref[at] = jnp.where(core == first, scan, more)
        send_ref[at] = jnp.where(core == first, more, scan)


def split(parts, extra, order, first):
    return pl.pallas_call(
        functools.partial(split_kernel, first),
        in_specs=[HERE] * (L + 2),
        out_specs=[HERE] * 2,
        out_shape=[QUARTERS] * 2,
        compiler_params=params(2),
        cost_estimate=cost(HALF * E * E, 2 * MIB),
        name="split",
    )(*near(*parts, extra, order))


def local_kernel(
    q_ref, g_ref, k_ref, v_ref, x_hbm, _, qh_ref, gh_ref, loc_ref, x_ref, mark_ref, acc, sem
):
    step = pl.program_id(0)
    at = rows(step)
    _, z, core = my_place()
    quarter = pltpu.make_async_copy(x_hbm.at[core * L + z], x_ref, sem)

    @pl.when(step == 0)
    def _():
        quarter.start()
        acc[...] = jnp.zeros_like(acc)
        mark_ref[...] = jnp.zeros_like(mark_ref)

    qh_ref[:, at] = heads_first(q_ref)
    gh_ref[:, at] = heads_first(g_ref)
    loc_ref[step] = acc[...].astype(bf16)

    @pl.when(step < NC - 1)
    def _():
        for h in range(HL):
            acc[h] += mm_tn(k_ref[h, at], v_ref[h, at])

    @pl.when(step == NC - 1)
    def _():
        quarter.wait()


def local_states(queries, out_grad, kh, vh, start, order):
    return pl.pallas_call(
        local_kernel,
        grid=(NC,),
        in_specs=[TOK] * 2 + [HERE] * 2 + [AWAY, HERE],
        out_specs=[HERE] * 5,
        out_shape=[MAJOR] * 2 + [STATES, QUARTER, MARK],
        scratch_shapes=[pltpu.VMEM((HL, E, E), f32), pltpu.SemaphoreType.DMA],
        compiler_params=params(12),
        cost_estimate=cost(2 * T * HL * E * E, 12 * MIB),
        name="local_states",
    )(*far(queries, out_grad), *near(kh, vh), *far(start), *near(order))


def inner_kernel(q_ref, k_ref, v_ref, loc_ref, _, att_ref, mark_ref, qk_ref):
    step = pl.program_id(0)
    at = rows(step)
    mask = causal()
    mark_ref[...] = jnp.zeros_like(mark_ref)
    for h in range(HL):
        qk_ref[h] = jnp.where(mask, mm_nt(q_ref[h, at], k_ref[h, at]), 0.0).astype(bf16)
    for h in range(HL):
        att = mm_lower(qk_ref[h], v_ref[h, at]) + mm(q_ref[h, at], loc_ref[step, h])
        att_ref[h, at] = att.astype(bf16)


def inner_part(qh, kh, vh, loc, order):
    return pl.pallas_call(
        inner_kernel,
        grid=(NC,),
        in_specs=[HERE] * 5,
        out_specs=[HERE] * 2,
        out_shape=[MAJOR, MARK],
        scratch_shapes=[pltpu.VMEM((HL, C, C), bf16)],
        compiler_params=params(8),
        cost_estimate=cost(2 * T * HL * (2 * C * E + E * E), 16 * MIB),
        name="inner_part",
    )(*near(qh, kh, vh, loc, order))


def square_kernel(q_ref, k_ref, _, kq_ref, mark_ref):
    at = rows(pl.program_id(0))
    mask = causal(later=True)
    mark_ref[...] = jnp.zeros_like(mark_ref)
    for h in range(HL):
        kq_ref[h, at] = jnp.where(mask, mm_nt(k_ref[h, at], q_ref[h, at]), 0.0).astype(bf16)


def square_part(qh, kh, order):
    return pl.pallas_call(
        square_kernel,
        grid=(NC,),
        in_specs=[HERE] * 3,
        out_specs=[HERE] * 2,
        out_shape=[SQUARES, MARK],
        compiler_params=params(4),
        cost_estimate=cost(2 * T * HL * C * E, 12 * MIB),
        name="square_part",
    )(*near(qh, kh, order))


def stats_half(first, h, state, refs, sq, pr, at):
    q_ref, g_ref, a_ref, gain_ref, att_ref = refs
    for j in range(HALF):
        att = a_ref[h + j, at].astype(f32) + mm(q_ref[h + j, at], state[j])
        att_ref[h + j, at] = att
        up = gain_ref[pl.ds(h + j, 1), :] * g_ref[h + j, at].astype(f32)
        sq = sq + att * att
        pr = pr + up * att
    return sq, pr


def stats_own_kernel(q_ref, g_ref, a_ref, own_ref, gain_ref, att_ref, sb_ref, sum_ref):
    step = pl.program_id(0)
    at = rows(step)
    mine, _ = my_heads()

    @pl.when(step == 0)
    def _():
        sb_ref[pl.ds(mine, HALF)] = own_ref[...].astype(bf16)

    state = [sb_ref[mine + j] for j in range(HALF)]
    zero = jnp.zeros((C, E), f32)
    refs = (q_ref, g_ref, a_ref, gain_ref, att_ref)
    sum_ref[0, at], sum_ref[1, at] = stats_half(0, mine, state, refs, zero, zero, at)


def stats_got_kernel(
    q_ref, g_ref, a_ref, got_ref, gain_ref, sum_ref, _, __, att_ref, sb_ref, o_ref
):
    step = pl.program_id(0)
    at = rows(step)
    _, other = my_heads()

    @pl.when(step == 0)
    def _():
        sb_ref[pl.ds(other, HALF)] = got_ref[...].astype(bf16)

    state = [sb_ref[other + j] for j in range(HALF)]
    refs = (q_ref, g_ref, a_ref, gain_ref, att_ref)
    sq, pr = stats_half(1, other, state, refs, sum_ref[0, at], sum_ref[1, at], at)
    o_ref[step, 0:1, :] = jnp.sum(sq.T, axis=0, keepdims=True)
    o_ref[step, 1:2, :] = jnp.sum(pr.T, axis=0, keepdims=True)


ATTENDED = pltpu.VMEM((HL, T, E), f32)
STATE = pltpu.VMEM((HL, E, E), bf16)


def stats_own(qh, gh, part, own, gain):
    return pl.pallas_call(
        stats_own_kernel,
        grid=(NC,),
        in_specs=[HERE] * 5,
        out_specs=[HERE] * 3,
        out_shape=[ATTENDED, STATE, pltpu.VMEM((2, T, E), f32)],
        compiler_params=params(6),
        cost_estimate=cost(T * HL * E * E, 5 * MIB),
        name="stats_own",
    )(*near(qh, gh, part, own, gain))


def stats_got(qh, gh, part, got, gain, sums, att, state):
    return pl.pallas_call(
        stats_got_kernel,
        grid=(NC,),
        in_specs=[HERE] * 8,
        out_specs=[HERE] * 3,
        out_shape=[ATTENDED, STATE, pltpu.VMEM((NC, 2, C), f32)],
        input_output_aliases={6: 0, 7: 1},
        compiler_params=params(6),
        cost_estimate=cost(T * HL * E * E, 5 * MIB),
        name="stats_got",
    )(*near(qh, gh, part, got, gain, sums, att, state))


def scales(sums, step):
    sums = (sums[0][step] + sums[1][step]) + (sums[2][step] + sums[3][step])
    rms = jnp.sqrt(sums[0:1, :] / WIDTH + epsilon)
    a = 1.0 / rms
    b = sums[1:2, :] / (WIDTH * rms * rms) * a
    a = jnp.broadcast_to(a, (E, C)).T
    b = jnp.broadcast_to(b, (E, C)).T
    return a, b


def pre_kernel(own, q_ref, g_ref, a_ref, gain_ref, s0, s1, s2, s3, *refs):
    p_ref, wl_ref, w_ref, acc = refs[-4:]
    step = pl.program_id(0)
    chunk = NC - 1 - step
    at = rows(chunk)
    first = my_heads()[0 if own else 1]

    @pl.when(step == 0)
    def _():
        acc[...] = jnp.zeros_like(acc)

    a, b = scales((s0, s1, s2, s3), chunk)
    wl_ref[chunk, pl.ds(first, HALF)] = acc[...].astype(bf16)
    for j in range(HALF):
        h = first + j
        up = gain_ref[pl.ds(h, 1), :] * g_ref[h, at].astype(f32)
        p = (up * a - a_ref[h, at] * b).astype(bf16)
        p_ref[h, at] = p
        acc[j] += mm_tn(q_ref[h, at], p)

    @pl.when(step == NC - 1)
    def _():
        for j in range(HALF):
            x = acc[j]
            for n in range(L * L):
                to = slice(64 * (n // L) + 8 * j, 64 * (n // L) + 8 * j + 8)
                w_ref[n % L, to, :] = x[8 * n : 8 * n + 8]


def pre_part(qh, gh, att, gain, sums, *half_done):
    own = len(half_done) > 0
    return pl.pallas_call(
        functools.partial(pre_kernel, own),
        grid=(NC,),
        in_specs=[HERE] * (8 + len(half_done)),
        out_specs=[HERE] * 3,
        out_shape=[MAJOR, STATES, QUARTERS],
        input_output_aliases={8: 0, 9: 1} if own else {},
        scratch_shapes=[pltpu.VMEM((HALF, E, E), f32)],
        compiler_params=params(6),
        cost_estimate=cost(T * HL * E * E, 8 * MIB),
        name="pre_own" if own else "pre_other",
    )(*near(qh, gh, att, gain, *sums, *half_done))


def query_kernel(k_ref, v_ref, p_ref, s_ref, loc_ref, _, qg_ref, mark_ref, gv_ref, sum_ref):
    step = pl.program_id(0)
    at = rows(step)
    mask = causal()
    mark_ref[...] = jnp.zeros_like(mark_ref)
    for h in range(HL):
        gv_ref[h] = jnp.where(mask, mm_nt(p_ref[h, at], v_ref[h, at]), 0.0).astype(bf16)
    for h in range(HL):
        p = p_ref[h, at]
        sum_ref[h] = mm_nt(
            jnp.concatenate([p, p], axis=1),
            jnp.concatenate([s_ref[h], loc_ref[step, h]], axis=1),
        )
    for h in range(HL):
        qg_ref[h, at] = (sum_ref[h] + mm_lower(gv_ref[h], k_ref[h, at])).astype(bf16)


def query_part(kh, vh, pre, state, loc, order):
    return pl.pallas_call(
        query_kernel,
        grid=(NC,),
        in_specs=[HERE] * 6,
        out_specs=[HERE] * 2,
        out_shape=[MAJOR, MARK],
        scratch_shapes=[pltpu.VMEM((HL, C, C), bf16), pltpu.VMEM((HL, C, E), f32)],
        compiler_params=params(8),
        cost_estimate=cost(2 * T * HL * (2 * C * E + 2 * E * E), 16 * MIB),
        name="query_part",
    )(*near(kh, vh, pre, state, loc, order))


def key_kernel(q_ref, v_ref, p_ref, wl_ref, _, kg_ref, mark_ref, vp_ref, sum_ref):
    step = pl.program_id(0)
    at = rows(step)
    mask = causal(later=True)
    mark_ref[...] = jnp.zeros_like(mark_ref)
    for h in range(HL):
        vp_ref[h] = jnp.where(mask, mm_nt(v_ref[h, at], p_ref[h, at]), 0.0).astype(bf16)
    for h in range(HL):
        sum_ref[h] = mm_nt(v_ref[h, at], wl_ref[step, h])
    for h in range(HL):
        kg_ref[h, at] = (sum_ref[h] + mm_upper(vp_ref[h], q_ref[h, at])).astype(bf16)


def key_part(qh, vh, pre, wloc, order):
    return pl.pallas_call(
        key_kernel,
        grid=(NC,),
        in_specs=[HERE] * 5,
        out_specs=[HERE] * 2,
        out_shape=[MAJOR, MARK],
        scratch_shapes=[pltpu.VMEM((HL, C, C), bf16), pltpu.VMEM((HL, C, E), f32)],
        compiler_params=params(8),
        cost_estimate=cost(2 * T * HL * (2 * C * E + E * E), 16 * MIB),
        name="key_part",
    )(*near(qh, vh, pre, wloc, order))


def value_kernel(
    k_ref, p_ref, kq_ref, wl_ref, a_ref, qh_ref, gain_ref, s0, s1, s2, s3, _, n_ref, qg_ref, vg_ref, mark_ref
):
    step = pl.program_id(0)
    at = rows(step)
    mark_ref[...] = jnp.zeros_like(mark_ref)
    a, _ = scales((s0, s1, s2, s3), step)
    normed = [(gain_ref[h : h + 1, :] * a_ref[h, at] * a).astype(bf16) for h in range(HL)]
    n_ref[...] = jnp.swapaxes(jnp.stack(normed), 0, 1)
    qg_ref[...] = jnp.swapaxes(qh_ref[:, at], 0, 1)
    for h in range(HL):
        part = mm_upper(kq_ref[h, at], p_ref[h, at]) + mm(k_ref[h, at], wl_ref[step, h])
        vg_ref[h, at] = part.astype(bf16)


def value_part(kh, pre, kq, wloc, att, grad, gain, sums, order):
    return pl.pallas_call(
        value_kernel,
        grid=(NC,),
        in_specs=[HERE] * 12,
        out_specs=[TOK, TOK, HERE, HERE],
        out_shape=[TOKENS, TOKENS, MAJOR, MARK],
        compiler_params=params(14),
        cost_estimate=cost(2 * T * HL * (C * E + E * E), 20 * MIB),
        name="value_part",
    )(*near(kh, pre, kq, wloc, att, grad, gain, *sums, order))


def final_half(first, l_ref, k_ref, v_ref, kg_ref, vg_ref, at):
    for j in range(HALF):
        h = first + j
        kg_ref[h, at] = (kg_ref[h, at].astype(f32) + mm_nt(v_ref[h, at], l_ref[j])).astype(bf16)
    for j in range(HALF):
        h = first + j
        vg_ref[h, at] = (vg_ref[h, at].astype(f32) + mm(k_ref[h, at], l_ref[j])).astype(bf16)


def in_order(l_ref, x_ref):
    for j in range(HALF):
        parts = []
        for n in range(L * L):
            first = 64 * (n // L) + 8 * j
            parts.append(x_ref[n % L, first : first + 8, :])
        l_ref[j] = jnp.concatenate(parts, axis=0).astype(bf16)


def final_own_kernel(k_ref, v_ref, own_ref, _, __, kg_ref, vg_ref, l_ref):
    step = pl.program_id(0)

    @pl.when(step == 0)
    def _():
        in_order(l_ref, own_ref)

    final_half(my_heads()[0], l_ref, k_ref, v_ref, kg_ref, vg_ref, rows(step))


def final_own(kh, vh, own, kpart, vpart):
    return pl.pallas_call(
        final_own_kernel,
        grid=(NC,),
        in_specs=[HERE] * 5,
        out_specs=[HERE] * 2,
        out_shape=[MAJOR] * 2,
        input_output_aliases={3: 0, 4: 1},
        scratch_shapes=[pltpu.VMEM((HALF, E, E), bf16)],
        compiler_params=params(4),
        cost_estimate=cost(2 * T * HL * E * E, 8 * MIB),
        name="final_own",
    )(*near(kh, vh, own, kpart, vpart))


def final_got_kernel(
    k_ref, v_ref, got_ref, kp_ref, vp_ref, mine_ref, theirs_ref, kg_ref, vg_ref, e_ref, l_ref
):
    step = pl.program_id(0)
    at = rows(step)
    mine, other = my_heads()

    @pl.when(step == 0)
    def _():
        in_order(l_ref, got_ref)
        e_ref[pl.ds(pl.multiple_of(mine * L, 8), HALF * L)] = mine_ref[...]
        e_ref[pl.ds(pl.multiple_of(other * L, 8), HALF * L)] = theirs_ref[...]

    final_half(other, l_ref, k_ref, v_ref, kp_ref, vp_ref, at)
    kg_ref[...] = jnp.swapaxes(kp_ref[:, at], 0, 1)
    vg_ref[...] = jnp.swapaxes(vp_ref[:, at], 0, 1)


def final_got(kh, vh, got, kpart, vpart, mine, theirs):
    return pl.pallas_call(
        final_got_kernel,
        grid=(NC,),
        in_specs=[HERE] * 7,
        out_specs=[TOK] * 2 + [HERE],
        out_shape=[TOKENS] * 2 + [jax.ShapeDtypeStruct((HL * L, E), f32)],
        scratch_shapes=[pltpu.VMEM((HALF, E, E), bf16)],
        compiler_params=params(14),
        cost_estimate=cost(2 * T * HL * E * E, 15 * MIB),
        name="final_got",
    )(*near(kh, vh, got, kpart, vpart, mine, theirs))


def along(x, move):
    def seq(y, z, core):
        return (y * L + z) * 2 + core

    places = [(y, z, core) for y in range(L) for z in range(L) for core in range(2)]
    return lax.ppermute(x, "seq", [(seq(*p), seq(*move(*p))) for p in places])


def across_cores(x):
    return along(x, lambda y, z, core: (y, z, 1 - core))


def across_z(parts):
    return list(parts[:1]) + [
        along(x, lambda y, z, core: (y, (z + k) % L, core)) for x, k in zip(parts[1:], ZSTEPS[1:])
    ]


def across_y(x):
    return [along(x, lambda y, z, core: ((y + k) % L, z, core)) for k in YSTEPS]


def across_heads(x):
    return [x] + [lax.ppermute(x, "head", [(i, (i + k) % X) for i in range(X)]) for k in range(1, X)]


def body(queries, keys, values, out_grad, gain, entry_state):
    rows_of = HALF * E // L
    start = entry_state.reshape(2 * L, rows_of, E)
    kh, vh, other = kv_other(keys, values)
    got = across_cores(other.reshape(L, rows_of, E))
    *parts, extra = pair(kv_mine(kh, vh).reshape(L, rows_of, E), got, 0)
    near_row = across_z(parts)
    qh, gh, loc, start, mark = local_states(queries, out_grad, kh, vh, start, parts[0])
    inrow, total = row_sums(near_row, mark, False)
    others = across_y(total)
    part, mark = inner_part(qh, kh, vh, loc, total)
    parts = prior_sums(inrow, others, start, mark)
    scan = across_z(parts)
    kq, mark = square_part(qh, kh, parts[0])
    own, other = split(scan, extra, mark, 0)
    got = across_cores(other)
    att, state, sums = stats_own(qh, gh, part, own.reshape(HALF, E, E), gain)
    got = got.reshape(HALF, E, E)
    att, state, sums = stats_got(qh, gh, part, got, gain, sums, att, state)
    sums = across_heads(sums)
    pre, wloc, other = pre_part(qh, gh, att, gain, sums)
    got = across_cores(other)
    pre, wloc, mine = pre_part(qh, gh, att, gain, sums, pre, wloc)
    *parts, extra = pair(mine, got, 1)
    near_row = across_z(parts)
    grad, mark = query_part(kh, vh, pre, state, loc, parts[0])
    inrow, total = row_sums(near_row, mark, True)
    others = across_y(total)
    kpart, mark = key_part(qh, vh, pre, wloc, total)
    *parts, mine, theirs = later_sums(inrow, total, others, mark)
    scan = across_z(parts)
    theirs = across_cores(theirs)
    normed, query_grad, vpart, mark = value_part(
        kh, pre, kq, wloc, att, grad, gain, sums, parts[0]
    )
    own, other = split(scan, extra, mark, 1)
    got = across_cores(other)
    kpart, vpart = final_own(kh, vh, own, kpart, vpart)
    key_grad, value_grad, entry_grad = final_got(kh, vh, got, kpart, vpart, mine, theirs)
    return normed, query_grad, key_grad, value_grad, entry_grad.reshape(HL, L, E)


def solution(mesh):
    tok = P("seq", "head", None)
    return jax.shard_map(
        body,
        mesh=mesh,
        in_specs=(tok, tok, tok, tok, P("head", None), P("head", None, None)),
        out_specs=(tok, tok, tok, tok, P("head", "seq", None)),
        check_vma=False,
    )
```

time: 104 us -> 93.2 us (0.90)
  waiting for transfers between devices: 20.7 us -> 6.74 us
  starting transfers between devices: 28.8 us -> 41.1 us
  blocking collectives: 8.06 us -> 0 us
  local copies, waits for them, and re-layouts: 2.32 us -> 0.01 us
  Pallas kernels: 42.7 us -> 44.4 us
    ppermute x22 -> x23, waiting for transfers between devices: 20.7 us -> 3.66 us  [along(): return lax.ppermute(x, 'seq', [(seq(*p), seq(*move(*p))) for p in places])]
    ppermute x22 -> x23, starting transfers between devices: 28.8 us -> 37.4 us  [along(): return lax.ppermute(x, 'seq', [(seq(*p), seq(*move(*p))) for p in places])]
    all_to_all x1 -> x0, blocking collectives: 8.06 us -> none  [body(): sums = lax.all_to_all(sums, 'head', 0, 0, tiled=True)]
    ppermute x0 -> x3, starting transfers between devices: none -> 3.68 us  [across_heads(): lax.ppermute(x, 'head', [(i, (i + k) % X) for i in range(X)])]
    ppermute x0 -> x3, waiting for transfers between devices: none -> 3.08 us  [across_heads(): lax.ppermute(x, 'head', [(i, (i + k) % X) for i in range(X)])]
    unnamed x16 -> x2, local copies, waits for them, and re-layouts: 2.23 us -> 0.01 us
    pallas_call x10 -> x16, Pallas kernels: 42.1 us -> 43.8 us  [the longest x1 5.22 us: query_part(): pl.pallas_call(query_kernel, grid=(NC,), in_specs=[HERE] * 6, out_specs=[...]
  transfers between devices with their start and end apart: 22 -> 26, of which waited for: 11 -> 10; matrix products, arithmetic and copies ran while one was open for 0% -> 0% of each run, Pallas kernels for 26% -> 33%
where the time goes in v4:
time: 93.2 us; the launch traced here: 93.1 us
  Pallas kernels  44.4 us (48%)
  starting transfers between devices  41.1 us (44%)
  waiting for transfers between devices  6.74 us (7%)
    ppermute x23, starting transfers between devices, along(): return lax.ppermute(x, 'seq', [(seq(*p), seq(*move(*p))) for p in places])  37.4 us
    pallas_call x1, Pallas kernels, query_part(): pl.pallas_call(query_kernel, grid=(NC,), in_specs=[HERE] * 6, out_specs=[...  5.22 us
    pallas_call x1, Pallas kernels, value_part(): pl.pallas_call(value_kernel, grid=(NC,), in_specs=[HERE] * 12, out_specs=...  5.1 us
    pallas_call x1, Pallas kernels, local_states(): pl.pallas_call(local_kernel, grid=(NC,), in_specs=[TOK] * 2 + [HERE] * 2...  4.95 us
    pallas_call x1, Pallas kernels, kv_other(): pl.pallas_call(kv_other_kernel, in_specs=[AWAY, AWAY], out_specs=[HERE] *...  4.8 us
    pallas_call x1, Pallas kernels, inner_part(): pl.pallas_call(inner_kernel, grid=(NC,), in_specs=[HERE] * 5, out_specs=[...  4.36 us
    pallas_call x1, Pallas kernels, final_got(): pl.pallas_call(final_got_kernel, grid=(NC,), in_specs=[HERE] * 7, out_spe...  4.35 us
    pallas_call x1, Pallas kernels, key_part(): pl.pallas_call(key_kernel, grid=(NC,), in_specs=[HERE] * 5, out_specs=[HE...  4.33 us
  transfers between devices with their start and end apart: 26, of which 10 were waited for; matrix products, arithmetic and copies ran while one was open for 0% of the time, Pallas kernels for 33%

profile of v4, /device:TPU:1, one launch (start us, length us, event | category | flops | bytes accessed | tf_op | source)
XLA Modules:
  0.0 93.1 jit_solution(11719181046181232202)
XLA Ops:
  0.6 4.8 %kv_other.1 = (bf16[16,768,128]{2,1,0:T(8,128)(2,1)S(1)}, bf16[16,768,128]{2,1,0:T(8,128)(2,1)S(1)}, f32[8,128,128]{2,1,0:T(8,128)S(1)}) custom-call(bf16[768,16,128]{2,1,0:T(8,128)(2,1)} %k_hbm.1, bf16[768,16,128]{2,1,0:T(8,128)(2,1)} %v_hbm.1), custom_call_target="tpu_custom_call" | custom-call | flops 201326592 | bytes 7340032 | tf_op jit(solution)/shard_map/kv_other/pallas_call | solution.py:127
  5.4 1.6 %collective-permute-start = (f32[4,256,128]{2,1,0:T(8,128)S(1)}, f32[4,256,128]{2,1,0:T(8,128)S(1)}, u32[]{:S(2)}, u32[]{:S(2)}) collective-permute-start(f32[4,256,128]{2,1,0:T(8,128)S(1)} %bitcast.9), channel_id=1, source_target_pairs={{0,4},{4,0},{8,12},{12,8},{16,20},{20,16},{24,28},{28,24},{32,36},... | collective-permute-start | bytes 1572872 | tf_op jit(solution)/shard_map/ppermute | solution.py:667
  8.7 3.8 %collective-permute-start.1 = (f32[256,128]{1,0:T(8,128)S(1)}, f32[256,128]{1,0:T(8,128)S(1)}, u32[]{:S(2)}, u32[]{:S(2)}) collective-permute-start(f32[256,128]{1,0:T(8,128)S(1)} %get-tuple-element.77), channel_id=1, source_target_pairs={{0,16},{4,20},{8,24},{12,28},{16,0},{20,4},{24,8},{28,12},{32,48},... | collective-permute-start | bytes 393224 | tf_op jit(solution)/shard_map/ppermute | solution.py:667
  13.2 1.9 %collective-permute-start.3 = (f32[256,128]{1,0:T(8,128)S(1)}, f32[256,128]{1,0:T(8,128)S(1)}, u32[]{:S(2)}, u32[]{:S(2)}) collective-permute-start(f32[256,128]{1,0:T(8,128)S(1)} %get-tuple-element.79), channel_id=1, source_target_pairs={{0,24},{4,28},{8,0},{12,4},{16,8},{20,12},{24,16},{28,20},{32,56},... | collective-permute-start | bytes 393224 | tf_op jit(solution)/shard_map/ppermute | solution.py:667
  15.2 5.0 %local_states.1 = (bf16[16,768,128]{2,1,0:T(8,128)(2,1)S(1)}, bf16[16,768,128]{2,1,0:T(8,128)(2,1)S(1)}, bf16[3,16,128,128]{3,2,1,0:T(8,128)(2,1)S(1)}, f32[256,128]{1,0:T(8,128)S(1)}, f32[8,128]{1,0:T(8,128)S(1)}) custom-call(bf16[768,16,128]{2,1,0:T(8,128)(2,1)} %q_ref.1, bf16[768,16,128]{2,1,0:T(8,128)(2,1)} %g_ref.1, ...), custom_call_target="tpu_custom_call" | custom-call | flops 402653184 | bytes 12582912 | tf_op jit(solution)/shard_map/local_states/pallas_call | solution.py:311
  20.3 3.0 %collective-permute-start.6 = (f32[256,128]{1,0:T(8,128)S(1)}, f32[256,128]{1,0:T(8,128)S(1)}, u32[]{:S(2)}, u32[]{:S(2)}) collective-permute-start(f32[256,128]{1,0:T(8,128)S(1)} %get-tuple-element.81._), channel_id=1, source_target_pairs={{0,64},{4,68},{8,72},{12,76},{16,80},{20,84},{24,88},{28,92},{32,9... | collective-permute-start | bytes 393224 | tf_op jit(solution)/shard_map/ppermute | solution.py:667
  24.7 4.4 %inner_part.1 = (bf16[16,768,128]{2,1,0:T(8,128)(2,1)S(1)}, f32[8,128]{1,0:T(8,128)S(1)}) custom-call(bf16[16,768,128]{2,1,0:T(8,128)(2,1)S(1)} %get-tuple-element.74.q_ref, bf16[16,768,128]{2,1,0:T(8,128)(2,1)S(1)} %get-tuple-element.70.k_ref, bf16[16,768,128]{2,1,0:T(8,128)(2,1)S(1)} %get-tuple-element.71.v_ref, ...), custom_call_target="tpu_custom_call" | custom-call | flops 2013265920 | bytes 16777216 | tf_op jit(solution)/shard_map/inner_part/pallas_call | solution.py:337
  29.5 1.0 %collective-permute-start.7 = (f32[256,128]{1,0:T(8,128)S(1)}, f32[256,128]{1,0:T(8,128)S(1)}, u32[]{:S(2)}, u32[]{:S(2)}) collective-permute-start(f32[256,128]{1,0:T(8,128)S(1)} %get-tuple-element.87), channel_id=1, source_target_pairs={{0,16},{4,20},{8,24},{12,28},{16,0},{20,4},{24,8},{28,12},{32,48},... | collective-permute-start | bytes 393224 | tf_op jit(solution)/shard_map/ppermute | solution.py:667
  30.5 1.3 %collective-permute-start.8 = (f32[256,128]{1,0:T(8,128)S(1)}, f32[256,128]{1,0:T(8,128)S(1)}, u32[]{:S(2)}, u32[]{:S(2)}) collective-permute-start(f32[256,128]{1,0:T(8,128)S(1)} %get-tuple-element.88), channel_id=1, source_target_pairs={{0,8},{4,12},{8,16},{12,20},{16,24},{20,28},{24,0},{28,4},{32,40},... | collective-permute-start | bytes 393224 | tf_op jit(solution)/shard_map/ppermute | solution.py:667
  31.8 1.4 %collective-permute-start.9 = (f32[256,128]{1,0:T(8,128)S(1)}, f32[256,128]{1,0:T(8,128)S(1)}, u32[]{:S(2)}, u32[]{:S(2)}) collective-permute-start(f32[256,128]{1,0:T(8,128)S(1)} %get-tuple-element.89), channel_id=1, source_target_pairs={{0,24},{4,28},{8,0},{12,4},{16,8},{20,12},{24,16},{28,20},{32,56},... | collective-permute-start | bytes 393224 | tf_op jit(solution)/shard_map/ppermute | solution.py:667
  33.2 2.2 %square_part.1 = (bf16[16,768,256]{2,1,0:T(8,128)(2,1)S(1)}, f32[8,128]{1,0:T(8,128)S(1)}) custom-call(bf16[16,768,128]{2,1,0:T(8,128)(2,1)S(1)} %get-tuple-element.74.q_ref, bf16[16,768,128]{2,1,0:T(8,128)(2,1)S(1)} %get-tuple-element.70.k_ref, f32[256,128]{1,0:T(8,128)S(1)} %get-tuple-element.86._.refs_0_), custom_call_target="tpu_custom_call" | custom-call | flops 805306368 | bytes 12582912 | tf_op jit(solution)/shard_map/square_part/pallas_call | solution.py:359
  36.4 4.0 %collective-permute-start.10 = (f32[4,256,128]{2,1,0:T(8,128)S(1)}, f32[4,256,128]{2,1,0:T(8,128)S(1)}, u32[]{:S(2)}, u32[]{:S(2)}) collective-permute-start(f32[4,256,128]{2,1,0:T(8,128)S(1)} %get-tuple-element.92), channel_id=1, source_target_pairs={{0,4},{4,0},{8,12},{12,8},{16,20},{20,16},{24,28},{28,24},{32,36},... | collective-permute-start | bytes 1572872 | tf_op jit(solution)/shard_map/ppermute | solution.py:667
  40.4 1.3 %stats_own.1 = (f32[16,768,128]{2,1,0:T(8,128)S(1)}, bf16[16,128,128]{2,1,0:T(8,128)(2,1)S(1)}, f32[2,768,128]{2,1,0:T(8,128)S(1)}) custom-call(bf16[16,768,128]{2,1,0:T(8,128)(2,1)S(1)} %get-tuple-element.74.q_ref, bf16[16,768,128]{2,1,0:T(8,128)(2,1)S(1)} %get-tuple-element.75.g_ref, bf16[16,768,128]{2,1,0:T(8,128)(2,1)S(1)} %get-tuple-element.82.a_ref, ...), custom_call_target="tpu_custom_call" | custom-call | flops 201326592 | bytes 5242880 | tf_op jit(solution)/shard_map/stats_own/pallas_call | solution.py:420
  41.9 1.7 %stats_got.1 = (f32[16,768,128]{2,1,0:T(8,128)S(1)}, bf16[16,128,128]{2,1,0:T(8,128)(2,1)S(1)}, f32[3,2,256]{2,1,0:T(2,128)S(1)}) custom-call(bf16[16,768,128]{2,1,0:T(8,128)(2,1)S(1)} %get-tuple-element.74.q_ref, bf16[16,768,128]{2,1,0:T(8,128)(2,1)S(1)} %get-tuple-element.75.g_ref, ...), custom_call_target="tpu_custom_call", output_to_operand_aliasing={{0}: (6, {}), {1}: (7, {})} | custom-call | flops 201326592 | bytes 5242880 | tf_op jit(solution)/shard_map/stats_got/pallas_call | solution.py:433
  43.6 2.5 %collective-permute-start.13 = (f32[3,2,256]{2,1,0:T(2,128)S(1)}, f32[3,2,256]{2,1,0:T(2,128)S(1)}, u32[]{:S(2)}, u32[]{:S(2)}) collective-permute-start(f32[3,2,256]{2,1,0:T(2,128)S(1)} %get-tuple-element.98.s0), channel_id=1, source_target_pairs={{0,3},{1,0},{2,1},{3,2},{4,7},{5,4},{6,5},{7,6},{8,11},{9,8},{10,9... | collective-permute-start | bytes 18440 | tf_op jit(solution)/shard_map/ppermute | solution.py:685
  47.3 2.9 %collective-permute-done.12.s2 = f32[3,2,256]{2,1,0:T(2,128)S(1)} collective-permute-done((f32[3,2,256]{2,1,0:T(2,128)S(1)}, f32[3,2,256]{2,1,0:T(2,128)S(1)}, u32[]{:S(2)}, u32[]{:S(2)}) %collective-permute-start.12) | collective-permute-done | bytes 6176 | tf_op jit(solution)/shard_map/ppermute | solution.py:685
  50.4 1.7 %pre_other.1 = (bf16[16,768,128]{2,1,0:T(8,128)(2,1)S(1)}, bf16[3,16,128,128]{3,2,1,0:T(8,128)(2,1)S(1)}, f32[4,256,128]{2,1,0:T(8,128)S(1)}) custom-call(bf16[16,768,128]{2,1,0:T(8,128)(2,1)S(1)} %get-tuple-element.74.q_ref, bf16[16,768,128]{2,1,0:T(8,128)(2,1)S(1)} %get-tuple-element.75.g_ref, f32[16,768,128]{2,1,0:T(8,128)S(1)} %get-tuple-element.97.a_ref, ...), custom_call_target="tpu_custom_call" | custom-call | flops 201326592 | bytes 8388608 | tf_op jit(solution)/shard_map/pre_other/pallas_call | solution.py:487
  52.1 2.2 %collective-permute-start.14 = (f32[4,256,128]{2,1,0:T(8,128)S(1)}, f32[4,256,128]{2,1,0:T(8,128)S(1)}, u32[]{:S(2)}, u32[]{:S(2)}) collective-permute-start(f32[4,256,128]{2,1,0:T(8,128)S(1)} %get-tuple-element.106), channel_id=1, source_target_pairs={{0,4},{4,0},{8,12},{12,8},{16,20},{20,16},{24,28},{28,24},{32,36},... | collective-permute-start | bytes 1572872 | tf_op jit(solution)/shard_map/ppermute | solution.py:667
  54.2 1.7 %pre_own.1 = (bf16[16,768,128]{2,1,0:T(8,128)(2,1)S(1)}, bf16[3,16,128,128]{3,2,1,0:T(8,128)(2,1)S(1)}, f32[4,256,128]{2,1,0:T(8,128)S(1)}) custom-call(bf16[16,768,128]{2,1,0:T(8,128)(2,1)S(1)} %get-tuple-element.74.q_ref, bf16[16,768,128]{2,1,0:T(8,128)(2,1)S(1)} %get-tuple-element.75.g_ref, ...), custom_call_target="tpu_custom_call", output_to_operand_aliasing={{0}: (8, {}), {1}: (9, {})} | custom-call | flops 201326592 | bytes 8388608 | tf_op jit(solution)/shard_map/pre_own/pallas_call | solution.py:487
  56.0 1.2 %collective-permute-start.15 = (f32[256,128]{1,0:T(8,128)S(1)}, f32[256,128]{1,0:T(8,128)S(1)}, u32[]{:S(2)}, u32[]{:S(2)}) collective-permute-start(f32[256,128]{1,0:T(8,128)S(1)} %get-tuple-element.109), channel_id=1, source_target_pairs={{0,16},{4,20},{8,24},{12,28},{16,0},{20,4},{24,8},{28,12},{32,48},... | collective-permute-start | bytes 393224 | tf_op jit(solution)/shard_map/ppermute | solution.py:667
  57.2 1.9 %collective-permute-start.16 = (f32[256,128]{1,0:T(8,128)S(1)}, f32[256,128]{1,0:T(8,128)S(1)}, u32[]{:S(2)}, u32[]{:S(2)}) collective-permute-start(f32[256,128]{1,0:T(8,128)S(1)} %get-tuple-element.110), channel_id=1, source_target_pairs={{0,8},{4,12},{8,16},{12,20},{16,24},{20,28},{24,0},{28,4},{32,40},... | collective-permute-start | bytes 393224 | tf_op jit(solution)/shard_map/ppermute | solution.py:667
  59.9 5.2 %query_part.1 = (bf16[16,768,128]{2,1,0:T(8,128)(2,1)S(1)}, f32[8,128]{1,0:T(8,128)S(1)}) custom-call(bf16[16,768,128]{2,1,0:T(8,128)(2,1)S(1)} %get-tuple-element.70.k_ref, bf16[16,768,128]{2,1,0:T(8,128)(2,1)S(1)} %get-tuple-element.71.v_ref, bf16[16,768,128]{2,1,0:T(8,128)(2,1)S(1)} %get-tuple-element.101.p_ref, ...), custom_call_target="tpu_custom_call" | custom-call | flops 2415919104 | bytes 16777216 | tf_op jit(solution)/shard_map/query_part/pallas_call | solution.py:519
  66.0 2.6 %collective-permute-start.20 = (f32[256,128]{1,0:T(8,128)S(1)}, f32[256,128]{1,0:T(8,128)S(1)}, u32[]{:S(2)}, u32[]{:S(2)}) collective-permute-start(f32[256,128]{1,0:T(8,128)S(1)} %get-tuple-element.114._.t_ref), channel_id=1, source_target_pairs={{0,64},{4,68},{8,72},{12,76},{16,80},{20,84},{24,88},{28,92},{32,9... | collective-permute-start | bytes 393224 | tf_op jit(solution)/shard_map/ppermute | solution.py:667
  68.5 1.0 %collective-permute-start.19 = (f32[256,128]{1,0:T(8,128)S(1)}, f32[256,128]{1,0:T(8,128)S(1)}, u32[]{:S(2)}, u32[]{:S(2)}) collective-permute-start(f32[256,128]{1,0:T(8,128)S(1)} %get-tuple-element.114._.t_ref), channel_id=1, source_target_pairs={{0,96},{4,100},{8,104},{12,108},{16,112},{20,116},{24,120},{28,124... | collective-permute-start | bytes 393224 | tf_op jit(solution)/shard_map/ppermute | solution.py:667
  70.0 4.3 %key_part.1 = (bf16[16,768,128]{2,1,0:T(8,128)(2,1)S(1)}, f32[8,128]{1,0:T(8,128)S(1)}) custom-call(bf16[16,768,128]{2,1,0:T(8,128)(2,1)S(1)} %get-tuple-element.74.q_ref, bf16[16,768,128]{2,1,0:T(8,128)(2,1)S(1)} %get-tuple-element.71.v_ref, bf16[16,768,128]{2,1,0:T(8,128)(2,1)S(1)} %get-tuple-element.101.p_ref, ...), custom_call_target="tpu_custom_call" | custom-call | flops 2013265920 | bytes 16777216 | tf_op jit(solution)/shard_map/key_part/pallas_call | solution.py:546
  74.9 1.7 %collective-permute-start.21 = (f32[256,128]{1,0:T(8,128)S(1)}, f32[256,128]{1,0:T(8,128)S(1)}, u32[]{:S(2)}, u32[]{:S(2)}) collective-permute-start(f32[256,128]{1,0:T(8,128)S(1)} %get-tuple-element.119), channel_id=1, source_target_pairs={{0,16},{4,20},{8,24},{12,28},{16,0},{20,4},{24,8},{28,12},{32,48},... | collective-permute-start | bytes 393224 | tf_op jit(solution)/shard_map/ppermute | solution.py:667
  76.7 1.5 %collective-permute-start.22 = (f32[256,128]{1,0:T(8,128)S(1)}, f32[256,128]{1,0:T(8,128)S(1)}, u32[]{:S(2)}, u32[]{:S(2)}) collective-permute-start(f32[256,128]{1,0:T(8,128)S(1)} %get-tuple-element.120), channel_id=1, source_target_pairs={{0,8},{4,12},{8,16},{12,20},{16,24},{20,28},{24,0},{28,4},{32,40},... | collective-permute-start | bytes 393224 | tf_op jit(solution)/shard_map/ppermute | solution.py:667
  78.2 1.2 %collective-permute-start.23 = (f32[256,128]{1,0:T(8,128)S(1)}, f32[256,128]{1,0:T(8,128)S(1)}, u32[]{:S(2)}, u32[]{:S(2)}) collective-permute-start(f32[256,128]{1,0:T(8,128)S(1)} %get-tuple-element.121), channel_id=1, source_target_pairs={{0,24},{4,28},{8,0},{12,4},{16,8},{20,12},{24,16},{28,20},{32,56},... | collective-permute-start | bytes 393224 | tf_op jit(solution)/shard_map/ppermute | solution.py:667
  79.3 5.1 %value_part.1 = (bf16[768,16,128]{2,1,0:T(8,128)(2,1)}, bf16[768,16,128]{2,1,0:T(8,128)(2,1)}, bf16[16,768,128]{2,1,0:T(8,128)(2,1)S(1)}, f32[8,128]{1,0:T(8,128)S(1)}) custom-call(bf16[16,768,128]{2,1,0:T(8,128)(2,1)S(1)} %get-tuple-element.70.k_ref, bf16[16,768,128]{2,1,0:T(8,128)(2,1)S(1)} %get-tuple-element.101.p_ref, ...), custom_call_target="tpu_custom_call" | custom-call | flops 1207959552 | bytes 20971520 | tf_op jit(solution)/shard_map/value_part/pallas_call | solution.py:575
  84.6 2.6 %collective-permute-start.24 = (f32[4,256,128]{2,1,0:T(8,128)S(1)}, f32[4,256,128]{2,1,0:T(8,128)S(1)}, u32[]{:S(2)}, u32[]{:S(2)}) collective-permute-start(f32[4,256,128]{2,1,0:T(8,128)S(1)} %get-tuple-element.124), channel_id=1, source_target_pairs={{0,4},{4,0},{8,12},{12,8},{16,20},{20,16},{24,28},{28,24},{32,36},... | collective-permute-start | bytes 1572872 | tf_op jit(solution)/shard_map/ppermute | solution.py:667
  87.3 1.4 %final_own.1 = (bf16[16,768,128]{2,1,0:T(8,128)(2,1)S(1)}, bf16[16,768,128]{2,1,0:T(8,128)(2,1)S(1)}) custom-call(bf16[16,768,128]{2,1,0:T(8,128)(2,1)S(1)} %get-tuple-element.70.k_ref, bf16[16,768,128]{2,1,0:T(8,128)(2,1)S(1)} %get-tuple-element.71.v_ref, ...), custom_call_target="tpu_custom_call", output_to_operand_aliasing={{0}: (3, {}), {1}: (4, {})} | custom-call | flops 402653184 | bytes 8388608 | tf_op jit(solution)/shard_map/final_own/pallas_call | solution.py:616
  88.8 4.3 %final_got.1 = (bf16[768,16,128]{2,1,0:T(8,128)(2,1)}, bf16[768,16,128]{2,1,0:T(8,128)(2,1)}, f32[64,128]{1,0:T(8,128)}) custom-call(bf16[16,768,128]{2,1,0:T(8,128)(2,1)S(1)} %get-tuple-element.70.k_ref, bf16[16,768,128]{2,1,0:T(8,128)(2,1)S(1)} %get-tuple-element.71.v_ref, f32[4,256,128]{2,1,0:T(8,128)S(1)} %collective-permute-done.24.got_ref, ...), custom_call_target="tpu_custom_call" | custom-call | flops 402653184 | bytes 15728640 | tf_op jit(solution)/shard_map/final_got/pallas_call | solution.py:649
  (44 shorter events, 10.0 us)
Async XLA Ops:
  5.4 3.2 %collective-permute-start = (f32[4,256,128]{2,1,0:T(8,128)S(1)}, f32[4,256,128]{2,1,0:T(8,128)S(1)}, u32[]{:S(2)}, u32[]{:S(2)}) collective-permute-start(f32[4,256,128]{2,1,0:T(8,128)S(1)} %bitcast.9), channel_id=1, source_target_pairs={{0,4},{4,0},{8,12},{12,8},{16,20},{20,16},{24,28},{28,24},{32,36},... | collective-permute-start | bytes 1572872 | tf_op jit(solution)/shard_map/ppermute | solution.py:667
  8.7 11.4 %collective-permute-start.1 = (f32[256,128]{1,0:T(8,128)S(1)}, f32[256,128]{1,0:T(8,128)S(1)}, u32[]{:S(2)}, u32[]{:S(2)}) collective-permute-start(f32[256,128]{1,0:T(8,128)S(1)} %get-tuple-element.77), channel_id=1, source_target_pairs={{0,16},{4,20},{8,24},{12,28},{16,0},{20,4},{24,8},{28,12},{32,48},... | collective-permute-start | bytes 393224 | tf_op jit(solution)/shard_map/ppermute | solution.py:667
  12.5 7.7 %collective-permute-start.2 = (f32[256,128]{1,0:T(8,128)S(1)}, f32[256,128]{1,0:T(8,128)S(1)}, u32[]{:S(2)}, u32[]{:S(2)}) collective-permute-start(f32[256,128]{1,0:T(8,128)S(1)} %get-tuple-element.78), channel_id=1, source_target_pairs={{0,8},{4,12},{8,16},{12,20},{16,24},{20,28},{24,0},{28,4},{32,40},... | collective-permute-start | bytes 393224 | tf_op jit(solution)/shard_map/ppermute | solution.py:667
  13.2 6.9 %collective-permute-start.3 = (f32[256,128]{1,0:T(8,128)S(1)}, f32[256,128]{1,0:T(8,128)S(1)}, u32[]{:S(2)}, u32[]{:S(2)}) collective-permute-start(f32[256,128]{1,0:T(8,128)S(1)} %get-tuple-element.79), channel_id=1, source_target_pairs={{0,24},{4,28},{8,0},{12,4},{16,8},{20,12},{24,16},{28,20},{32,56},... | collective-permute-start | bytes 393224 | tf_op jit(solution)/shard_map/ppermute | solution.py:667
  20.3 8.8 %collective-permute-start.6 = (f32[256,128]{1,0:T(8,128)S(1)}, f32[256,128]{1,0:T(8,128)S(1)}, u32[]{:S(2)}, u32[]{:S(2)}) collective-permute-start(f32[256,128]{1,0:T(8,128)S(1)} %get-tuple-element.81._), channel_id=1, source_target_pairs={{0,64},{4,68},{8,72},{12,76},{16,80},{20,84},{24,88},{28,92},{32,9... | collective-permute-start | bytes 393224 | tf_op jit(solution)/shard_map/ppermute | solution.py:667
  23.3 5.8 %collective-permute-start.5 = (f32[256,128]{1,0:T(8,128)S(1)}, f32[256,128]{1,0:T(8,128)S(1)}, u32[]{:S(2)}, u32[]{:S(2)}) collective-permute-start(f32[256,128]{1,0:T(8,128)S(1)} %get-tuple-element.81._), channel_id=1, source_target_pairs={{0,96},{4,100},{8,104},{12,108},{16,112},{20,116},{24,120},{28,124... | collective-permute-start | bytes 393224 | tf_op jit(solution)/shard_map/ppermute | solution.py:667
  24.0 5.4 %collective-permute-start.4 = (f32[256,128]{1,0:T(8,128)S(1)}, f32[256,128]{1,0:T(8,128)S(1)}, u32[]{:S(2)}, u32[]{:S(2)}) collective-permute-start(f32[256,128]{1,0:T(8,128)S(1)} %get-tuple-element.81._), channel_id=1, source_target_pairs={{0,32},{4,36},{8,40},{12,44},{16,48},{20,52},{24,56},{28,60},{32,6... | collective-permute-start | bytes 393224 | tf_op jit(solution)/shard_map/ppermute | solution.py:667
  29.5 5.9 %collective-permute-start.7 = (f32[256,128]{1,0:T(8,128)S(1)}, f32[256,128]{1,0:T(8,128)S(1)}, u32[]{:S(2)}, u32[]{:S(2)}) collective-permute-start(f32[256,128]{1,0:T(8,128)S(1)} %get-tuple-element.87), channel_id=1, source_target_pairs={{0,16},{4,20},{8,24},{12,28},{16,0},{20,4},{24,8},{28,12},{32,48},... | collective-permute-start | bytes 393224 | tf_op jit(solution)/shard_map/ppermute | solution.py:667
  30.5 5.8 %collective-permute-start.8 = (f32[256,128]{1,0:T(8,128)S(1)}, f32[256,128]{1,0:T(8,128)S(1)}, u32[]{:S(2)}, u32[]{:S(2)}) collective-permute-start(f32[256,128]{1,0:T(8,128)S(1)} %get-tuple-element.88), channel_id=1, source_target_pairs={{0,8},{4,12},{8,16},{12,20},{16,24},{20,28},{24,0},{28,4},{32,40},... | collective-permute-start | bytes 393224 | tf_op jit(solution)/shard_map/ppermute | solution.py:667
  31.8 4.5 %collective-permute-start.9 = (f32[256,128]{1,0:T(8,128)S(1)}, f32[256,128]{1,0:T(8,128)S(1)}, u32[]{:S(2)}, u32[]{:S(2)}) collective-permute-start(f32[256,128]{1,0:T(8,128)S(1)} %get-tuple-element.89), channel_id=1, source_target_pairs={{0,24},{4,28},{8,0},{12,4},{16,8},{20,12},{24,16},{28,20},{32,56},... | collective-permute-start | bytes 393224 | tf_op jit(solution)/shard_map/ppermute | solution.py:667
  33.2 7.2 %copy-start = (f32[16,128]{1,0:T(8,128)S(1)}, f32[16,128]{1,0:T(8,128)}, u32[]{:S(2)}) copy-start(f32[16,128]{1,0:T(8,128)} %gain_ref.9) | copy-start | bytes 24580
  36.4 5.5 %collective-permute-start.10 = (f32[4,256,128]{2,1,0:T(8,128)S(1)}, f32[4,256,128]{2,1,0:T(8,128)S(1)}, u32[]{:S(2)}, u32[]{:S(2)}) collective-permute-start(f32[4,256,128]{2,1,0:T(8,128)S(1)} %get-tuple-element.92), channel_id=1, source_target_pairs={{0,4},{4,0},{8,12},{12,8},{16,20},{20,16},{24,28},{28,24},{32,36},... | collective-permute-start | bytes 1572872 | tf_op jit(solution)/shard_map/ppermute | solution.py:667
  43.6 3.7 %collective-permute-start.13 = (f32[3,2,256]{2,1,0:T(2,128)S(1)}, f32[3,2,256]{2,1,0:T(2,128)S(1)}, u32[]{:S(2)}, u32[]{:S(2)}) collective-permute-start(f32[3,2,256]{2,1,0:T(2,128)S(1)} %get-tuple-element.98.s0), channel_id=1, source_target_pairs={{0,3},{1,0},{2,1},{3,2},{4,7},{5,4},{6,5},{7,6},{8,11},{9,8},{10,9... | collective-permute-start | bytes 18440 | tf_op jit(solution)/shard_map/ppermute | solution.py:685
  46.2 4.0 %collective-permute-start.12 = (f32[3,2,256]{2,1,0:T(2,128)S(1)}, f32[3,2,256]{2,1,0:T(2,128)S(1)}, u32[]{:S(2)}, u32[]{:S(2)}) collective-permute-start(f32[3,2,256]{2,1,0:T(2,128)S(1)} %get-tuple-element.98.s0), channel_id=1, source_target_pairs={{0,2},{1,3},{2,0},{3,1},{4,6},{5,7},{6,4},{7,5},{8,10},{9,11},{10,... | collective-permute-start | bytes 18440 | tf_op jit(solution)/shard_map/ppermute | solution.py:685
  46.7 3.7 %collective-permute-start.11 = (f32[3,2,256]{2,1,0:T(2,128)S(1)}, f32[3,2,256]{2,1,0:T(2,128)S(1)}, u32[]{:S(2)}, u32[]{:S(2)}) collective-permute-start(f32[3,2,256]{2,1,0:T(2,128)S(1)} %get-tuple-element.98.s0), channel_id=1, source_target_pairs={{0,1},{1,2},{2,3},{3,0},{4,5},{5,6},{6,7},{7,4},{8,9},{9,10},{10,1... | collective-permute-start | bytes 18440 | tf_op jit(solution)/shard_map/ppermute | solution.py:685
  52.1 3.8 %collective-permute-start.14 = (f32[4,256,128]{2,1,0:T(8,128)S(1)}, f32[4,256,128]{2,1,0:T(8,128)S(1)}, u32[]{:S(2)}, u32[]{:S(2)}) collective-permute-start(f32[4,256,128]{2,1,0:T(8,128)S(1)} %get-tuple-element.106), channel_id=1, source_target_pairs={{0,4},{4,0},{8,12},{12,8},{16,20},{20,16},{24,28},{28,24},{32,36},... | collective-permute-start | bytes 1572872 | tf_op jit(solution)/shard_map/ppermute | solution.py:667
  56.0 9.1 %collective-permute-start.15 = (f32[256,128]{1,0:T(8,128)S(1)}, f32[256,128]{1,0:T(8,128)S(1)}, u32[]{:S(2)}, u32[]{:S(2)}) collective-permute-start(f32[256,128]{1,0:T(8,128)S(1)} %get-tuple-element.109), channel_id=1, source_target_pairs={{0,16},{4,20},{8,24},{12,28},{16,0},{20,4},{24,8},{28,12},{32,48},... | collective-permute-start | bytes 393224 | tf_op jit(solution)/shard_map/ppermute | solution.py:667
  57.2 8.6 %collective-permute-start.16 = (f32[256,128]{1,0:T(8,128)S(1)}, f32[256,128]{1,0:T(8,128)S(1)}, u32[]{:S(2)}, u32[]{:S(2)}) collective-permute-start(f32[256,128]{1,0:T(8,128)S(1)} %get-tuple-element.110), channel_id=1, source_target_pairs={{0,8},{4,12},{8,16},{12,20},{16,24},{20,28},{24,0},{28,4},{32,40},... | collective-permute-start | bytes 393224 | tf_op jit(solution)/shard_map/ppermute | solution.py:667
  59.1 6.7 %collective-permute-start.17 = (f32[256,128]{1,0:T(8,128)S(1)}, f32[256,128]{1,0:T(8,128)S(1)}, u32[]{:S(2)}, u32[]{:S(2)}) collective-permute-start(f32[256,128]{1,0:T(8,128)S(1)} %get-tuple-element.111), channel_id=1, source_target_pairs={{0,24},{4,28},{8,0},{12,4},{16,8},{20,12},{24,16},{28,20},{32,56},... | collective-permute-start | bytes 393224 | tf_op jit(solution)/shard_map/ppermute | solution.py:667
  66.0 8.4 %collective-permute-start.20 = (f32[256,128]{1,0:T(8,128)S(1)}, f32[256,128]{1,0:T(8,128)S(1)}, u32[]{:S(2)}, u32[]{:S(2)}) collective-permute-start(f32[256,128]{1,0:T(8,128)S(1)} %get-tuple-element.114._.t_ref), channel_id=1, source_target_pairs={{0,64},{4,68},{8,72},{12,76},{16,80},{20,84},{24,88},{28,92},{32,9... | collective-permute-start | bytes 393224 | tf_op jit(solution)/shard_map/ppermute | solution.py:667
  68.5 6.2 %collective-permute-start.19 = (f32[256,128]{1,0:T(8,128)S(1)}, f32[256,128]{1,0:T(8,128)S(1)}, u32[]{:S(2)}, u32[]{:S(2)}) collective-permute-start(f32[256,128]{1,0:T(8,128)S(1)} %get-tuple-element.114._.t_ref), channel_id=1, source_target_pairs={{0,96},{4,100},{8,104},{12,108},{16,112},{20,116},{24,120},{28,124... | collective-permute-start | bytes 393224 | tf_op jit(solution)/shard_map/ppermute | solution.py:667
  69.5 5.3 %collective-permute-start.18 = (f32[256,128]{1,0:T(8,128)S(1)}, f32[256,128]{1,0:T(8,128)S(1)}, u32[]{:S(2)}, u32[]{:S(2)}) collective-permute-start(f32[256,128]{1,0:T(8,128)S(1)} %get-tuple-element.114._.t_ref), channel_id=1, source_target_pairs={{0,32},{4,36},{8,40},{12,44},{16,48},{20,52},{24,56},{28,60},{32,6... | collective-permute-start | bytes 393224 | tf_op jit(solution)/shard_map/ppermute | solution.py:667
  74.9 9.5 %collective-permute-start.21 = (f32[256,128]{1,0:T(8,128)S(1)}, f32[256,128]{1,0:T(8,128)S(1)}, u32[]{:S(2)}, u32[]{:S(2)}) collective-permute-start(f32[256,128]{1,0:T(8,128)S(1)} %get-tuple-element.119), channel_id=1, source_target_pairs={{0,16},{4,20},{8,24},{12,28},{16,0},{20,4},{24,8},{28,12},{32,48},... | collective-permute-start | bytes 393224 | tf_op jit(solution)/shard_map/ppermute | solution.py:667
  76.7 7.8 %collective-permute-start.22 = (f32[256,128]{1,0:T(8,128)S(1)}, f32[256,128]{1,0:T(8,128)S(1)}, u32[]{:S(2)}, u32[]{:S(2)}) collective-permute-start(f32[256,128]{1,0:T(8,128)S(1)} %get-tuple-element.120), channel_id=1, source_target_pairs={{0,8},{4,12},{8,16},{12,20},{16,24},{20,28},{24,0},{28,4},{32,40},... | collective-permute-start | bytes 393224 | tf_op jit(solution)/shard_map/ppermute | solution.py:667
  78.2 6.3 %collective-permute-start.23 = (f32[256,128]{1,0:T(8,128)S(1)}, f32[256,128]{1,0:T(8,128)S(1)}, u32[]{:S(2)}, u32[]{:S(2)}) collective-permute-start(f32[256,128]{1,0:T(8,128)S(1)} %get-tuple-element.121), channel_id=1, source_target_pairs={{0,24},{4,28},{8,0},{12,4},{16,8},{20,12},{24,16},{28,20},{32,56},... | collective-permute-start | bytes 393224 | tf_op jit(solution)/shard_map/ppermute | solution.py:667
  84.6 4.2 %collective-permute-start.24 = (f32[4,256,128]{2,1,0:T(8,128)S(1)}, f32[4,256,128]{2,1,0:T(8,128)S(1)}, u32[]{:S(2)}, u32[]{:S(2)}) collective-permute-start(f32[4,256,128]{2,1,0:T(8,128)S(1)} %get-tuple-element.124), channel_id=1, source_target_pairs={{0,4},{4,0},{8,12},{12,8},{16,20},{20,16},{24,28},{28,24},{32,36},... | collective-permute-start | bytes 1572872 | tf_op jit(solution)/shard_map/ppermute | solution.py:667
  87.2 1.6 %collective-permute-start.25 = (f32[32,128]{1,0:T(8,128)S(1)}, f32[32,128]{1,0:T(8,128)S(1)}, u32[]{:S(2)}, u32[]{:S(2)}) collective-permute-start(f32[32,128]{1,0:T(8,128)S(1)} %get-tuple-element.131), channel_id=1, source_target_pairs={{0,4},{4,0},{8,12},{12,8},{16,20},{20,16},{24,28},{28,24},{32,36},... | collective-permute-start | bytes 49160 | tf_op jit(solution)/shard_map/ppermute | solution.py:667
